TPU v7x, 32 devices: a whole 2x2x4 slice. The times are simulated.
32 devices in a mesh: bead: 4 (over y, x), space: 8 (over z, core).
Axes of the slice: x: 2, y: 2, z: 4, core: 2. Of those that a mesh axis runs over, the one named last changes fastest.
Arguments:
- positions: float32 [32, 3, 128, 128], P('bead', None, 'space'), may hold values from -0.1 to 1.1
- momenta: float32 [32, 3, 128, 128], P('bead', None, 'space'), may hold values from -6 to 6
- molecules: int32 [128, 42, 3], P('space'), may hold values from 0 to 128, as said below
Outputs:
- final_positions: float32 [32, 3, 128, 128], P('bead', None, 'space')
- final_momenta: float32 [32, 3, 128, 128], P('bead', None, 'space')
Inputs may be any that keep to these rules, and one draw needn't show every extreme that they name: In each cell, the slots of all listed atoms differ; used molecules come first and unused ones carry 128 in all three places; each cell has 21 to 42 used molecules.
All inputs are finite; a program needn't handle non-finite values.
Results may differ from a plain program's by a relative error of at most 0.0003.
Values sent between devices are 32-bit elements; how exact they have to be, the bound alone decides.
No kernel may reach another device: no remote copies, remote signals or barrier semaphores. Data moves between devices by JAX's collectives and lax.ppermute only.
A program may use at most 64 MiB of HBM per device.

v0:
```python
import functools

import jax
import jax.numpy as jnp
import ml_dtypes
import numpy as np
from jax import lax
from jax.experimental import pallas as pl
from jax.experimental.pallas import tpu as pltpu
from jax.sharding import PartitionSpec as P

charge_oxygen = -0.8476
charge_hydrogen = 0.4238
coulomb_scale = 24.0
coulomb_soft = 0.004
well_depth = 0.02
sigma_square = 0.0841
lennard_soft = 0.04
bond_stiffness = 20000.0
bond_square = 0.0081
angle_stiffness = 5000.0
angle_square = 0.0204
cycle_frequency = 60.0
outer_step = 0.02
inner_step = 0.01
oxygen_mass = 16.0

REACH = 1
X_HALO = 2 * REACH
P_HALO = REACH

F32 = jnp.float32
BF16 = jnp.bfloat16


def rounded(a):
    return a.astype(BF16).astype(F32)


def split3(a):
    high = rounded(a)
    rest = a - high
    mid = rounded(rest)
    return high, mid, rest - mid


def two_part(a):
    high = rounded(a)
    return high + rounded(a - high)


def dot_nn(a, b):
    return lax.dot_general(a, b, (((1,), (0,)), ((), ())), preferred_element_type=F32)


def dot_nt(a, b):
    return lax.dot_general(a, b, (((1,), (1,)), ((), ())), preferred_element_type=F32)


def propagator(beads, beads_dev):
    j = np.arange(beads)
    angles = 2.0 * np.pi * ((j[:, None] * j[None, :]) % beads) / beads
    half = beads // 2
    col = j[None, :]
    u = np.where(
        col == 0,
        np.sqrt(1.0 / beads),
        np.where(
            col < half,
            np.sqrt(2.0 / beads) * np.cos(angles),
            np.where(
                col == half,
                np.sqrt(1.0 / beads) * np.cos(angles),
                np.sqrt(2.0 / beads) * np.sin(angles),
            ),
        ),
    )
    w = 2.0 * cycle_frequency * np.sin(np.pi * j / beads)
    cosines = np.cos(w * inner_step)
    spring = w * np.sin(w * inner_step)
    drift = np.where(j == 0, inner_step, np.sin(w * inner_step) / np.where(j == 0, 1.0, w))
    def circulant(values, bead):
        first = ((u * values) @ u.T)[:, 0]
        return first[(bead[:, None] - bead[None, :]) % beads]

    out = []
    for b in range(beads // beads_dev):
        bead = ((j // beads_dev) ^ b) * beads_dev + j % beads_dev
        a = circulant(cosines, bead)
        whole = np.block([[a, circulant(drift, bead)], [-circulant(spring, bead), a]])
        high = whole.astype(ml_dtypes.bfloat16)
        rest = whole - high.astype(np.float64)
        mid = rest.astype(ml_dtypes.bfloat16)
        low = (rest - mid.astype(np.float64)).astype(ml_dtypes.bfloat16)
        out.append(np.concatenate([high, high, mid, mid, high, low], axis=1))
    return np.stack(out)


def lane_tables(lanes, mols, slots):
    lane = lax.broadcasted_iota(jnp.int32, lanes.shape, 1)
    unit = jnp.where(lane < mols, charge_oxygen / charge_hydrogen, 1.0)
    return jnp.where(lanes < slots, unit, 0.0)


def permuted(rows, perm):
    n = rows.shape[0]
    stacked = jnp.concatenate(split3(rows), axis=0).astype(BF16)
    moved = dot_nn(stacked, perm)
    return moved[:n] + moved[n : 2 * n] + moved[2 * n :]


def unpermuted(rows, perm):
    n = rows.shape[0]
    stacked = jnp.concatenate(split3(rows), axis=0).astype(BF16)
    moved = dot_nt(stacked, perm)
    return moved[:n] + moved[n : 2 * n] + moved[2 * n :]


def order_kernel(lb, cells, mols, slots, mol_hbm, x_hbm, p_hbm, *refs):
    xo, po, perm_ref, q_ref, to_right, to_left = refs[:6]
    mol_ref, x_ref, p_ref, wide, held_ref, sems = refs[6:]
    copies = [
        pltpu.make_async_copy(source, dest, sems.at[i])
        for i, (source, dest) in enumerate(
            ((mol_hbm, mol_ref), (x_hbm, x_ref), (p_hbm, p_ref))
        )
    ]
    for copy in copies:
        copy.start()
    row = lax.broadcasted_iota(jnp.int32, (slots, slots), 0)
    col = lax.broadcasted_iota(jnp.int32, (slots, slots), 1)
    upper = (row < col).astype(F32).astype(BF16)
    row = row.astype(F32)
    lane = lax.broadcasted_iota(jnp.int32, (cells, slots), 1)
    far = 4.0 * slots
    wide[...] = jnp.full(wide.shape, slots, jnp.int32)
    copies[0].wait()
    for t in range(3):
        wide[t, :, :mols] = mol_ref[t]
    lanes = jnp.where(
        lane < mols,
        wide[0],
        jnp.where(lane < 2 * mols, pltpu.roll(wide[1], mols, 1), pltpu.roll(wide[2], 2 * mols, 1)),
    )
    lanes = jnp.where(lane < 3 * mols, lanes, slots)
    charges = lane_tables(lanes, mols, slots)
    q_ref[...] = charges
    free = lanes >= slots
    key = jnp.where(
        free, far + dot_nn(free.astype(F32).astype(BF16), upper), lanes.astype(F32)
    )
    ones = jnp.ones((16, slots), BF16)
    for cell in range(cells):
        held = (row == key[cell : cell + 1]).astype(F32).astype(BF16)
        held_ref[cell : cell + 1, :] = dot_nt(ones, held)[0:1]
    used = held_ref[...]
    rank = dot_nn((1.0 - used).astype(BF16), upper)
    slot_key = jnp.where(used > 0.5, lane.astype(F32), far + rank)
    copies[1].wait()
    copies[2].wait()
    n = 3 * lb
    for cell in range(cells):
        slot_column = jnp.broadcast_to(slot_key[cell : cell + 1], (slots, slots)).T
        perm = (slot_column == key[cell : cell + 1]).astype(F32).astype(BF16)
        perm_ref[cell] = perm
        rows = [
            ref[pl.ds(comp * cells + cell, lb, stride=3 * cells), :]
            for ref in (x_ref, p_ref)
            for comp in range(3)
        ]
        moved = permuted(jnp.concatenate(rows, axis=0), perm)
        xo[cell] = moved[:n]
        po[cell] = moved[n:]
    for out, xs, ps in (
        (to_right, (cells - 2, cells - 1), cells - 1),
        (to_left, (0, 1), 0),
    ):
        out[9 * lb :, :] = jnp.zeros((8, slots), F32)
        for e, cell in enumerate(xs):
            out[pl.ds(e * n, n), :] = xo[cell]
            out[pl.ds(9 * lb + e, 1), :] = charges[cell : cell + 1]
        out[pl.ds(2 * n, n), :] = po[ps]


def put_tiles(scratch, first, count, rows):
    for index, value in rows:
        scratch[pl.ds(first * 8 + index, count, stride=8), :] = value


OFFSETS = (-1.0, 0.0, 1.0)


def build_tiles(tiles, first, count, x, y, z):
    x, y, z = two_part(x - 0.5), two_part(y - 0.5), two_part(z - 0.5)
    norm = x * x + y * y + z * z + 0.5 * coulomb_soft
    high = two_part(norm)
    low = norm - high
    put_tiles(
        tiles, first, count, ((0, x), (1, y), (2, z), (3, high), (4, low), (5, high), (6, low))
    )


def store_shapes(count, beads, slots):
    n = count * beads
    return (
        [((n * 8, slots), F32), ((n // 2, slots, 64), BF16)]
        + [((n // 2, 32, slots), BF16)] * 3
        + [((n, 32, slots), BF16)]
    )


STORE = 6


class Store:
    def __init__(self, refs, beads):
        self.tiles, self.peers, *sums, self.targets = refs
        self.sums = sums
        self.beads = beads


def tile_of(ref, n):
    return ref[pl.ds(pl.multiple_of(n * 8, 8), 8), :]


def prepare(store, charges, count, slots):
    tiles, beads = store.tiles, store.beads
    row8 = lax.broadcasted_iota(jnp.int32, (8, slots), 0)
    place, norms = row8 < 3, row8 < 5
    target_rows = place | (row8 == 5) | (row8 == 6)
    ones_low = jnp.where((row8 == 3) | (row8 == 4), 1.0, 0.0)
    ones_high = jnp.where((row8 == 5) | (row8 == 6), 1.0, 0.0)
    ones_last = jnp.where(row8 == 7, 1.0, 0.0)
    pairs = beads // 2
    total = count * pairs
    unroll = max(n for n in range(1, max(2, min(17, total // 4 + 1))) if total % n == 0)

    def stack(values):
        return jnp.concatenate(values, axis=0).astype(BF16)

    def step(index, carry):
        for u in range(unroll):
            m = index * unroll + u
            charge = charges[lax.div(m, pairs)]
            units = [
                jnp.where(row8 == 3, charge, jnp.where(row8 == 4, offset * charge, 0.0))
                for offset in OFFSETS
            ]
            left, high_rows, mid_rows = [], [], []
            for h in range(2):
                value = tile_of(tiles, 2 * m + h)
                high = rounded(value)
                mid = value - high
                x_high, x_mid = high[0:1], mid[0:1]
                left_high = jnp.where(place, -2.0 * high, jnp.where(norms, high, ones_high))
                left_mid = jnp.where(place, -2.0 * mid, jnp.where(norms, mid, 0.0))
                left_last = jnp.where(
                    place,
                    -2.0 * mid,
                    jnp.where(
                        row8 == 3,
                        2.0 * x_high,
                        jnp.where(row8 == 4, 2.0 * x_mid, ones_last - 2.0 * ones_high),
                    ),
                )
                left += [left_high, left_high, left_mid, left_last]
                right_high = jnp.where(target_rows, high, ones_low)
                right_mid = jnp.where(target_rows, mid, 0.0)
                right_last = jnp.where(
                    place,
                    mid,
                    jnp.where(
                        row8 == 5, x_high, jnp.where(row8 == 6, x_mid, ones_low + ones_last)
                    ),
                )
                store.targets[2 * m + h] = stack([right_high, right_mid, right_high, right_last])
                high_rows.append(high * charge)
                mid_rows.append(jnp.where(place, mid * charge, 0.0))
            store.peers[m] = stack(left).T
            for o in range(3):
                rows = []
                for h in range(2):
                    rows += [jnp.where(place, high_rows[h], units[o]), mid_rows[h]]
                store.sums[o][m] = stack(rows)
        return carry

    lax.fori_loop(0, total // unroll, step, 0)


class PairLoop:
    def __init__(self, mols, slots, beads, keep):
        self.mols, self.slots, self.keep = mols, slots, keep
        self.pairs = beads // 2
        self.unroll = min(self.pairs, 4)
        self.per_cell = self.pairs // self.unroll
        orows = -(-mols // 8) * 8
        self.row8 = lax.broadcasted_iota(jnp.int32, (8, slots), 0)
        lj_row = lax.broadcasted_iota(jnp.int32, (orows, slots), 0)
        lj_lane = lax.broadcasted_iota(jnp.int32, (orows, slots), 1)
        self.first_lanes, self.second_lanes = lj_lane < mols, lj_lane < 2 * mols
        self.corner = (lj_row < mols) & self.first_lanes

        i = lax.broadcasted_iota(jnp.int32, (slots, slots), 0)
        j = lax.broadcasted_iota(jnp.int32, (slots, slots), 1)
        i = jnp.where(i >= 2 * mols, i - 2 * mols, jnp.where(i >= mols, i - mols, i))
        j = jnp.where(j >= 2 * mols, j - 2 * mols, jnp.where(j >= mols, j - mols, j))
        keep[...] = (i != j).astype(F32)

        lane64 = lax.broadcasted_iota(jnp.int32, (slots, 64), 1) & 31
        odd = (lane64 >= 27) & (lane64 < 31)
        even = lane64 == 31
        self.signs = [
            jnp.where(odd, offset, jnp.where(even, offset * offset, 1.0)).astype(BF16)
            for offset in OFFSETS
        ]
        self.zero = jnp.zeros((32, slots), BF16)

    def pair(self, peers, charge):
        mols, slots = self.mols, self.slots
        orows = self.corner.shape[0]
        pair_scale = coulomb_scale * charge_hydrogen * charge_hydrogen
        k3 = sigma_square**3
        ratio = (charge_hydrogen / charge_oxygen) ** 2 / pair_scale
        lj_a = 24.0 * well_depth * 2.0 * k3 * k3 * ratio
        lj_b = 24.0 * well_depth * k3 * ratio
        zero = self.zero
        own, m = peers[1]
        left = jnp.concatenate(
            [store.peers[index] * sign for (store, index), sign in zip(peers, self.signs)], axis=0
        )
        right = jnp.concatenate(
            [
                jnp.concatenate([own.targets[2 * m], zero], axis=1),
                jnp.concatenate([zero, own.targets[2 * m + 1]], axis=1),
            ],
            axis=0,
        )
        squares = dot_nn(left, right)
        blocks = [[], [], []]
        for h in range(2):
            lanes = slice(h * slots, (h + 1) * slots)
            near = [squares[o * slots : o * slots + orows, lanes] for o in range(3)]
            packed = jnp.where(
                self.first_lanes,
                near[0],
                jnp.where(
                    self.second_lanes,
                    pltpu.roll(near[1], mols, 1),
                    pltpu.roll(near[2], 2 * mols, 1),
                ),
            )
            root = lax.rsqrt(packed + (lennard_soft - coulomb_soft))
            inverse = root * root
            cube = inverse * inverse * inverse
            lj = (cube * lj_a - lj_b) * (cube * inverse)
            for o in range(3):
                root = lax.rsqrt(squares[o * slots : (o + 1) * slots, lanes])
                strength = root * root * root
                part = pltpu.roll(lj, slots - o * mols, 1) if o else lj
                strength = jnp.concatenate(
                    [strength[:orows] + jnp.where(self.corner, part, 0.0), strength[orows:]],
                    axis=0,
                )
                if o == 1:
                    strength = strength * self.keep[...]
                high = strength.astype(BF16)
                low = (strength - high.astype(F32)).astype(BF16)
                blocks[o].append(jnp.concatenate([high, low], axis=0))
        sums = None
        for o, (store, index) in enumerate(peers):
            weights = store.sums[o][index]
            value = dot_nn(
                jnp.concatenate([weights, weights], axis=1), jnp.concatenate(blocks[o], axis=1)
            )
            sums = value if sums is None else sums + value
        scale = charge * pair_scale
        out = []
        for h in range(2):
            part = sums[16 * h : 16 * h + 16, h * slots : (h + 1) * slots]
            total = part[0:8] + part[8:16]
            total = total + jnp.where(self.row8 == 0, total[4:5], 0.0)
            out.append((tile_of(own.tiles, 2 * m + h) * total[3:4] - total) * scale)
        return out

    def cells(self, store, charges, first, last, forces, limit):
        total = (last - first) * self.pairs
        unroll = max(n for n in range(1, limit + 1) if total % n == 0)

        def step(index, carry):
            for u in range(unroll):
                m = index * unroll + u
                at = m + first * self.pairs
                peers = [(store, at + (o - 1) * self.pairs) for o in range(3)]
                out = self.pair(peers, charges[lax.div(at, self.pairs)])
                for h in range(2):
                    n = 2 * m + h
                    forces[pl.ds(pl.multiple_of(n * 8, 8), 8), :] = out[h]
            return carry

        lax.fori_loop(0, total // unroll, step, 0)


def read_force(forces, w, beads, comp):
    return forces[pl.ds(w * beads * 8 + comp, beads, stride=8), :]


def own_kernel(cells, lb, slots, x_ref, q_ref, *refs):
    store = Store(refs, lb)
    for w in range(cells):
        rows = x_ref[w]
        build_tiles(store.tiles, w * lb, lb, rows[:lb], rows[lb : 2 * lb], rows[2 * lb :])
    prepare(store, Rows(q_ref, 0), cells, slots)


def interior_kernel(cells, lb, mols, slots, q_ref, *refs):
    store = Store(refs[:STORE], lb)
    forces, keep = refs[STORE:]
    PairLoop(mols, slots, lb, keep).cells(store, Rows(q_ref, 0), 1, cells - 1, forces, 64)


def edge_kernel(nb, group, lb, cells, mols, slots, b_ref, *refs):
    x_ref, p_ref, q_ref, left, right, inner = refs[:6]
    own = Store(refs[6 : 6 + STORE], lb)
    refs = refs[6 + STORE :]
    outs, q_out = refs[:nb], refs[nb]
    kicked, halo_forces, keep = refs[nb + 1 : nb + 4]
    halo = Store(refs[nb + 4 :], lb)
    n = 3 * lb
    count = cells + 2 * X_HALO
    b = b_ref[0]

    charge_rows = [left[pl.ds(9 * lb + e, 1), :] for e in range(2)]
    charge_rows += [q_ref[c : c + 1, :] for c in range(cells)]
    charge_rows += [right[pl.ds(9 * lb + e, 1), :] for e in range(2)]
    q_out[...] = jnp.zeros(q_out.shape, F32)
    for w in range(count):
        q_out[w : w + 1, :] = charge_rows[w]
    for e in range(4):
        edge = (left, right)[e // 2]
        rows = edge[pl.ds((e % 2) * n, n), :]
        build_tiles(halo.tiles, e * lb, lb, rows[:lb], rows[lb : 2 * lb], rows[2 * lb :])

    class Edges:
        def __getitem__(self, e):
            return q_out[pl.ds(jnp.where(e < 2, e, e + cells), 1), :]

    prepare(halo, Edges(), 4, slots)
    loop = PairLoop(mols, slots, lb, keep)

    def place(w):
        if w < X_HALO:
            return halo, w
        if w >= cells + X_HALO:
            return halo, w - cells
        return own, w - X_HALO

    targets = (1, 2, cells + 1, cells + 2)

    def edge_step(step, carry):
        for e, w in enumerate(targets):
            for u in range(loop.unroll):
                index = step * loop.unroll + u
                peers = [
                    (store, cell * loop.pairs + index) for store, cell in map(place, (w - 1, w, w + 1))
                ]
                out = loop.pair(peers, charge_rows[w])
                for h in range(2):
                    at = (e * lb + 2 * index + h) * 8
                    halo_forces[pl.ds(pl.multiple_of(at, 8), 8), :] = out[h]
        return carry

    lax.fori_loop(0, loop.per_cell, edge_step, 0)
    half = 0.5 * outer_step
    for w in range(1, count - 1):
        if w < X_HALO:
            old = left[pl.ds(2 * n, n), :]
        elif w >= cells + X_HALO:
            old = right[pl.ds(2 * n, n), :]
        else:
            old = p_ref[w - X_HALO]
        source, cell = (
            (halo_forces, targets.index(w)) if w in targets else (inner, w - X_HALO - 1)
        )
        force = jnp.concatenate([read_force(source, cell, lb, c) for c in range(3)], axis=0)
        kicked[w - 1] = old + half * force
    width = group + 2 * P_HALO
    for k in range(nb):
        first = jnp.bitwise_xor(b, k) * group
        for w in range(width):
            outs[k][pl.ds((width + w) * n, n), :] = kicked[first + w]
            source = first + w - P_HALO
            inside = x_ref[jnp.clip(source, 0, cells - 1)]
            if w < P_HALO:
                inside = jnp.where(source < 0, left[pl.ds(n, n), :], inside)
            elif w >= group + P_HALO:
                inside = jnp.where(source >= cells, right[pl.ds(0, n), :], inside)
            outs[k][pl.ds(w * n, n), :] = inside


class Rows:
    def __init__(self, ref, first):
        self.ref, self.first = ref, first

    def __getitem__(self, index):
        return self.ref[pl.ds(self.first + index, 1), :]


def bond_forces(x, y, z, used, mols, slots):
    def partner(a, t):
        return pltpu.roll(a, slots - t * mols, 1)

    first = [a - partner(a, 1) for a in (x, y, z)]
    second = [a - partner(a, 2) for a in (x, y, z)]
    third = [s - f for f, s in zip(first, second)]

    def pull(bond, stiffness, square):
        length = bond[0] * bond[0] + bond[1] * bond[1] + bond[2] * bond[2]
        return (stiffness * used) * (length - square)

    c1 = pull(first, bond_stiffness, bond_square)
    c2 = pull(second, bond_stiffness, bond_square)
    c3 = pull(third, angle_stiffness, angle_square)
    out = []
    for f, s, t in zip(first, second, third):
        on_first = c1 * f - c3 * t
        on_second = c2 * s + c3 * t
        on_oxygen = -(c1 * f + c2 * s)
        out.append(
            on_oxygen + pltpu.roll(on_first, mols, 1) + pltpu.roll(on_second, 2 * mols, 1)
        )
    return out


def steps_kernel(nb, group, lb, mols, slots, b_ref, *refs):
    blocks = refs[:nb]
    step_ref, q_ref, xv = refs[nb : nb + 3]
    beads = nb * lb
    store = Store(refs[nb + 3 :], beads)
    width = group + 2 * P_HALO
    n = 3 * lb
    b = b_ref[0]
    step = step_ref[b]
    charges = Rows(q_ref, b * group + P_HALO)

    def advance(states):
        flat = [
            jnp.concatenate([x, v], axis=0) for pos, vel in states for x, v in zip(pos, vel)
        ]
        high, mid, low = split3(jnp.concatenate(flat, axis=1))
        stacked = jnp.concatenate([high, mid, high, mid, low, high], axis=0).astype(BF16)
        new = dot_nn(step, stacked)
        out = []
        for i in range(len(states)):
            columns = [
                new[:, (3 * i + c) * slots : (3 * i + c + 1) * slots] for c in range(3)
            ]
            out.append(([a[:beads] for a in columns], [a[beads:] for a in columns]))
        return out

    def gather(w, a, comp):
        return jnp.concatenate(
            [block[pl.ds((a * width + w) * n + comp * lb, lb), :] for block in blocks], axis=0
        )

    def kick(state, oxygen, scale):
        pos, vel = state
        force = bond_forces(*pos, oxygen, mols, slots)
        return pos, [v + scale * f for v, f in zip(vel, force)]

    for first in range(0, width, 2):
        members = range(first, min(first + 2, width))
        charge = [charges[w] for w in members]
        oxygen = [(q < -1.5).astype(F32) for q in charge]
        inverse = [jnp.where(q < -1.5, 1.0 / oxygen_mass, 1.0) for q in charge]
        states = [
            (
                [gather(w, 0, c) for c in range(3)],
                [gather(w, 1, c) * scale for c in range(3)],
            )
            for w, scale in zip(members, inverse)
        ]
        for part in (0.5, 1.0):
            states = [
                kick(state, o, (part * inner_step) * scale)
                for state, o, scale in zip(states, oxygen, inverse)
            ]
            states = advance(states)
        for w, state, q, o, scale in zip(members, states, charge, oxygen, inverse):
            if 1 <= w <= width - 2:
                pos, vel = kick(state, o, (0.5 * inner_step) * scale)
                mass = jnp.where(q < -1.5, oxygen_mass, 1.0)
                for c in range(3):
                    xv[w - 1, pl.ds(c * beads, beads), :] = pos[c]
                    xv[w - 1, pl.ds((3 + c) * beads, beads), :] = vel[c] * mass
            build_tiles(store.tiles, w * beads, beads, *state[0])
    prepare(store, charges, width, slots)


def final_kernel(nb, group, lb, mols, slots, b_ref, *refs):
    perm_ref, q_ref, xv = refs[:3]
    beads = nb * lb
    store = Store(refs[3 : 3 + STORE], beads)
    ys = refs[3 + STORE : 3 + STORE + nb]
    forces, keep = refs[3 + STORE + nb :]
    b = b_ref[0]
    charges = Rows(q_ref, b * group + P_HALO)
    loop = PairLoop(mols, slots, beads, keep)
    loop.cells(store, charges, P_HALO, P_HALO + group, forces, 32)
    for w in range(group):
        old = xv[w]
        m = 3 * beads
        force = jnp.concatenate([read_force(forces, w, beads, c) for c in range(3)], axis=0)
        state = jnp.concatenate([old[:m], old[m:] + (0.5 * outer_step) * force], axis=0)
        state = unpermuted(state, perm_ref[b * group + w])
        for a in range(2):
            for c in range(3):
                for k in range(nb):
                    row = (a * 3 + c) * beads + k * lb
                    ys[k][pl.ds(((a * group + w) * 3 + c) * lb, lb), :] = state[row : row + lb]


def unpack_kernel(nb, group, lb, cells, b_ref, *refs):
    ys = refs[:nb]
    outs = refs[nb:]
    b = b_ref[0]
    for k in range(nb):
        source = jnp.bitwise_xor(b, k)
        for a in range(2):
            for w in range(group):
                for c in range(3):
                    outs[a][pl.ds(c * cells + source * group + w, lb, stride=3 * cells), :] = ys[
                        k
                    ][pl.ds(((a * group + w) * 3 + c) * lb, lb), :]


def call(kernel, outs, scratch, scalar, *operands, space=pltpu.VMEM):
    vmem = pl.BlockSpec(memory_space=pltpu.VMEM)
    smem = pl.BlockSpec(memory_space=pltpu.SMEM)
    return pl.pallas_call(
        kernel,
        out_shape=outs,
        in_specs=([] if scalar is None else [smem]) + [pl.BlockSpec(memory_space=space)] * len(operands),
        out_specs=[vmem] * len(outs),
        scratch_shapes=scratch,
        compiler_params=pltpu.CompilerParams(vmem_limit_bytes=24 * 1024 * 1024),
    )(*(() if scalar is None else (scalar,)), *operands)


def exchange(blocks, nb):
    out = list(blocks)
    for k in reversed(range(1, nb)):
        out[k] = lax.ppermute(blocks[k], "bead", [(i, i ^ k) for i in range(nb)])
    return out


def local(nb, ns, positions, momenta, molecules):
    lb, _, cells, slots = positions.shape
    mols = molecules.shape[1]
    group = cells // nb
    beads = lb * nb
    width = group + 2 * P_HALO
    b = lax.axis_index("bead").astype(jnp.int32).reshape(1)

    def shape(*dims):
        return jax.ShapeDtypeStruct(dims, F32)

    edge = shape(9 * lb + 8, slots)
    rows = lb * 3 * cells
    xs, ps, perm, charges, to_right, to_left = call(
        functools.partial(order_kernel, lb, cells, mols, slots),
        [shape(cells, 3 * lb, slots)] * 2
        + [jax.ShapeDtypeStruct((cells, slots, slots), BF16), shape(cells, slots), edge, edge],
        [
            pltpu.VMEM((3, cells, mols), jnp.int32),
            pltpu.VMEM((rows, slots), F32),
            pltpu.VMEM((rows, slots), F32),
            pltpu.VMEM((3, cells, slots), jnp.int32),
            pltpu.VMEM((cells, slots), F32),
            pltpu.SemaphoreType.DMA((3,)),
        ],
        None,
        *(
            pltpu.with_memory_space_constraint(a, pltpu.HBM)
            for a in (
                jnp.transpose(molecules, (2, 0, 1)),
                positions.reshape(rows, slots),
                momenta.reshape(rows, slots),
            )
        ),
        space=pltpu.HBM,
    )
    left = lax.ppermute(to_right, "space", [(s, (s + 1) % ns) for s in range(ns)])
    right = lax.ppermute(to_left, "space", [(s, (s - 1) % ns) for s in range(ns)])
    q_rows = -(-(cells + 2 * X_HALO) // 8) * 8

    def store(count, store_beads):
        return [
            jax.ShapeDtypeStruct(*entry) for entry in store_shapes(count, store_beads, slots)
        ]

    keep = pltpu.VMEM((slots, slots), F32)
    own = call(
        functools.partial(own_kernel, cells, lb, slots), store(cells, lb), [], None, xs, charges
    )
    (inner,) = call(
        functools.partial(interior_kernel, cells, lb, mols, slots),
        [shape((cells - 2) * lb * 8, slots)],
        [keep],
        None,
        charges,
        *own,
    )
    *blocks, q_wide = call(
        functools.partial(edge_kernel, nb, group, lb, cells, mols, slots),
        [shape(2 * width * 3 * lb, slots)] * nb + [shape(q_rows, slots)],
        [
            pltpu.VMEM((cells + 2 * P_HALO, 3 * lb, slots), F32),
            pltpu.VMEM((4 * lb * 8, slots), F32),
            keep,
        ]
        + [pltpu.VMEM(*entry) for entry in store_shapes(4, lb, slots)],
        b,
        xs,
        ps,
        charges,
        left,
        right,
        inner,
        *own,
    )
    blocks = exchange(blocks, nb)
    step = jnp.asarray(propagator(beads, lb))
    xv, *stepped = call(
        functools.partial(steps_kernel, nb, group, lb, mols, slots),
        [shape(group, 6 * beads, slots)] + store(width, beads),
        [],
        b,
        *blocks,
        step,
        q_wide,
    )
    ys = call(
        functools.partial(final_kernel, nb, group, lb, mols, slots),
        [shape(2 * group * 3 * lb, slots)] * nb,
        [pltpu.VMEM((group * beads * 8, slots), F32), keep],
        b,
        perm,
        q_wide,
        xv,
        *stepped,
    )
    ys = exchange(ys, nb)
    new_x, new_p = call(
        functools.partial(unpack_kernel, nb, group, lb, cells),
        [shape(lb * 3 * cells, slots)] * 2,
        [],
        b,
        *ys,
    )
    return new_x.reshape(positions.shape), new_p.reshape(positions.shape)


def solution(mesh):
    spec = P("bead", None, "space", None)
    return jax.shard_map(
        functools.partial(local, mesh.shape["bead"], mesh.shape["space"]),
        mesh=mesh,
        in_specs=(spec, spec, P("space", None, None)),
        out_specs=(spec, spec),
        check_vma=False,
    )
```

profile of v0, /device:TPU:0, one launch (start us, length us, event | category | flops | bytes accessed | tf_op | source)
XLA Modules:
  0.0 49.9 jit_solution(101402538600240384)
XLA Ops:
  0.6 2.0 %shard_map.59 = (f32[16,24,128]{2,1,0:T(8,128)S(1)}, f32[16,24,128]{2,1,0:T(8,128)S(1)}, bf16[16,128,128]{2,1,0:T(8,128)(2,1)S(1)}, f32[16,128]{1,0:T(8,128)S(1)...) custom-call(s32[3,16,42]{2,1,0:T(8,128)} %bitcast.8, f32[384,128]{1,0:T(8,128)} %bitcast.6, f32[384,128]{1,0:T(8,128)} %bitcast.7), custom_call_target="tpu_custom_call" | custom-call | tf_op jit(solution)/shard_map/pallas_call | solution.py:639
  2.7 0.5 %collective-permute-start = (f32[80,128]{1,0:T(8,128)S(1)}, f32[80,128]{1,0:T(8,128)S(1)}, u32[]{:S(2)}, u32[]{:S(2)}) collective-permute-start(f32[80,128]{1,0:T(8,128)S(1)} %get-tuple-element.36), channel_id=1, source_target_pairs={{0,1},{1,2},{2,3},{3,4},{4,5},{5,6},{6,7},{7,0},{8,9},{9,10},{10,1... | collective-permute-start | bytes 122888 | tf_op jit(solution)/shard_map/ppermute | solution.py:692
  3.2 4.1 %collective-permute-start.1 = (f32[80,128]{1,0:T(8,128)S(1)}, f32[80,128]{1,0:T(8,128)S(1)}, u32[]{:S(2)}, u32[]{:S(2)}) collective-permute-start(f32[80,128]{1,0:T(8,128)S(1)} %get-tuple-element.37), channel_id=1, source_target_pairs={{0,7},{1,0},{2,1},{3,2},{4,3},{5,4},{6,5},{7,6},{8,15},{9,8},{10,9... | collective-permute-start | bytes 122888 | tf_op jit(solution)/shard_map/ppermute | solution.py:693
  7.3 1.2 %shard_map.60 = (f32[1024,128]{1,0:T(8,128)S(1)}, bf16[64,128,64]{2,1,0:T(8,128)(2,1)S(1)}, bf16[64,32,128]{2,1,0:T(8,128)(2,1)S(1)}, bf16[64,32,128]{2,1,0:T(8,...) custom-call(f32[16,24,128]{2,1,0:T(8,128)S(1)} %get-tuple-element.33.x_ref.refs_0_, ...), custom_call_target="tpu_custom_call" | custom-call | tf_op jit(solution)/shard_map/pallas_call | solution.py:639
  8.5 7.6 %shard_map.61.refs_5_ = f32[896,128]{1,0:T(8,128)S(1)} custom-call(f32[16,128]{1,0:T(8,128)S(1)} %get-tuple-element.35.q_ref.refs_2_, f32[1024,128]{1,0:T(8,128)S(1)} %get-tuple-element.38.refs_0_.refs_6_, bf16[64,128,64]{2,1,0:T(8,128)(2,1)S(1)} %get-tuple-element.39.refs_1_.refs_7_, bf16[64,32,128]{2,1,0:T(8,128)(2,1)S(1)} %get-tuple-element.40.refs_2_.refs_8_, ...), custom_call_target="tpu_custom_call" | custom-call | tf_op jit(solution)/shard_map/pallas_call | solution.py:639
  16.1 0.0 collective-permute-done.refs_3_
  16.1 0.0 collective-permute-done.1.refs_4_
  16.1 0.0 copy-start
  16.1 3.3 %shard_map.62 = (f32[288,128]{1,0:T(8,128)S(1)}, f32[288,128]{1,0:T(8,128)S(1)}, f32[288,128]{1,0:T(8,128)S(1)}, f32[288,128]{1,0:T(8,128)S(1)}, f32[24,128]{1,0:T(8,128)S(1)}) custom-call(s32[1]{0:T(128)} %bitcast.b_ref, f32[16,24,128]{2,1,0:T(8,128)S(1)} %get-tuple-element.33.x_ref.refs_0_, f32[16,24,128]{2,1,0:T(8,128)S(1)} %get-tuple-element.34.refs_1_, ...), custom_call_target="tpu_custom_call" | custom-call | tf_op jit(solution)/shard_map/pallas_call | solution.py:639
  19.4 2.0 %collective-permute-start.2 = (f32[288,128]{1,0:T(8,128)S(1)}, f32[288,128]{1,0:T(8,128)S(1)}, u32[]{:S(2)}, u32[]{:S(2)}) collective-permute-start(f32[288,128]{1,0:T(8,128)S(1)} %get-tuple-element.46), channel_id=1, source_target_pairs={{0,8},{8,0},{16,24},{24,16},{1,9},{9,1},{17,25},{25,17},{2,10},{10... | collective-permute-start | bytes 442376 | tf_op jit(solution)/shard_map/ppermute | solution.py:652
  21.4 1.5 %collective-permute-start.3 = (f32[288,128]{1,0:T(8,128)S(1)}, f32[288,128]{1,0:T(8,128)S(1)}, u32[]{:S(2)}, u32[]{:S(2)}) collective-permute-start(f32[288,128]{1,0:T(8,128)S(1)} %get-tuple-element.47), channel_id=1, source_target_pairs={{0,16},{8,24},{16,0},{24,8},{1,17},{9,25},{17,1},{25,9},{2,18},{10... | collective-permute-start | bytes 442376 | tf_op jit(solution)/shard_map/ppermute | solution.py:652
  22.9 0.0 collective-permute-start.4
  23.0 3.2 %collective-permute-done.2.refs_1_ = f32[288,128]{1,0:T(8,128)S(1)} collective-permute-done((f32[288,128]{1,0:T(8,128)S(1)}, f32[288,128]{1,0:T(8,128)S(1)}, u32[]{:S(2)}, u32[]{:S(2)}) %collective-permute-start.2) | collective-permute-done | bytes 147488 | tf_op jit(solution)/shard_map/ppermute | solution.py:652
  26.2 1.6 %collective-permute-done.3.refs_2_ = f32[288,128]{1,0:T(8,128)S(1)} collective-permute-done((f32[288,128]{1,0:T(8,128)S(1)}, f32[288,128]{1,0:T(8,128)S(1)}, u32[]{:S(2)}, u32[]{:S(2)}) %collective-permute-start.3) | collective-permute-done | bytes 147488 | tf_op jit(solution)/shard_map/ppermute | solution.py:652
  27.8 1.3 %collective-permute-done.4.refs_3_ = f32[288,128]{1,0:T(8,128)S(1)} collective-permute-done((f32[288,128]{1,0:T(8,128)S(1)}, f32[288,128]{1,0:T(8,128)S(1)}, u32[]{:S(2)}, u32[]{:S(2)}) %collective-permute-start.4) | collective-permute-done | bytes 147488 | tf_op jit(solution)/shard_map/ppermute | solution.py:652
  29.1 0.0 copy-done
  29.1 3.9 %shard_map.63 = (f32[4,192,128]{2,1,0:T(8,128)S(1)}, f32[1536,128]{1,0:T(8,128)S(1)}, bf16[96,128,64]{2,1,0:T(8,128)(2,1)S(1)}, bf16[96,32,128]{2,1,0:T(8,128)(2...) custom-call(s32[1]{0:T(128)} %bitcast.b_ref, ...), custom_call_target="tpu_custom_call" | custom-call | tf_op jit(solution)/shard_map/pallas_call | solution.py:639
  33.0 9.2 %shard_map.64 = (f32[192,128]{1,0:T(8,128)S(1)}, f32[192,128]{1,0:T(8,128)S(1)}, f32[192,128]{1,0:T(8,128)S(1)}, f32[192,128]{1,0:T(8,128)S(1)}) custom-call(s32[1]{0:T(128)} %bitcast.b_ref, bf16[16,128,128]{2,1,0:T(8,128)(2,1)S(1)} %get-tuple-element.32.refs_0_, f32[24,128]{1,0:T(8,128)S(1)} %get-tuple-element.44.refs_5_.refs_1_, ...), custom_call_target="tpu_custom_call" | custom-call | tf_op jit(solution)/shard_map/pallas_call | solution.py:639
  42.1 0.5 %collective-permute-start.5 = (f32[192,128]{1,0:T(8,128)S(1)}, f32[192,128]{1,0:T(8,128)S(1)}, u32[]{:S(2)}, u32[]{:S(2)}) collective-permute-start(f32[192,128]{1,0:T(8,128)S(1)} %get-tuple-element.57), channel_id=1, source_target_pairs={{0,8},{8,0},{16,24},{24,16},{1,9},{9,1},{17,25},{25,17},{2,10},{10... | collective-permute-start | bytes 294920 | tf_op jit(solution)/shard_map/ppermute | solution.py:652
  42.6 0.8 %collective-permute-start.6 = (f32[192,128]{1,0:T(8,128)S(1)}, f32[192,128]{1,0:T(8,128)S(1)}, u32[]{:S(2)}, u32[]{:S(2)}) collective-permute-start(f32[192,128]{1,0:T(8,128)S(1)} %get-tuple-element.58), channel_id=1, source_target_pairs={{0,16},{8,24},{16,0},{24,8},{1,17},{9,25},{17,1},{25,9},{2,18},{10... | collective-permute-start | bytes 294920 | tf_op jit(solution)/shard_map/ppermute | solution.py:652
  43.5 2.2 %collective-permute-start.7 = (f32[192,128]{1,0:T(8,128)S(1)}, f32[192,128]{1,0:T(8,128)S(1)}, u32[]{:S(2)}, u32[]{:S(2)}) collective-permute-start(f32[192,128]{1,0:T(8,128)S(1)} %get-tuple-element.59), channel_id=1, source_target_pairs={{0,24},{8,16},{16,8},{24,0},{1,25},{9,17},{17,9},{25,1},{2,26},{10... | collective-permute-start | bytes 294920 | tf_op jit(solution)/shard_map/ppermute | solution.py:652
  45.7 1.1 %collective-permute-done.5.refs_1_ = f32[192,128]{1,0:T(8,128)S(1)} collective-permute-done((f32[192,128]{1,0:T(8,128)S(1)}, f32[192,128]{1,0:T(8,128)S(1)}, u32[]{:S(2)}, u32[]{:S(2)}) %collective-permute-start.5) | collective-permute-done | bytes 98336 | tf_op jit(solution)/shard_map/ppermute | solution.py:652
  46.8 0.4 collective-permute-done.6.refs_2_
  47.3 1.7 %collective-permute-done.7.refs_3_ = f32[192,128]{1,0:T(8,128)S(1)} collective-permute-done((f32[192,128]{1,0:T(8,128)S(1)}, f32[192,128]{1,0:T(8,128)S(1)}, u32[]{:S(2)}, u32[]{:S(2)}) %collective-permute-start.7) | collective-permute-done | bytes 98336 | tf_op jit(solution)/shard_map/ppermute | solution.py:652
  49.0 0.9 %shard_map.65 = (f32[384,128]{1,0:T(8,128)}, f32[384,128]{1,0:T(8,128)}) custom-call(s32[1]{0:T(128)} %bitcast.b_ref, f32[192,128]{1,0:T(8,128)S(1)} %get-tuple-element.56.refs_0_, f32[192,128]{1,0:T(8,128)S(1)} %collective-permute-done.5.refs_1_, f32[192,128]{1,0:T(8,128)S(1)} %collective-permute-done.6.refs_2_, f32[192,128]{1,0:T(8,128)S(1)} %collective-permute-done.7.refs_3_), custom_call_target="tpu_custom_call" | custom-call | tf_op jit(solution)/shard_map/pallas_call | solution.py:639
Async XLA Ops:
  2.7 13.5 %collective-permute-start = (f32[80,128]{1,0:T(8,128)S(1)}, f32[80,128]{1,0:T(8,128)S(1)}, u32[]{:S(2)}, u32[]{:S(2)}) collective-permute-start(f32[80,128]{1,0:T(8,128)S(1)} %get-tuple-element.36), channel_id=1, source_target_pairs={{0,1},{1,2},{2,3},{3,4},{4,5},{5,6},{6,7},{7,0},{8,9},{9,10},{10,1... | collective-permute-start | bytes 122888 | tf_op jit(solution)/shard_map/ppermute | solution.py:692
  3.2 13.0 %collective-permute-start.1 = (f32[80,128]{1,0:T(8,128)S(1)}, f32[80,128]{1,0:T(8,128)S(1)}, u32[]{:S(2)}, u32[]{:S(2)}) collective-permute-start(f32[80,128]{1,0:T(8,128)S(1)} %get-tuple-element.37), channel_id=1, source_target_pairs={{0,7},{1,0},{2,1},{3,2},{4,3},{5,4},{6,5},{7,6},{8,15},{9,8},{10,9... | collective-permute-start | bytes 122888 | tf_op jit(solution)/shard_map/ppermute | solution.py:693
  16.1 12.9 %copy-start = (bf16[4,64,384]{2,1,0:T(8,128)(2,1)S(1)}, bf16[4,64,384]{2,1,0:T(8,128)(2,1)}, u32[]{:S(2)}) copy-start(bf16[4,64,384]{2,1,0:T(8,128)(2,1)} %constant.7.clone.refs_4_) | copy-start | bytes 589828
  19.4 6.8 %collective-permute-start.2 = (f32[288,128]{1,0:T(8,128)S(1)}, f32[288,128]{1,0:T(8,128)S(1)}, u32[]{:S(2)}, u32[]{:S(2)}) collective-permute-start(f32[288,128]{1,0:T(8,128)S(1)} %get-tuple-element.46), channel_id=1, source_target_pairs={{0,8},{8,0},{16,24},{24,16},{1,9},{9,1},{17,25},{25,17},{2,10},{10... | collective-permute-start | bytes 442376 | tf_op jit(solution)/shard_map/ppermute | solution.py:652
  21.4 6.4 %collective-permute-start.3 = (f32[288,128]{1,0:T(8,128)S(1)}, f32[288,128]{1,0:T(8,128)S(1)}, u32[]{:S(2)}, u32[]{:S(2)}) collective-permute-start(f32[288,128]{1,0:T(8,128)S(1)} %get-tuple-element.47), channel_id=1, source_target_pairs={{0,16},{8,24},{16,0},{24,8},{1,17},{9,25},{17,1},{25,9},{2,18},{10... | collective-permute-start | bytes 442376 | tf_op jit(solution)/shard_map/ppermute | solution.py:652
  22.9 6.1 %collective-permute-start.4 = (f32[288,128]{1,0:T(8,128)S(1)}, f32[288,128]{1,0:T(8,128)S(1)}, u32[]{:S(2)}, u32[]{:S(2)}) collective-permute-start(f32[288,128]{1,0:T(8,128)S(1)} %get-tuple-element.48), channel_id=1, source_target_pairs={{0,24},{8,16},{16,8},{24,0},{1,25},{9,17},{17,9},{25,1},{2,26},{10... | collective-permute-start | bytes 442376 | tf_op jit(solution)/shard_map/ppermute | solution.py:652
  42.1 4.7 %collective-permute-start.5 = (f32[192,128]{1,0:T(8,128)S(1)}, f32[192,128]{1,0:T(8,128)S(1)}, u32[]{:S(2)}, u32[]{:S(2)}) collective-permute-start(f32[192,128]{1,0:T(8,128)S(1)} %get-tuple-element.57), channel_id=1, source_target_pairs={{0,8},{8,0},{16,24},{24,16},{1,9},{9,1},{17,25},{25,17},{2,10},{10... | collective-permute-start | bytes 294920 | tf_op jit(solution)/shard_map/ppermute | solution.py:652
  42.6 4.6 %collective-permute-start.6 = (f32[192,128]{1,0:T(8,128)S(1)}, f32[192,128]{1,0:T(8,128)S(1)}, u32[]{:S(2)}, u32[]{:S(2)}) collective-permute-start(f32[192,128]{1,0:T(8,128)S(1)} %get-tuple-element.58), channel_id=1, source_target_pairs={{0,16},{8,24},{16,0},{24,8},{1,17},{9,25},{17,1},{25,9},{2,18},{10... | collective-permute-start | bytes 294920 | tf_op jit(solution)/shard_map/ppermute | solution.py:652
  43.5 5.5 %collective-permute-start.7 = (f32[192,128]{1,0:T(8,128)S(1)}, f32[192,128]{1,0:T(8,128)S(1)}, u32[]{:S(2)}, u32[]{:S(2)}) collective-permute-start(f32[192,128]{1,0:T(8,128)S(1)} %get-tuple-element.59), channel_id=1, source_target_pairs={{0,24},{8,16},{16,8},{24,0},{1,25},{9,17},{17,9},{25,1},{2,26},{10... | collective-permute-start | bytes 294920 | tf_op jit(solution)/shard_map/ppermute | solution.py:652
where the time goes:
time: 50 us; the launch traced here: 49.9 us
  Pallas kernels  28.1 us (56%)
  starting transfers between devices  11.7 us (23%)
  waiting for transfers between devices  9.39 us (19%)
  between operations  0.71 us (1%)
    pallas_call x7, Pallas kernels, call(): pl.pallas_call(kernel, out_shape=outs, in_specs=([] if scalar is None els...  28.1 us
    ppermute x6, waiting for transfers between devices, exchange(): out[k] = lax.ppermute(blocks[k], 'bead', [(i, i ^ k) for i in range(nb)])  9.38 us
    ppermute x6, starting transfers between devices, exchange(): out[k] = lax.ppermute(blocks[k], 'bead', [(i, i ^ k) for i in range(nb)])  7.11 us
    ppermute x1, starting transfers between devices, local(): lax.ppermute(to_left, 'space', [(s, (s - 1) % ns) for s in range(ns)])  4.1 us
  transfers between devices with their start and end apart: 8, of which 6 were waited for; matrix products, arithmetic and copies ran while one was open for 0% of the time, Pallas kernels for 18%

commit v1 on v0

--- a/solution.py
+++ b/solution.py
@@ -55,6 +55,10 @@
 
 def dot_nt(a, b):
     return lax.dot_general(a, b, (((1,), (1,)), ((), ())), preferred_element_type=F32)
+
+
+def block_order(nb):
+    return sorted(range(nb), key=lambda k: (k > 0, -bin(k).count("1"), k))
 
 
 def propagator(beads, beads_dev):
@@ -85,7 +89,8 @@
 
     out = []
     for b in range(beads // beads_dev):
-        bead = ((j // beads_dev) ^ b) * beads_dev + j % beads_dev
+        block = np.array(block_order(beads // beads_dev))[j // beads_dev]
+        bead = (block ^ b) * beads_dev + j % beads_dev
         a = circulant(cosines, bead)
         whole = np.block([[a, circulant(drift, bead)], [-circulant(spring, bead), a]])
         high = whole.astype(ml_dtypes.bfloat16)
@@ -118,7 +123,7 @@
 
 def order_kernel(lb, cells, mols, slots, mol_hbm, x_hbm, p_hbm, *refs):
     xo, po, perm_ref, q_ref, to_right, to_left = refs[:6]
-    mol_ref, x_ref, p_ref, wide, held_ref, sems = refs[6:]
+    mol_ref, x_ref, p_ref, wide, sems = refs[6:]
     copies = [
         pltpu.make_async_copy(source, dest, sems.at[i])
         for i, (source, dest) in enumerate(
@@ -130,7 +135,7 @@
     row = lax.broadcasted_iota(jnp.int32, (slots, slots), 0)
     col = lax.broadcasted_iota(jnp.int32, (slots, slots), 1)
     upper = (row < col).astype(F32).astype(BF16)
-    row = row.astype(F32)
+    rows, row = row, row.astype(F32)
     lane = lax.broadcasted_iota(jnp.int32, (cells, slots), 1)
     far = 4.0 * slots
     wide[...] = jnp.full(wide.shape, slots, jnp.int32)
@@ -149,26 +154,26 @@
     key = jnp.where(
         free, far + dot_nn(free.astype(F32).astype(BF16), upper), lanes.astype(F32)
     )
-    ones = jnp.ones((16, slots), BF16)
+    ones = jnp.ones((slots, slots), BF16)
+    used = jnp.zeros((slots, slots), F32)
     for cell in range(cells):
         held = (row == key[cell : cell + 1]).astype(F32).astype(BF16)
-        held_ref[cell : cell + 1, :] = dot_nt(ones, held)[0:1]
-    used = held_ref[...]
-    rank = dot_nn((1.0 - used).astype(BF16), upper)
-    slot_key = jnp.where(used > 0.5, lane.astype(F32), far + rank)
+        used = jnp.where(col == cell, dot_nn(held, ones), used)
+    rank = dot_nn((col < rows).astype(F32).astype(BF16), (1.0 - used).astype(BF16))
+    slot_key = jnp.where(used > 0.5, row, far + rank)
     copies[1].wait()
     copies[2].wait()
     n = 3 * lb
     for cell in range(cells):
-        slot_column = jnp.broadcast_to(slot_key[cell : cell + 1], (slots, slots)).T
+        slot_column = jnp.broadcast_to(slot_key[:, cell : cell + 1], (slots, slots))
         perm = (slot_column == key[cell : cell + 1]).astype(F32).astype(BF16)
         perm_ref[cell] = perm
-        rows = [
+        atoms = [
             ref[pl.ds(comp * cells + cell, lb, stride=3 * cells), :]
             for ref in (x_ref, p_ref)
             for comp in range(3)
         ]
-        moved = permuted(jnp.concatenate(rows, axis=0), perm)
+        moved = permuted(jnp.concatenate(atoms, axis=0), perm)
         xo[cell] = moved[:n]
         po[cell] = moved[n:]
     for out, xs, ps in (
@@ -310,8 +315,9 @@
         odd = (lane64 >= 27) & (lane64 < 31)
         even = lane64 == 31
         self.signs = [
-            jnp.where(odd, offset, jnp.where(even, offset * offset, 1.0)).astype(BF16)
-            for offset in OFFSETS
+            jnp.where(odd, -1.0, 1.0).astype(BF16),
+            jnp.where(odd | even, 0.0, 1.0).astype(BF16),
+            None,
         ]
         self.zero = jnp.zeros((32, slots), BF16)
 
@@ -326,7 +332,11 @@
         zero = self.zero
         own, m = peers[1]
         left = jnp.concatenate(
-            [store.peers[index] * sign for (store, index), sign in zip(peers, self.signs)], axis=0
+            [
+                store.peers[index] if sign is None else store.peers[index] * sign
+                for (store, index), sign in zip(peers, self.signs)
+            ],
+            axis=0,
         )
         right = jnp.concatenate(
             [
@@ -484,17 +494,17 @@
         force = jnp.concatenate([read_force(source, cell, lb, c) for c in range(3)], axis=0)
         kicked[w - 1] = old + half * force
     width = group + 2 * P_HALO
-    for k in range(nb):
+    for i, k in enumerate(block_order(nb)):
         first = jnp.bitwise_xor(b, k) * group
         for w in range(width):
-            outs[k][pl.ds((width + w) * n, n), :] = kicked[first + w]
+            outs[i][pl.ds((width + w) * n, n), :] = kicked[first + w]
             source = first + w - P_HALO
             inside = x_ref[jnp.clip(source, 0, cells - 1)]
             if w < P_HALO:
                 inside = jnp.where(source < 0, left[pl.ds(n, n), :], inside)
             elif w >= group + P_HALO:
                 inside = jnp.where(source >= cells, right[pl.ds(0, n), :], inside)
-            outs[k][pl.ds(w * n, n), :] = inside
+            outs[i][pl.ds(w * n, n), :] = inside
 
 
 class Rows:
@@ -623,13 +633,13 @@
     ys = refs[:nb]
     outs = refs[nb:]
     b = b_ref[0]
-    for k in range(nb):
+    for i, k in enumerate(block_order(nb)):
         source = jnp.bitwise_xor(b, k)
         for a in range(2):
             for w in range(group):
                 for c in range(3):
                     outs[a][pl.ds(c * cells + source * group + w, lb, stride=3 * cells), :] = ys[
-                        k
+                        i
                     ][pl.ds(((a * group + w) * 3 + c) * lb, lb), :]
 
 
@@ -647,10 +657,10 @@
 
 
 def exchange(blocks, nb):
-    out = list(blocks)
-    for k in reversed(range(1, nb)):
-        out[k] = lax.ppermute(blocks[k], "bead", [(i, i ^ k) for i in range(nb)])
-    return out
+    return [
+        lax.ppermute(block, "bead", [(i, i ^ k) for i in range(nb)]) if k else block
+        for block, k in zip(blocks, block_order(nb))
+    ]
 
 
 def local(nb, ns, positions, momenta, molecules):
@@ -675,7 +685,6 @@
             pltpu.VMEM((rows, slots), F32),
             pltpu.VMEM((rows, slots), F32),
             pltpu.VMEM((3, cells, slots), jnp.int32),
-            pltpu.VMEM((cells, slots), F32),
             pltpu.SemaphoreType.DMA((3,)),
         ],
         None,

time: 50 us -> 49.6 us (level)
  no operation moved by 1% of the time
where the time goes in v1:
time: 49.6 us; the launch traced here: 49.5 us
  Pallas kernels  28.1 us (57%)
  starting transfers between devices  11.8 us (24%)
  waiting for transfers between devices  8.98 us (18%)
  between operations  0.71 us (1%)
    pallas_call x7, Pallas kernels, call(): pl.pallas_call(kernel, out_shape=outs, in_specs=([] if scalar is None els...  28.1 us
    ppermute x6, waiting for transfers between devices, exchange(): lax.ppermute(block, 'bead', [(i, i ^ k) for i in range(nb)])  8.97 us
    ppermute x6, starting transfers between devices, exchange(): lax.ppermute(block, 'bead', [(i, i ^ k) for i in range(nb)])  7.14 us
    ppermute x1, starting transfers between devices, local(): lax.ppermute(to_left, 'space', [(s, (s - 1) % ns) for s in range(ns)])  4.1 us
  transfers between devices with their start and end apart: 8, of which 6 were waited for; matrix products, arithmetic and copies ran while one was open for 0% of the time, Pallas kernels for 18%

profile of v1, /device:TPU:0, one launch (start us, length us, event | category | flops | bytes accessed | tf_op | source)
XLA Modules:
  0.0 49.5 jit_solution(16053224242824481981)
XLA Ops:
  0.6 2.0 %shard_map.59 = (f32[16,24,128]{2,1,0:T(8,128)S(1)}, f32[16,24,128]{2,1,0:T(8,128)S(1)}, bf16[16,128,128]{2,1,0:T(8,128)(2,1)S(1)}, f32[16,128]{1,0:T(8,128)S(1)...) custom-call(s32[3,16,42]{2,1,0:T(8,128)} %bitcast.8, f32[384,128]{1,0:T(8,128)} %bitcast.6, f32[384,128]{1,0:T(8,128)} %bitcast.7), custom_call_target="tpu_custom_call" | custom-call | tf_op jit(solution)/shard_map/pallas_call | solution.py:649
  2.6 0.5 %collective-permute-start = (f32[80,128]{1,0:T(8,128)S(1)}, f32[80,128]{1,0:T(8,128)S(1)}, u32[]{:S(2)}, u32[]{:S(2)}) collective-permute-start(f32[80,128]{1,0:T(8,128)S(1)} %get-tuple-element.36), channel_id=1, source_target_pairs={{0,1},{1,2},{2,3},{3,4},{4,5},{5,6},{6,7},{7,0},{8,9},{9,10},{10,1... | collective-permute-start | bytes 122888 | tf_op jit(solution)/shard_map/ppermute | solution.py:701
  3.1 4.1 %collective-permute-start.1 = (f32[80,128]{1,0:T(8,128)S(1)}, f32[80,128]{1,0:T(8,128)S(1)}, u32[]{:S(2)}, u32[]{:S(2)}) collective-permute-start(f32[80,128]{1,0:T(8,128)S(1)} %get-tuple-element.37), channel_id=1, source_target_pairs={{0,7},{1,0},{2,1},{3,2},{4,3},{5,4},{6,5},{7,6},{8,15},{9,8},{10,9... | collective-permute-start | bytes 122888 | tf_op jit(solution)/shard_map/ppermute | solution.py:702
  7.3 1.2 %shard_map.60 = (f32[1024,128]{1,0:T(8,128)S(1)}, bf16[64,128,64]{2,1,0:T(8,128)(2,1)S(1)}, bf16[64,32,128]{2,1,0:T(8,128)(2,1)S(1)}, bf16[64,32,128]{2,1,0:T(8,...) custom-call(f32[16,24,128]{2,1,0:T(8,128)S(1)} %get-tuple-element.33.x_ref.refs_0_, ...), custom_call_target="tpu_custom_call" | custom-call | tf_op jit(solution)/shard_map/pallas_call | solution.py:649
  8.4 7.6 %shard_map.61.refs_5_ = f32[896,128]{1,0:T(8,128)S(1)} custom-call(f32[16,128]{1,0:T(8,128)S(1)} %get-tuple-element.35.q_ref.refs_2_, f32[1024,128]{1,0:T(8,128)S(1)} %get-tuple-element.38.refs_0_.refs_6_, bf16[64,128,64]{2,1,0:T(8,128)(2,1)S(1)} %get-tuple-element.39.refs_1_.refs_7_, bf16[64,32,128]{2,1,0:T(8,128)(2,1)S(1)} %get-tuple-element.40.refs_2_.refs_8_, ...), custom_call_target="tpu_custom_call" | custom-call | tf_op jit(solution)/shard_map/pallas_call | solution.py:649
  16.1 0.0 collective-permute-done.refs_3_
  16.1 0.0 collective-permute-done.1.refs_4_
  16.1 0.0 copy-start
  16.1 3.3 %shard_map.62 = (f32[288,128]{1,0:T(8,128)S(1)}, f32[288,128]{1,0:T(8,128)S(1)}, f32[288,128]{1,0:T(8,128)S(1)}, f32[288,128]{1,0:T(8,128)S(1)}, f32[24,128]{1,0:T(8,128)S(1)}) custom-call(s32[1]{0:T(128)} %bitcast.b_ref, f32[16,24,128]{2,1,0:T(8,128)S(1)} %get-tuple-element.33.x_ref.refs_0_, f32[16,24,128]{2,1,0:T(8,128)S(1)} %get-tuple-element.34.refs_1_, ...), custom_call_target="tpu_custom_call" | custom-call | tf_op jit(solution)/shard_map/pallas_call | solution.py:649
  19.4 2.9 %collective-permute-start.2 = (f32[288,128]{1,0:T(8,128)S(1)}, f32[288,128]{1,0:T(8,128)S(1)}, u32[]{:S(2)}, u32[]{:S(2)}) collective-permute-start(f32[288,128]{1,0:T(8,128)S(1)} %get-tuple-element.46), channel_id=1, source_target_pairs={{0,24},{8,16},{16,8},{24,0},{1,25},{9,17},{17,9},{25,1},{2,26},{10... | collective-permute-start | bytes 442376 | tf_op jit(solution)/shard_map/ppermute | solution.py:661
  22.3 0.5 %collective-permute-start.3 = (f32[288,128]{1,0:T(8,128)S(1)}, f32[288,128]{1,0:T(8,128)S(1)}, u32[]{:S(2)}, u32[]{:S(2)}) collective-permute-start(f32[288,128]{1,0:T(8,128)S(1)} %get-tuple-element.47), channel_id=1, source_target_pairs={{0,8},{8,0},{16,24},{24,16},{1,9},{9,1},{17,25},{25,17},{2,10},{10... | collective-permute-start | bytes 442376 | tf_op jit(solution)/shard_map/ppermute | solution.py:661
  22.9 0.1 collective-permute-start.4
  23.0 3.3 %collective-permute-done.2.refs_1_ = f32[288,128]{1,0:T(8,128)S(1)} collective-permute-done((f32[288,128]{1,0:T(8,128)S(1)}, f32[288,128]{1,0:T(8,128)S(1)}, u32[]{:S(2)}, u32[]{:S(2)}) %collective-permute-start.2) | collective-permute-done | bytes 147488 | tf_op jit(solution)/shard_map/ppermute | solution.py:661
  26.3 1.6 %collective-permute-done.3.refs_2_ = f32[288,128]{1,0:T(8,128)S(1)} collective-permute-done((f32[288,128]{1,0:T(8,128)S(1)}, f32[288,128]{1,0:T(8,128)S(1)}, u32[]{:S(2)}, u32[]{:S(2)}) %collective-permute-start.3) | collective-permute-done | bytes 147488 | tf_op jit(solution)/shard_map/ppermute | solution.py:661
  27.9 0.1 collective-permute-done.4.refs_3_
  28.0 0.0 copy-done
  28.0 3.9 %shard_map.63 = (f32[4,192,128]{2,1,0:T(8,128)S(1)}, f32[1536,128]{1,0:T(8,128)S(1)}, bf16[96,128,64]{2,1,0:T(8,128)(2,1)S(1)}, bf16[96,32,128]{2,1,0:T(8,128)(2...) custom-call(s32[1]{0:T(128)} %bitcast.b_ref, ...), custom_call_target="tpu_custom_call" | custom-call | tf_op jit(solution)/shard_map/pallas_call | solution.py:649
  31.9 9.2 %shard_map.64 = (f32[192,128]{1,0:T(8,128)S(1)}, f32[192,128]{1,0:T(8,128)S(1)}, f32[192,128]{1,0:T(8,128)S(1)}, f32[192,128]{1,0:T(8,128)S(1)}) custom-call(s32[1]{0:T(128)} %bitcast.b_ref, bf16[16,128,128]{2,1,0:T(8,128)(2,1)S(1)} %get-tuple-element.32.refs_0_, f32[24,128]{1,0:T(8,128)S(1)} %get-tuple-element.44.refs_5_.refs_1_, ...), custom_call_target="tpu_custom_call" | custom-call | tf_op jit(solution)/shard_map/pallas_call | solution.py:649
  41.1 2.4 %collective-permute-start.5 = (f32[192,128]{1,0:T(8,128)S(1)}, f32[192,128]{1,0:T(8,128)S(1)}, u32[]{:S(2)}, u32[]{:S(2)}) collective-permute-start(f32[192,128]{1,0:T(8,128)S(1)} %get-tuple-element.57), channel_id=1, source_target_pairs={{0,24},{8,16},{16,8},{24,0},{1,25},{9,17},{17,9},{25,1},{2,26},{10... | collective-permute-start | bytes 294920 | tf_op jit(solution)/shard_map/ppermute | solution.py:661
  43.5 0.5 %collective-permute-start.6 = (f32[192,128]{1,0:T(8,128)S(1)}, f32[192,128]{1,0:T(8,128)S(1)}, u32[]{:S(2)}, u32[]{:S(2)}) collective-permute-start(f32[192,128]{1,0:T(8,128)S(1)} %get-tuple-element.58), channel_id=1, source_target_pairs={{0,8},{8,0},{16,24},{24,16},{1,9},{9,1},{17,25},{25,17},{2,10},{10... | collective-permute-start | bytes 294920 | tf_op jit(solution)/shard_map/ppermute | solution.py:661
  44.0 0.7 %collective-permute-start.7 = (f32[192,128]{1,0:T(8,128)S(1)}, f32[192,128]{1,0:T(8,128)S(1)}, u32[]{:S(2)}, u32[]{:S(2)}) collective-permute-start(f32[192,128]{1,0:T(8,128)S(1)} %get-tuple-element.59), channel_id=1, source_target_pairs={{0,16},{8,24},{16,0},{24,8},{1,17},{9,25},{17,1},{25,9},{2,18},{10... | collective-permute-start | bytes 294920 | tf_op jit(solution)/shard_map/ppermute | solution.py:661
  44.7 2.0 %collective-permute-done.5.refs_1_ = f32[192,128]{1,0:T(8,128)S(1)} collective-permute-done((f32[192,128]{1,0:T(8,128)S(1)}, f32[192,128]{1,0:T(8,128)S(1)}, u32[]{:S(2)}, u32[]{:S(2)}) %collective-permute-start.5) | collective-permute-done | bytes 98336 | tf_op jit(solution)/shard_map/ppermute | solution.py:661
  46.7 1.4 %collective-permute-done.6.refs_2_ = f32[192,128]{1,0:T(8,128)S(1)} collective-permute-done((f32[192,128]{1,0:T(8,128)S(1)}, f32[192,128]{1,0:T(8,128)S(1)}, u32[]{:S(2)}, u32[]{:S(2)}) %collective-permute-start.6) | collective-permute-done | bytes 98336 | tf_op jit(solution)/shard_map/ppermute | solution.py:661
  48.1 0.5 %collective-permute-done.7.refs_3_ = f32[192,128]{1,0:T(8,128)S(1)} collective-permute-done((f32[192,128]{1,0:T(8,128)S(1)}, f32[192,128]{1,0:T(8,128)S(1)}, u32[]{:S(2)}, u32[]{:S(2)}) %collective-permute-start.7) | collective-permute-done | bytes 98336 | tf_op jit(solution)/shard_map/ppermute | solution.py:661
  48.6 0.9 %shard_map.65 = (f32[384,128]{1,0:T(8,128)}, f32[384,128]{1,0:T(8,128)}) custom-call(s32[1]{0:T(128)} %bitcast.b_ref, f32[192,128]{1,0:T(8,128)S(1)} %get-tuple-element.56.refs_0_, f32[192,128]{1,0:T(8,128)S(1)} %collective-permute-done.5.refs_1_, f32[192,128]{1,0:T(8,128)S(1)} %collective-permute-done.6.refs_2_, f32[192,128]{1,0:T(8,128)S(1)} %collective-permute-done.7.refs_3_), custom_call_target="tpu_custom_call" | custom-call | tf_op jit(solution)/shard_map/pallas_call | solution.py:649
Async XLA Ops:
  2.6 13.5 %collective-permute-start = (f32[80,128]{1,0:T(8,128)S(1)}, f32[80,128]{1,0:T(8,128)S(1)}, u32[]{:S(2)}, u32[]{:S(2)}) collective-permute-start(f32[80,128]{1,0:T(8,128)S(1)} %get-tuple-element.36), channel_id=1, source_target_pairs={{0,1},{1,2},{2,3},{3,4},{4,5},{5,6},{6,7},{7,0},{8,9},{9,10},{10,1... | collective-permute-start | bytes 122888 | tf_op jit(solution)/shard_map/ppermute | solution.py:701
  3.1 13.0 %collective-permute-start.1 = (f32[80,128]{1,0:T(8,128)S(1)}, f32[80,128]{1,0:T(8,128)S(1)}, u32[]{:S(2)}, u32[]{:S(2)}) collective-permute-start(f32[80,128]{1,0:T(8,128)S(1)} %get-tuple-element.37), channel_id=1, source_target_pairs={{0,7},{1,0},{2,1},{3,2},{4,3},{5,4},{6,5},{7,6},{8,15},{9,8},{10,9... | collective-permute-start | bytes 122888 | tf_op jit(solution)/shard_map/ppermute | solution.py:702
  16.1 11.9 %copy-start = (bf16[4,64,384]{2,1,0:T(8,128)(2,1)S(1)}, bf16[4,64,384]{2,1,0:T(8,128)(2,1)}, u32[]{:S(2)}) copy-start(bf16[4,64,384]{2,1,0:T(8,128)(2,1)} %constant.7.clone.refs_4_) | copy-start | bytes 589828
  19.4 6.9 %collective-permute-start.2 = (f32[288,128]{1,0:T(8,128)S(1)}, f32[288,128]{1,0:T(8,128)S(1)}, u32[]{:S(2)}, u32[]{:S(2)}) collective-permute-start(f32[288,128]{1,0:T(8,128)S(1)} %get-tuple-element.46), channel_id=1, source_target_pairs={{0,24},{8,16},{16,8},{24,0},{1,25},{9,17},{17,9},{25,1},{2,26},{10... | collective-permute-start | bytes 442376 | tf_op jit(solution)/shard_map/ppermute | solution.py:661
  22.3 5.6 %collective-permute-start.3 = (f32[288,128]{1,0:T(8,128)S(1)}, f32[288,128]{1,0:T(8,128)S(1)}, u32[]{:S(2)}, u32[]{:S(2)}) collective-permute-start(f32[288,128]{1,0:T(8,128)S(1)} %get-tuple-element.47), channel_id=1, source_target_pairs={{0,8},{8,0},{16,24},{24,16},{1,9},{9,1},{17,25},{25,17},{2,10},{10... | collective-permute-start | bytes 442376 | tf_op jit(solution)/shard_map/ppermute | solution.py:661
  22.9 5.1 %collective-permute-start.4 = (f32[288,128]{1,0:T(8,128)S(1)}, f32[288,128]{1,0:T(8,128)S(1)}, u32[]{:S(2)}, u32[]{:S(2)}) collective-permute-start(f32[288,128]{1,0:T(8,128)S(1)} %get-tuple-element.48), channel_id=1, source_target_pairs={{0,16},{8,24},{16,0},{24,8},{1,17},{9,25},{17,1},{25,9},{2,18},{10... | collective-permute-start | bytes 442376 | tf_op jit(solution)/shard_map/ppermute | solution.py:661
  41.1 5.6 %collective-permute-start.5 = (f32[192,128]{1,0:T(8,128)S(1)}, f32[192,128]{1,0:T(8,128)S(1)}, u32[]{:S(2)}, u32[]{:S(2)}) collective-permute-start(f32[192,128]{1,0:T(8,128)S(1)} %get-tuple-element.57), channel_id=1, source_target_pairs={{0,24},{8,16},{16,8},{24,0},{1,25},{9,17},{17,9},{25,1},{2,26},{10... | collective-permute-start | bytes 294920 | tf_op jit(solution)/shard_map/ppermute | solution.py:661
  43.5 4.6 %collective-permute-start.6 = (f32[192,128]{1,0:T(8,128)S(1)}, f32[192,128]{1,0:T(8,128)S(1)}, u32[]{:S(2)}, u32[]{:S(2)}) collective-permute-start(f32[192,128]{1,0:T(8,128)S(1)} %get-tuple-element.58), channel_id=1, source_target_pairs={{0,8},{8,0},{16,24},{24,16},{1,9},{9,1},{17,25},{25,17},{2,10},{10... | collective-permute-start | bytes 294920 | tf_op jit(solution)/shard_map/ppermute | solution.py:661
  44.0 4.6 %collective-permute-start.7 = (f32[192,128]{1,0:T(8,128)S(1)}, f32[192,128]{1,0:T(8,128)S(1)}, u32[]{:S(2)}, u32[]{:S(2)}) collective-permute-start(f32[192,128]{1,0:T(8,128)S(1)} %get-tuple-element.59), channel_id=1, source_target_pairs={{0,16},{8,24},{16,0},{24,8},{1,17},{9,25},{17,1},{25,9},{2,18},{10... | collective-permute-start | bytes 294920 | tf_op jit(solution)/shard_map/ppermute | solution.py:661

commit v2 on v1

--- a/solution.py
+++ b/solution.py
@@ -121,8 +121,8 @@
     return moved[:n] + moved[n : 2 * n] + moved[2 * n :]
 
 
-def order_kernel(lb, cells, mols, slots, mol_hbm, x_hbm, p_hbm, *refs):
-    xo, po, perm_ref, q_ref, to_right, to_left = refs[:6]
+def order_kernel(lb, cells, mols, slots, odd_ref, mol_hbm, x_hbm, p_hbm, *refs):
+    xo, po, perm_ref, q_ref, first_out, second_out = refs[:6]
     mol_ref, x_ref, p_ref, wide, sems = refs[6:]
     copies = [
         pltpu.make_async_copy(source, dest, sems.at[i])
@@ -176,15 +176,14 @@
         moved = permuted(jnp.concatenate(atoms, axis=0), perm)
         xo[cell] = moved[:n]
         po[cell] = moved[n:]
-    for out, xs, ps in (
-        (to_right, (cells - 2, cells - 1), cells - 1),
-        (to_left, (0, 1), 0),
-    ):
+    odd = odd_ref[0]
+    for out, low in ((first_out, odd), (second_out, 1 - odd)):
         out[9 * lb :, :] = jnp.zeros((8, slots), F32)
-        for e, cell in enumerate(xs):
+        for e in range(2):
+            cell = jnp.where(low == 1, e, cells - 2 + e)
             out[pl.ds(e * n, n), :] = xo[cell]
-            out[pl.ds(9 * lb + e, 1), :] = charges[cell : cell + 1]
-        out[pl.ds(2 * n, n), :] = po[ps]
+            out[pl.ds(9 * lb + e, 1), :] = q_ref[pl.ds(cell, 1), :]
+        out[pl.ds(2 * n, n), :] = po[jnp.where(low == 1, 0, cells - 1)]
 
 
 def put_tiles(scratch, first, count, rows):
@@ -429,12 +428,15 @@
 
 
 def edge_kernel(nb, group, lb, cells, mols, slots, b_ref, *refs):
-    x_ref, p_ref, q_ref, left, right, inner = refs[:6]
+    x_ref, p_ref, q_ref, first, second, inner = refs[:6]
     own = Store(refs[6 : 6 + STORE], lb)
     refs = refs[6 + STORE :]
     outs, q_out = refs[:nb], refs[nb]
-    kicked, halo_forces, keep = refs[nb + 1 : nb + 4]
-    halo = Store(refs[nb + 4 :], lb)
+    kicked, halo_forces, keep, left, right = refs[nb + 1 : nb + 6]
+    halo = Store(refs[nb + 6 :], lb)
+    odd = b_ref[1] == 1
+    left[...] = jnp.where(odd, first[...], second[...])
+    right[...] = jnp.where(odd, second[...], first[...])
     n = 3 * lb
     count = cells + 2 * X_HALO
     b = b_ref[0]
@@ -624,8 +626,8 @@
         state = unpermuted(state, perm_ref[b * group + w])
         for a in range(2):
             for c in range(3):
-                for k in range(nb):
-                    row = (a * 3 + c) * beads + k * lb
+                for i, k in enumerate(block_order(nb)):
+                    row = (a * 3 + c) * beads + i * lb
                     ys[k][pl.ds(((a * group + w) * 3 + c) * lb, lb), :] = state[row : row + lb]
 
 
@@ -633,13 +635,13 @@
     ys = refs[:nb]
     outs = refs[nb:]
     b = b_ref[0]
-    for i, k in enumerate(block_order(nb)):
+    for k in range(nb):
         source = jnp.bitwise_xor(b, k)
         for a in range(2):
             for w in range(group):
                 for c in range(3):
                     outs[a][pl.ds(c * cells + source * group + w, lb, stride=3 * cells), :] = ys[
-                        i
+                        k
                     ][pl.ds(((a * group + w) * 3 + c) * lb, lb), :]
 
 
@@ -656,10 +658,10 @@
     )(*(() if scalar is None else (scalar,)), *operands)
 
 
-def exchange(blocks, nb):
+def exchange(blocks, order):
     return [
-        lax.ppermute(block, "bead", [(i, i ^ k) for i in range(nb)]) if k else block
-        for block, k in zip(blocks, block_order(nb))
+        lax.ppermute(block, "bead", [(i, i ^ k) for i in range(len(order))]) if k else block
+        for block, k in zip(blocks, order)
     ]
 
 
@@ -670,13 +672,14 @@
     beads = lb * nb
     width = group + 2 * P_HALO
     b = lax.axis_index("bead").astype(jnp.int32).reshape(1)
+    odd = (lax.axis_index("space").astype(jnp.int32) & 1).reshape(1)
 
     def shape(*dims):
         return jax.ShapeDtypeStruct(dims, F32)
 
     edge = shape(9 * lb + 8, slots)
     rows = lb * 3 * cells
-    xs, ps, perm, charges, to_right, to_left = call(
+    xs, ps, perm, charges, first, second = call(
         functools.partial(order_kernel, lb, cells, mols, slots),
         [shape(cells, 3 * lb, slots)] * 2
         + [jax.ShapeDtypeStruct((cells, slots, slots), BF16), shape(cells, slots), edge, edge],
@@ -687,7 +690,7 @@
             pltpu.VMEM((3, cells, slots), jnp.int32),
             pltpu.SemaphoreType.DMA((3,)),
         ],
-        None,
+        odd,
         *(
             pltpu.with_memory_space_constraint(a, pltpu.HBM)
             for a in (
@@ -698,8 +701,10 @@
         ),
         space=pltpu.HBM,
     )
-    left = lax.ppermute(to_right, "space", [(s, (s + 1) % ns) for s in range(ns)])
-    right = lax.ppermute(to_left, "space", [(s, (s - 1) % ns) for s in range(ns)])
+    first = lax.ppermute(first, "space", [(s, s ^ 1) for s in range(ns)])
+    second = lax.ppermute(
+        second, "space", [(s, (s + 1 if s % 2 else s - 1) % ns) for s in range(ns)]
+    )
     q_rows = -(-(cells + 2 * X_HALO) // 8) * 8
 
     def store(count, store_beads):
@@ -726,18 +731,20 @@
             pltpu.VMEM((cells + 2 * P_HALO, 3 * lb, slots), F32),
             pltpu.VMEM((4 * lb * 8, slots), F32),
             keep,
+            pltpu.VMEM(edge.shape, F32),
+            pltpu.VMEM(edge.shape, F32),
         ]
         + [pltpu.VMEM(*entry) for entry in store_shapes(4, lb, slots)],
-        b,
+        jnp.concatenate([b, odd]),
         xs,
         ps,
         charges,
-        left,
-        right,
+        first,
+        second,
         inner,
         *own,
     )
-    blocks = exchange(blocks, nb)
+    blocks = exchange(blocks, block_order(nb))
     step = jnp.asarray(propagator(beads, lb))
     xv, *stepped = call(
         functools.partial(steps_kernel, nb, group, lb, mols, slots),
@@ -758,7 +765,7 @@
         xv,
         *stepped,
     )
-    ys = exchange(ys, nb)
+    ys = exchange(ys, range(nb))
     new_x, new_p = call(
         functools.partial(unpack_kernel, nb, group, lb, cells),
         [shape(lb * 3 * cells, slots)] * 2,

time: 49.6 us -> 51.3 us (1.034)
    ppermute x8, starting transfers between devices: 11.8 us -> 12.3 us  [the longest x6 7.11 us: exchange(): lax.ppermute(block, 'bead', [(i, i ^ k) for i in range(len(order))])]
    pallas_call x7, Pallas kernels: 28.1 us -> 28.6 us  [call(): pl.pallas_call(kernel, out_shape=outs, in_specs=([] if scalar is None els...]
  transfers between devices with their start and end apart: 8 -> 8, of which waited for: 6 -> 6; matrix products, arithmetic and copies ran while one was open for 0% -> 0% of each run, Pallas kernels for 18% -> 17%
where the time goes in v2:
time: 51.3 us; the launch traced here: 51.2 us
  Pallas kernels  28.6 us (56%)
  starting transfers between devices  12.3 us (24%)
  waiting for transfers between devices  9.42 us (18%)
  between operations  0.71 us (1%)
    pallas_call x7, Pallas kernels, call(): pl.pallas_call(kernel, out_shape=outs, in_specs=([] if scalar is None els...  28.6 us
    ppermute x6, waiting for transfers between devices, exchange(): lax.ppermute(block, 'bead', [(i, i ^ k) for i in range(len(order))])  9.42 us
    ppermute x6, starting transfers between devices, exchange(): lax.ppermute(block, 'bead', [(i, i ^ k) for i in range(len(order))])  7.11 us
    ppermute x1, starting transfers between devices, local(): lax.ppermute(second, 'space', [(s, (s + 1 if s % 2 else s - 1) % ns) for...  4.71 us
  transfers between devices with their start and end apart: 8, of which 6 were waited for; matrix products, arithmetic and copies ran while one was open for 0% of the time, Pallas kernels for 17%

profile of v2, /device:TPU:0, one launch (start us, length us, event | category | flops | bytes accessed | tf_op | source)
XLA Modules:
  0.0 51.2 jit_solution(15550199228868173112)
XLA Ops:
  0.6 2.0 %shard_map.59 = (f32[16,24,128]{2,1,0:T(8,128)S(1)}, f32[16,24,128]{2,1,0:T(8,128)S(1)}, bf16[16,128,128]{2,1,0:T(8,128)(2,1)S(1)}, f32[16,128]{1,0:T(8,128)S(1)...) custom-call(s32[1]{0:T(128)} %bitcast.1.odd_ref, s32[3,16,42]{2,1,0:T(8,128)} %bitcast.9, f32[384,128]{1,0:T(8,128)} %bitcast.7, ...), custom_call_target="tpu_custom_call" | custom-call | tf_op jit(solution)/shard_map/pallas_call | solution.py:651
  2.7 0.5 %collective-permute-start = (f32[80,128]{1,0:T(8,128)S(1)}, f32[80,128]{1,0:T(8,128)S(1)}, u32[]{:S(2)}, u32[]{:S(2)}) collective-permute-start(f32[80,128]{1,0:T(8,128)S(1)} %get-tuple-element.36), channel_id=1, source_target_pairs={{0,1},{1,0},{2,3},{3,2},{4,5},{5,4},{6,7},{7,6},{8,9},{9,8},{10,11... | collective-permute-start | bytes 122888 | tf_op jit(solution)/shard_map/ppermute | solution.py:704
  3.2 4.7 %collective-permute-start.1 = (f32[80,128]{1,0:T(8,128)S(1)}, f32[80,128]{1,0:T(8,128)S(1)}, u32[]{:S(2)}, u32[]{:S(2)}) collective-permute-start(f32[80,128]{1,0:T(8,128)S(1)} %get-tuple-element.37), channel_id=1, source_target_pairs={{0,7},{1,2},{2,1},{3,4},{4,3},{5,6},{6,5},{7,0},{8,15},{9,10},{10,... | collective-permute-start | bytes 122888 | tf_op jit(solution)/shard_map/ppermute | solution.py:705
  7.9 0.1 pad_add_fusion.b_ref
  8.0 1.2 %shard_map.60 = (f32[1024,128]{1,0:T(8,128)S(1)}, bf16[64,128,64]{2,1,0:T(8,128)(2,1)S(1)}, bf16[64,32,128]{2,1,0:T(8,128)(2,1)S(1)}, bf16[64,32,128]{2,1,0:T(8,...) custom-call(f32[16,24,128]{2,1,0:T(8,128)S(1)} %get-tuple-element.33.x_ref.refs_0_, ...), custom_call_target="tpu_custom_call" | custom-call | tf_op jit(solution)/shard_map/pallas_call | solution.py:651
  9.2 7.6 %shard_map.61.refs_5_ = f32[896,128]{1,0:T(8,128)S(1)} custom-call(f32[16,128]{1,0:T(8,128)S(1)} %get-tuple-element.35.q_ref.refs_2_, f32[1024,128]{1,0:T(8,128)S(1)} %get-tuple-element.38.refs_0_.refs_6_, bf16[64,128,64]{2,1,0:T(8,128)(2,1)S(1)} %get-tuple-element.39.refs_1_.refs_7_, bf16[64,32,128]{2,1,0:T(8,128)(2,1)S(1)} %get-tuple-element.40.refs_2_.refs_8_, ...), custom_call_target="tpu_custom_call" | custom-call | tf_op jit(solution)/shard_map/pallas_call | solution.py:651
  16.8 0.0 collective-permute-done.refs_3_
  16.8 0.0 collective-permute-done.1.refs_4_
  16.8 0.0 copy-start
  16.8 3.8 %shard_map.62 = (f32[288,128]{1,0:T(8,128)S(1)}, f32[288,128]{1,0:T(8,128)S(1)}, f32[288,128]{1,0:T(8,128)S(1)}, f32[288,128]{1,0:T(8,128)S(1)}, f32[24,128]{1,0:T(8,128)S(1)}) custom-call(s32[2]{0:T(128)S(1)} %pad_add_fusion.b_ref, f32[16,24,128]{2,1,0:T(8,128)S(1)} %get-tuple-element.33.x_ref.refs_0_, f32[16,24,128]{2,1,0:T(8,128)S(1)} %get-tuple-element.34.refs_1_, ...), custom_call_target="tpu_custom_call" | custom-call | tf_op jit(solution)/shard_map/pallas_call | solution.py:651
  20.7 2.5 %collective-permute-start.2 = (f32[288,128]{1,0:T(8,128)S(1)}, f32[288,128]{1,0:T(8,128)S(1)}, u32[]{:S(2)}, u32[]{:S(2)}) collective-permute-start(f32[288,128]{1,0:T(8,128)S(1)} %get-tuple-element.46), channel_id=1, source_target_pairs={{0,24},{8,16},{16,8},{24,0},{1,25},{9,17},{17,9},{25,1},{2,26},{10... | collective-permute-start | bytes 442376 | tf_op jit(solution)/shard_map/ppermute | solution.py:663
  23.2 0.5 %collective-permute-start.3 = (f32[288,128]{1,0:T(8,128)S(1)}, f32[288,128]{1,0:T(8,128)S(1)}, u32[]{:S(2)}, u32[]{:S(2)}) collective-permute-start(f32[288,128]{1,0:T(8,128)S(1)} %get-tuple-element.47), channel_id=1, source_target_pairs={{0,8},{8,0},{16,24},{24,16},{1,9},{9,1},{17,25},{25,17},{2,10},{10... | collective-permute-start | bytes 442376 | tf_op jit(solution)/shard_map/ppermute | solution.py:663
  23.7 0.5 collective-permute-start.4
  24.2 2.8 %collective-permute-done.2.refs_1_ = f32[288,128]{1,0:T(8,128)S(1)} collective-permute-done((f32[288,128]{1,0:T(8,128)S(1)}, f32[288,128]{1,0:T(8,128)S(1)}, u32[]{:S(2)}, u32[]{:S(2)}) %collective-permute-start.2) | collective-permute-done | bytes 147488 | tf_op jit(solution)/shard_map/ppermute | solution.py:663
  27.0 1.6 %collective-permute-done.3.refs_2_ = f32[288,128]{1,0:T(8,128)S(1)} collective-permute-done((f32[288,128]{1,0:T(8,128)S(1)}, f32[288,128]{1,0:T(8,128)S(1)}, u32[]{:S(2)}, u32[]{:S(2)}) %collective-permute-start.3) | collective-permute-done | bytes 147488 | tf_op jit(solution)/shard_map/ppermute | solution.py:663
  28.7 0.2 collective-permute-done.4.refs_3_
  28.9 0.0 copy-done
  28.9 3.9 %shard_map.63 = (f32[4,192,128]{2,1,0:T(8,128)S(1)}, f32[1536,128]{1,0:T(8,128)S(1)}, bf16[96,128,64]{2,1,0:T(8,128)(2,1)S(1)}, bf16[96,32,128]{2,1,0:T(8,128)(2...) custom-call(s32[1]{0:T(128)} %bitcast.b_ref, ...), custom_call_target="tpu_custom_call" | custom-call | tf_op jit(solution)/shard_map/pallas_call | solution.py:651
  32.8 9.2 %shard_map.64 = (f32[192,128]{1,0:T(8,128)S(1)}, f32[192,128]{1,0:T(8,128)S(1)}, f32[192,128]{1,0:T(8,128)S(1)}, f32[192,128]{1,0:T(8,128)S(1)}) custom-call(s32[1]{0:T(128)} %bitcast.b_ref, bf16[16,128,128]{2,1,0:T(8,128)(2,1)S(1)} %get-tuple-element.32.refs_0_, f32[24,128]{1,0:T(8,128)S(1)} %get-tuple-element.44.refs_5_.refs_1_, ...), custom_call_target="tpu_custom_call" | custom-call | tf_op jit(solution)/shard_map/pallas_call | solution.py:651
  41.9 1.6 %collective-permute-start.5 = (f32[192,128]{1,0:T(8,128)S(1)}, f32[192,128]{1,0:T(8,128)S(1)}, u32[]{:S(2)}, u32[]{:S(2)}) collective-permute-start(f32[192,128]{1,0:T(8,128)S(1)} %get-tuple-element.57), channel_id=1, source_target_pairs={{0,8},{8,0},{16,24},{24,16},{1,9},{9,1},{17,25},{25,17},{2,10},{10... | collective-permute-start | bytes 294920 | tf_op jit(solution)/shard_map/ppermute | solution.py:663
  43.5 1.3 %collective-permute-start.6 = (f32[192,128]{1,0:T(8,128)S(1)}, f32[192,128]{1,0:T(8,128)S(1)}, u32[]{:S(2)}, u32[]{:S(2)}) collective-permute-start(f32[192,128]{1,0:T(8,128)S(1)} %get-tuple-element.58), channel_id=1, source_target_pairs={{0,16},{8,24},{16,0},{24,8},{1,17},{9,25},{17,1},{25,9},{2,18},{10... | collective-permute-start | bytes 294920 | tf_op jit(solution)/shard_map/ppermute | solution.py:663
  44.7 0.7 %collective-permute-start.7 = (f32[192,128]{1,0:T(8,128)S(1)}, f32[192,128]{1,0:T(8,128)S(1)}, u32[]{:S(2)}, u32[]{:S(2)}) collective-permute-start(f32[192,128]{1,0:T(8,128)S(1)} %get-tuple-element.59), channel_id=1, source_target_pairs={{0,24},{8,16},{16,8},{24,0},{1,25},{9,17},{17,9},{25,1},{2,26},{10... | collective-permute-start | bytes 294920 | tf_op jit(solution)/shard_map/ppermute | solution.py:663
  45.5 1.1 %collective-permute-done.5.refs_1_ = f32[192,128]{1,0:T(8,128)S(1)} collective-permute-done((f32[192,128]{1,0:T(8,128)S(1)}, f32[192,128]{1,0:T(8,128)S(1)}, u32[]{:S(2)}, u32[]{:S(2)}) %collective-permute-start.5) | collective-permute-done | bytes 98336 | tf_op jit(solution)/shard_map/ppermute | solution.py:663
  46.6 1.5 %collective-permute-done.6.refs_2_ = f32[192,128]{1,0:T(8,128)S(1)} collective-permute-done((f32[192,128]{1,0:T(8,128)S(1)}, f32[192,128]{1,0:T(8,128)S(1)}, u32[]{:S(2)}, u32[]{:S(2)}) %collective-permute-start.6) | collective-permute-done | bytes 98336 | tf_op jit(solution)/shard_map/ppermute | solution.py:663
  48.1 2.1 %collective-permute-done.7.refs_3_ = f32[192,128]{1,0:T(8,128)S(1)} collective-permute-done((f32[192,128]{1,0:T(8,128)S(1)}, f32[192,128]{1,0:T(8,128)S(1)}, u32[]{:S(2)}, u32[]{:S(2)}) %collective-permute-start.7) | collective-permute-done | bytes 98336 | tf_op jit(solution)/shard_map/ppermute | solution.py:663
  50.3 0.9 %shard_map.65 = (f32[384,128]{1,0:T(8,128)}, f32[384,128]{1,0:T(8,128)}) custom-call(s32[1]{0:T(128)} %bitcast.b_ref, f32[192,128]{1,0:T(8,128)S(1)} %get-tuple-element.56.refs_0_, f32[192,128]{1,0:T(8,128)S(1)} %collective-permute-done.5.refs_1_, f32[192,128]{1,0:T(8,128)S(1)} %collective-permute-done.6.refs_2_, f32[192,128]{1,0:T(8,128)S(1)} %collective-permute-done.7.refs_3_), custom_call_target="tpu_custom_call" | custom-call | tf_op jit(solution)/shard_map/pallas_call | solution.py:651
Async XLA Ops:
  2.7 14.2 %collective-permute-start = (f32[80,128]{1,0:T(8,128)S(1)}, f32[80,128]{1,0:T(8,128)S(1)}, u32[]{:S(2)}, u32[]{:S(2)}) collective-permute-start(f32[80,128]{1,0:T(8,128)S(1)} %get-tuple-element.36), channel_id=1, source_target_pairs={{0,1},{1,0},{2,3},{3,2},{4,5},{5,4},{6,7},{7,6},{8,9},{9,8},{10,11... | collective-permute-start | bytes 122888 | tf_op jit(solution)/shard_map/ppermute | solution.py:704
  3.2 13.6 %collective-permute-start.1 = (f32[80,128]{1,0:T(8,128)S(1)}, f32[80,128]{1,0:T(8,128)S(1)}, u32[]{:S(2)}, u32[]{:S(2)}) collective-permute-start(f32[80,128]{1,0:T(8,128)S(1)} %get-tuple-element.37), channel_id=1, source_target_pairs={{0,7},{1,2},{2,1},{3,4},{4,3},{5,6},{6,5},{7,0},{8,15},{9,10},{10,... | collective-permute-start | bytes 122888 | tf_op jit(solution)/shard_map/ppermute | solution.py:705
  16.8 12.0 %copy-start = (bf16[4,64,384]{2,1,0:T(8,128)(2,1)S(1)}, bf16[4,64,384]{2,1,0:T(8,128)(2,1)}, u32[]{:S(2)}) copy-start(bf16[4,64,384]{2,1,0:T(8,128)(2,1)} %constant.12.clone.refs_4_) | copy-start | bytes 589828
  20.7 6.4 %collective-permute-start.2 = (f32[288,128]{1,0:T(8,128)S(1)}, f32[288,128]{1,0:T(8,128)S(1)}, u32[]{:S(2)}, u32[]{:S(2)}) collective-permute-start(f32[288,128]{1,0:T(8,128)S(1)} %get-tuple-element.46), channel_id=1, source_target_pairs={{0,24},{8,16},{16,8},{24,0},{1,25},{9,17},{17,9},{25,1},{2,26},{10... | collective-permute-start | bytes 442376 | tf_op jit(solution)/shard_map/ppermute | solution.py:663
  23.2 5.5 %collective-permute-start.3 = (f32[288,128]{1,0:T(8,128)S(1)}, f32[288,128]{1,0:T(8,128)S(1)}, u32[]{:S(2)}, u32[]{:S(2)}) collective-permute-start(f32[288,128]{1,0:T(8,128)S(1)} %get-tuple-element.47), channel_id=1, source_target_pairs={{0,8},{8,0},{16,24},{24,16},{1,9},{9,1},{17,25},{25,17},{2,10},{10... | collective-permute-start | bytes 442376 | tf_op jit(solution)/shard_map/ppermute | solution.py:663
  23.7 5.1 %collective-permute-start.4 = (f32[288,128]{1,0:T(8,128)S(1)}, f32[288,128]{1,0:T(8,128)S(1)}, u32[]{:S(2)}, u32[]{:S(2)}) collective-permute-start(f32[288,128]{1,0:T(8,128)S(1)} %get-tuple-element.48), channel_id=1, source_target_pairs={{0,16},{8,24},{16,0},{24,8},{1,17},{9,25},{17,1},{25,9},{2,18},{10... | collective-permute-start | bytes 442376 | tf_op jit(solution)/shard_map/ppermute | solution.py:663
  41.9 4.7 %collective-permute-start.5 = (f32[192,128]{1,0:T(8,128)S(1)}, f32[192,128]{1,0:T(8,128)S(1)}, u32[]{:S(2)}, u32[]{:S(2)}) collective-permute-start(f32[192,128]{1,0:T(8,128)S(1)} %get-tuple-element.57), channel_id=1, source_target_pairs={{0,8},{8,0},{16,24},{24,16},{1,9},{9,1},{17,25},{25,17},{2,10},{10... | collective-permute-start | bytes 294920 | tf_op jit(solution)/shard_map/ppermute | solution.py:663
  43.5 4.6 %collective-permute-start.6 = (f32[192,128]{1,0:T(8,128)S(1)}, f32[192,128]{1,0:T(8,128)S(1)}, u32[]{:S(2)}, u32[]{:S(2)}) collective-permute-start(f32[192,128]{1,0:T(8,128)S(1)} %get-tuple-element.58), channel_id=1, source_target_pairs={{0,16},{8,24},{16,0},{24,8},{1,17},{9,25},{17,1},{25,9},{2,18},{10... | collective-permute-start | bytes 294920 | tf_op jit(solution)/shard_map/ppermute | solution.py:663
  44.7 5.5 %collective-permute-start.7 = (f32[192,128]{1,0:T(8,128)S(1)}, f32[192,128]{1,0:T(8,128)S(1)}, u32[]{:S(2)}, u32[]{:S(2)}) collective-permute-start(f32[192,128]{1,0:T(8,128)S(1)} %get-tuple-element.59), channel_id=1, source_target_pairs={{0,24},{8,16},{16,8},{24,0},{1,25},{9,17},{17,9},{25,1},{2,26},{10... | collective-permute-start | bytes 294920 | tf_op jit(solution)/shard_map/ppermute | solution.py:663

commit v3 on v1

--- a/solution.py
+++ b/solution.py
@@ -409,6 +409,16 @@
 
         lax.fori_loop(0, total // unroll, step, 0)
 
+    def some(self, store, charges, first, last, pairs, forces):
+        index = 0
+        for w in range(first, last):
+            for pair in pairs:
+                at = w * self.pairs + pair
+                peers = [(store, at + (o - 1) * self.pairs) for o in range(3)]
+                for value in self.pair(peers, charges[w]):
+                    forces[pl.ds(8 * index, 8), :] = value
+                    index += 1
+
 
 def read_force(forces, w, beads, comp):
     return forces[pl.ds(w * beads * 8 + comp, beads, stride=8), :]
@@ -606,27 +616,33 @@
     prepare(store, charges, width, slots)
 
 
-def final_kernel(nb, group, lb, mols, slots, b_ref, *refs):
+def final_kernel(nb, group, lb, mols, slots, which, b_ref, *refs):
     perm_ref, q_ref, xv = refs[:3]
     beads = nb * lb
     store = Store(refs[3 : 3 + STORE], beads)
-    ys = refs[3 + STORE : 3 + STORE + nb]
-    forces, keep = refs[3 + STORE + nb :]
+    ys = refs[3 + STORE : 3 + STORE + len(which)]
+    forces, keep = refs[3 + STORE + len(which) :]
     b = b_ref[0]
     charges = Rows(q_ref, b * group + P_HALO)
     loop = PairLoop(mols, slots, beads, keep)
-    loop.cells(store, charges, P_HALO, P_HALO + group, forces, 32)
+    pairs = [i * (lb // 2) + u for i in which for u in range(lb // 2)]
+    loop.some(store, charges, P_HALO, P_HALO + group, pairs, forces)
+    some = len(which) * lb
     for w in range(group):
-        old = xv[w]
-        m = 3 * beads
-        force = jnp.concatenate([read_force(forces, w, beads, c) for c in range(3)], axis=0)
-        state = jnp.concatenate([old[:m], old[m:] + (0.5 * outer_step) * force], axis=0)
-        state = unpermuted(state, perm_ref[b * group + w])
+        rows = []
         for a in range(2):
             for c in range(3):
-                for k in range(nb):
-                    row = (a * 3 + c) * beads + k * lb
-                    ys[k][pl.ds(((a * group + w) * 3 + c) * lb, lb), :] = state[row : row + lb]
+                old = [xv[w, pl.ds((a * 3 + c) * beads + i * lb, lb), :] for i in which]
+                old = jnp.concatenate(old, axis=0)
+                if a:
+                    old = old + (0.5 * outer_step) * read_force(forces, w, some, c)
+                rows.append(old)
+        state = unpermuted(jnp.concatenate(rows, axis=0), perm_ref[b * group + w])
+        for a in range(2):
+            for c in range(3):
+                for i in range(len(which)):
+                    row = (a * 3 + c) * some + i * lb
+                    ys[i][pl.ds(((a * group + w) * 3 + c) * lb, lb), :] = state[row : row + lb]
 
 
 def unpack_kernel(nb, group, lb, cells, b_ref, *refs):
@@ -643,7 +659,7 @@
                     ][pl.ds(((a * group + w) * 3 + c) * lb, lb), :]
 
 
-def call(kernel, outs, scratch, scalar, *operands, space=pltpu.VMEM):
+def call(kernel, outs, scratch, scalar, *operands, space=pltpu.VMEM, flops=0):
     vmem = pl.BlockSpec(memory_space=pltpu.VMEM)
     smem = pl.BlockSpec(memory_space=pltpu.SMEM)
     return pl.pallas_call(
@@ -652,14 +668,17 @@
         in_specs=([] if scalar is None else [smem]) + [pl.BlockSpec(memory_space=space)] * len(operands),
         out_specs=[vmem] * len(outs),
         scratch_shapes=scratch,
+        cost_estimate=(
+            pl.CostEstimate(flops=flops, bytes_accessed=0, transcendentals=0) if flops else None
+        ),
         compiler_params=pltpu.CompilerParams(vmem_limit_bytes=24 * 1024 * 1024),
     )(*(() if scalar is None else (scalar,)), *operands)
 
 
-def exchange(blocks, nb):
+def exchange(blocks, nb, order):
     return [
         lax.ppermute(block, "bead", [(i, i ^ k) for i in range(nb)]) if k else block
-        for block, k in zip(blocks, block_order(nb))
+        for block, k in zip(blocks, order)
     ]
 
 
@@ -737,7 +756,7 @@
         inner,
         *own,
     )
-    blocks = exchange(blocks, nb)
+    blocks = exchange(blocks, nb, block_order(nb))
     step = jnp.asarray(propagator(beads, lb))
     xv, *stepped = call(
         functools.partial(steps_kernel, nb, group, lb, mols, slots),
@@ -748,17 +767,28 @@
         step,
         q_wide,
     )
-    ys = call(
-        functools.partial(final_kernel, nb, group, lb, mols, slots),
-        [shape(2 * group * 3 * lb, slots)] * nb,
-        [pltpu.VMEM((group * beads * 8, slots), F32), keep],
-        b,
-        perm,
-        q_wide,
-        xv,
-        *stepped,
-    )
-    ys = exchange(ys, nb)
+    order = block_order(nb)
+    early = list(range(1, nb // 2 + 1))
+    late = [0] + list(range(nb // 2 + 1, nb))
+    ys = [None] * nb
+    for which in (early, late):
+        out = call(
+            functools.partial(final_kernel, nb, group, lb, mols, slots, which),
+            [shape(2 * group * 3 * lb, slots)] * len(which),
+            [pltpu.VMEM((group * len(which) * lb * 8, slots), F32), keep],
+            b,
+            perm,
+            q_wide,
+            xv,
+            *stepped,
+            flops=group * len(which) * lb * 3 * slots * slots * 1024,
+        )
+        arrived = [block for block in ys if block is not None]
+        out, xv, arrived = lax.optimization_barrier((out, xv, arrived))
+        for i, block in zip([i for i in range(nb) if ys[i] is not None], arrived):
+            ys[i] = block
+        for i, block in zip(which, exchange(out, nb, [order[i] for i in which])):
+            ys[i] = block
     new_x, new_p = call(
         functools.partial(unpack_kernel, nb, group, lb, cells),
         [shape(lb * 3 * cells, slots)] * 2,

time: 49.6 us -> 50.8 us (1.024)
  Pallas kernels: 28.1 us -> 29.2 us
    pallas_call x7 -> x8, Pallas kernels: 28.1 us -> 29.2 us  [call(): pl.pallas_call(kernel, out_shape=outs, in_specs=([] if scalar is None els...]
  transfers between devices with their start and end apart: 8 -> 8, of which waited for: 6 -> 4; matrix products, arithmetic and copies ran while one was open for 0% -> 0% of each run, Pallas kernels for 18% -> 28%
where the time goes in v3:
time: 50.8 us; the launch traced here: 50.7 us
  Pallas kernels  29.2 us (57%)
  starting transfers between devices  11.8 us (23%)
  waiting for transfers between devices  9 us (18%)
  between operations  0.72 us (1%)
    pallas_call x8, Pallas kernels, call(): pl.pallas_call(kernel, out_shape=outs, in_specs=([] if scalar is None els...  29.2 us
    ppermute x6, waiting for transfers between devices, exchange(): lax.ppermute(block, 'bead', [(i, i ^ k) for i in range(nb)])  8.99 us
    ppermute x6, starting transfers between devices, exchange(): lax.ppermute(block, 'bead', [(i, i ^ k) for i in range(nb)])  7.17 us
    ppermute x1, starting transfers between devices, local(): lax.ppermute(to_left, 'space', [(s, (s - 1) % ns) for s in range(ns)])  4.1 us
  transfers between devices with their start and end apart: 8, of which 4 were waited for; matrix products, arithmetic and copies ran while one was open for 0% of the time, Pallas kernels for 28%

profile of v3, /device:TPU:0, one launch (start us, length us, event | category | flops | bytes accessed | tf_op | source)
XLA Modules:
  0.0 50.7 jit_solution(16949986878675463544)
XLA Ops:
  0.6 2.0 %shard_map.59 = (f32[16,24,128]{2,1,0:T(8,128)S(1)}, f32[16,24,128]{2,1,0:T(8,128)S(1)}, bf16[16,128,128]{2,1,0:T(8,128)(2,1)S(1)}, f32[16,128]{1,0:T(8,128)S(1)...) custom-call(s32[3,16,42]{2,1,0:T(8,128)} %bitcast.8, f32[384,128]{1,0:T(8,128)} %bitcast.6, f32[384,128]{1,0:T(8,128)} %bitcast.7), custom_call_target="tpu_custom_call" | custom-call | tf_op jit(solution)/shard_map/pallas_call | solution.py:665
  2.6 0.5 collective-permute-start
  3.1 4.1 %collective-permute-start.1 = (f32[80,128]{1,0:T(8,128)S(1)}, f32[80,128]{1,0:T(8,128)S(1)}, u32[]{:S(2)}, u32[]{:S(2)}) collective-permute-start(f32[80,128]{1,0:T(8,128)S(1)} %get-tuple-element.44), channel_id=1, source_target_pairs={{0,7},{1,0},{2,1},{3,2},{4,3},{5,4},{6,5},{7,6},{8,15},{9,8},{10,9... | collective-permute-start | bytes 122888 | tf_op jit(solution)/shard_map/ppermute | solution.py:721
  7.3 1.2 %shard_map.60 = (f32[1024,128]{1,0:T(8,128)S(1)}, bf16[64,128,64]{2,1,0:T(8,128)(2,1)S(1)}, bf16[64,32,128]{2,1,0:T(8,128)(2,1)S(1)}, bf16[64,32,128]{2,1,0:T(8,...) custom-call(f32[16,24,128]{2,1,0:T(8,128)S(1)} %get-tuple-element.40.x_ref.refs_0_, ...), custom_call_target="tpu_custom_call" | custom-call | tf_op jit(solution)/shard_map/pallas_call | solution.py:665
  8.4 7.6 %shard_map.61.refs_5_ = f32[896,128]{1,0:T(8,128)S(1)} custom-call(f32[16,128]{1,0:T(8,128)S(1)} %get-tuple-element.42.q_ref.refs_2_, f32[1024,128]{1,0:T(8,128)S(1)} %get-tuple-element.45.refs_0_.refs_6_, bf16[64,128,64]{2,1,0:T(8,128)(2,1)S(1)} %get-tuple-element.46.refs_1_.refs_7_, bf16[64,32,128]{2,1,0:T(8,128)(2,1)S(1)} %get-tuple-element.47.refs_2_.refs_8_, ...), custom_call_target="tpu_custom_call" | custom-call | tf_op jit(solution)/shard_map/pallas_call | solution.py:665
  16.1 0.0 collective-permute-done.refs_3_
  16.1 0.0 collective-permute-done.1.refs_4_
  16.1 0.0 copy-start
  16.1 3.3 %shard_map.62 = (f32[288,128]{1,0:T(8,128)S(1)}, f32[288,128]{1,0:T(8,128)S(1)}, f32[288,128]{1,0:T(8,128)S(1)}, f32[288,128]{1,0:T(8,128)S(1)}, f32[24,128]{1,0:T(8,128)S(1)}) custom-call(s32[1]{0:T(128)} %bitcast.b_ref, f32[16,24,128]{2,1,0:T(8,128)S(1)} %get-tuple-element.40.x_ref.refs_0_, f32[16,24,128]{2,1,0:T(8,128)S(1)} %get-tuple-element.41.refs_1_, ...), custom_call_target="tpu_custom_call" | custom-call | tf_op jit(solution)/shard_map/pallas_call | solution.py:665
  19.4 2.9 %collective-permute-start.2 = (f32[288,128]{1,0:T(8,128)S(1)}, f32[288,128]{1,0:T(8,128)S(1)}, u32[]{:S(2)}, u32[]{:S(2)}) collective-permute-start(f32[288,128]{1,0:T(8,128)S(1)} %get-tuple-element.53), channel_id=1, source_target_pairs={{0,24},{8,16},{16,8},{24,0},{1,25},{9,17},{17,9},{25,1},{2,26},{10... | collective-permute-start | bytes 442376 | tf_op jit(solution)/shard_map/ppermute | solution.py:680
  22.3 0.5 %collective-permute-start.3 = (f32[288,128]{1,0:T(8,128)S(1)}, f32[288,128]{1,0:T(8,128)S(1)}, u32[]{:S(2)}, u32[]{:S(2)}) collective-permute-start(f32[288,128]{1,0:T(8,128)S(1)} %get-tuple-element.54), channel_id=1, source_target_pairs={{0,8},{8,0},{16,24},{24,16},{1,9},{9,1},{17,25},{25,17},{2,10},{10... | collective-permute-start | bytes 442376 | tf_op jit(solution)/shard_map/ppermute | solution.py:680
  22.9 0.1 collective-permute-start.4
  23.0 3.3 %collective-permute-done.2.refs_1_ = f32[288,128]{1,0:T(8,128)S(1)} collective-permute-done((f32[288,128]{1,0:T(8,128)S(1)}, f32[288,128]{1,0:T(8,128)S(1)}, u32[]{:S(2)}, u32[]{:S(2)}) %collective-permute-start.2) | collective-permute-done | bytes 147488 | tf_op jit(solution)/shard_map/ppermute | solution.py:680
  26.3 1.6 %collective-permute-done.3.refs_2_ = f32[288,128]{1,0:T(8,128)S(1)} collective-permute-done((f32[288,128]{1,0:T(8,128)S(1)}, f32[288,128]{1,0:T(8,128)S(1)}, u32[]{:S(2)}, u32[]{:S(2)}) %collective-permute-start.3) | collective-permute-done | bytes 147488 | tf_op jit(solution)/shard_map/ppermute | solution.py:680
  27.9 0.1 collective-permute-done.4.refs_3_
  28.0 0.0 copy-done
  28.0 3.9 %shard_map.63 = (f32[4,192,128]{2,1,0:T(8,128)S(1)}, f32[1536,128]{1,0:T(8,128)S(1)}, bf16[96,128,64]{2,1,0:T(8,128)(2,1)S(1)}, bf16[96,32,128]{2,1,0:T(8,128)(2...) custom-call(s32[1]{0:T(128)} %bitcast.b_ref, ...), custom_call_target="tpu_custom_call" | custom-call | tf_op jit(solution)/shard_map/pallas_call | solution.py:665
  31.9 5.2 %shard_map.64 = (f32[192,128]{1,0:T(8,128)S(1)}, f32[192,128]{1,0:T(8,128)S(1)}) custom-call(s32[1]{0:T(128)} %bitcast.b_ref, bf16[16,128,128]{2,1,0:T(8,128)(2,1)S(1)} %get-tuple-element.39.refs_0_, f32[24,128]{1,0:T(8,128)S(1)} %get-tuple-element.51.refs_5_.refs_1_, f32[4,192,128]{2,1,0:T(8,128)S(1)} %get-tuple-element.65.refs_2_, ...), custom_call_target="tpu_custom_call" | custom-call | flops 3221225472 | tf_op jit(solution)/shard_map/pallas_call | solution.py:665
  37.1 2.3 %collective-permute-start.5 = (f32[192,128]{1,0:T(8,128)S(1)}, f32[192,128]{1,0:T(8,128)S(1)}, u32[]{:S(2)}, u32[]{:S(2)}) collective-permute-start(f32[192,128]{1,0:T(8,128)S(1)} %get-tuple-element.68), channel_id=1, source_target_pairs={{0,24},{8,16},{16,8},{24,0},{1,25},{9,17},{17,9},{25,1},{2,26},{10... | collective-permute-start | bytes 294920 | tf_op jit(solution)/shard_map/ppermute | solution.py:680
  39.4 0.5 %collective-permute-start.6 = (f32[192,128]{1,0:T(8,128)S(1)}, f32[192,128]{1,0:T(8,128)S(1)}, u32[]{:S(2)}, u32[]{:S(2)}) collective-permute-start(f32[192,128]{1,0:T(8,128)S(1)} %get-tuple-element.69), channel_id=1, source_target_pairs={{0,8},{8,0},{16,24},{24,16},{1,9},{9,1},{17,25},{25,17},{2,10},{10... | collective-permute-start | bytes 294920 | tf_op jit(solution)/shard_map/ppermute | solution.py:680
  39.9 5.2 %shard_map.65 = (f32[192,128]{1,0:T(8,128)S(1)}, f32[192,128]{1,0:T(8,128)S(1)}) custom-call(s32[1]{0:T(128)} %bitcast.b_ref, bf16[16,128,128]{2,1,0:T(8,128)(2,1)S(1)} %get-tuple-element.39.refs_0_, f32[24,128]{1,0:T(8,128)S(1)} %get-tuple-element.51.refs_5_.refs_1_, f32[4,192,128]{2,1,0:T(8,128)S(1)} %get-tuple-element.65.refs_2_, ...), custom_call_target="tpu_custom_call" | custom-call | flops 3221225472 | tf_op jit(solution)/shard_map/pallas_call | solution.py:665
  45.1 0.0 collective-permute-done.5.refs_1_
  45.1 0.0 collective-permute-done.6.refs_2_
  45.1 0.7 %collective-permute-start.7 = (f32[192,128]{1,0:T(8,128)S(1)}, f32[192,128]{1,0:T(8,128)S(1)}, u32[]{:S(2)}, u32[]{:S(2)}) collective-permute-start(f32[192,128]{1,0:T(8,128)S(1)} %get-tuple-element.73), channel_id=1, source_target_pairs={{0,16},{8,24},{16,0},{24,8},{1,17},{9,25},{17,1},{25,9},{2,18},{10... | collective-permute-start | bytes 294920 | tf_op jit(solution)/shard_map/ppermute | solution.py:680
  45.9 3.9 %collective-permute-done.7.refs_3_ = f32[192,128]{1,0:T(8,128)S(1)} collective-permute-done((f32[192,128]{1,0:T(8,128)S(1)}, f32[192,128]{1,0:T(8,128)S(1)}, u32[]{:S(2)}, u32[]{:S(2)}) %collective-permute-start.7) | collective-permute-done | bytes 98336 | tf_op jit(solution)/shard_map/ppermute | solution.py:680
  49.8 0.9 %shard_map.66 = (f32[384,128]{1,0:T(8,128)}, f32[384,128]{1,0:T(8,128)}) custom-call(s32[1]{0:T(128)} %bitcast.b_ref, f32[192,128]{1,0:T(8,128)S(1)} %get-tuple-element.70.refs_0_, f32[192,128]{1,0:T(8,128)S(1)} %collective-permute-done.5.refs_1_, f32[192,128]{1,0:T(8,128)S(1)} %collective-permute-done.6.refs_2_, f32[192,128]{1,0:T(8,128)S(1)} %collective-permute-done.7.refs_3_), custom_call_target="tpu_custom_call" | custom-call | tf_op jit(solution)/shard_map/pallas_call | solution.py:665
Async XLA Ops:
  2.6 13.5 %collective-permute-start = (f32[80,128]{1,0:T(8,128)S(1)}, f32[80,128]{1,0:T(8,128)S(1)}, u32[]{:S(2)}, u32[]{:S(2)}) collective-permute-start(f32[80,128]{1,0:T(8,128)S(1)} %get-tuple-element.43), channel_id=1, source_target_pairs={{0,1},{1,2},{2,3},{3,4},{4,5},{5,6},{6,7},{7,0},{8,9},{9,10},{10,1... | collective-permute-start | bytes 122888 | tf_op jit(solution)/shard_map/ppermute | solution.py:720
  3.1 13.0 %collective-permute-start.1 = (f32[80,128]{1,0:T(8,128)S(1)}, f32[80,128]{1,0:T(8,128)S(1)}, u32[]{:S(2)}, u32[]{:S(2)}) collective-permute-start(f32[80,128]{1,0:T(8,128)S(1)} %get-tuple-element.44), channel_id=1, source_target_pairs={{0,7},{1,0},{2,1},{3,2},{4,3},{5,4},{6,5},{7,6},{8,15},{9,8},{10,9... | collective-permute-start | bytes 122888 | tf_op jit(solution)/shard_map/ppermute | solution.py:721
  16.1 11.9 %copy-start = (bf16[4,64,384]{2,1,0:T(8,128)(2,1)S(1)}, bf16[4,64,384]{2,1,0:T(8,128)(2,1)}, u32[]{:S(2)}) copy-start(bf16[4,64,384]{2,1,0:T(8,128)(2,1)} %constant.7.clone.refs_4_) | copy-start | bytes 589828
  19.4 6.9 %collective-permute-start.2 = (f32[288,128]{1,0:T(8,128)S(1)}, f32[288,128]{1,0:T(8,128)S(1)}, u32[]{:S(2)}, u32[]{:S(2)}) collective-permute-start(f32[288,128]{1,0:T(8,128)S(1)} %get-tuple-element.53), channel_id=1, source_target_pairs={{0,24},{8,16},{16,8},{24,0},{1,25},{9,17},{17,9},{25,1},{2,26},{10... | collective-permute-start | bytes 442376 | tf_op jit(solution)/shard_map/ppermute | solution.py:680
  22.3 5.6 %collective-permute-start.3 = (f32[288,128]{1,0:T(8,128)S(1)}, f32[288,128]{1,0:T(8,128)S(1)}, u32[]{:S(2)}, u32[]{:S(2)}) collective-permute-start(f32[288,128]{1,0:T(8,128)S(1)} %get-tuple-element.54), channel_id=1, source_target_pairs={{0,8},{8,0},{16,24},{24,16},{1,9},{9,1},{17,25},{25,17},{2,10},{10... | collective-permute-start | bytes 442376 | tf_op jit(solution)/shard_map/ppermute | solution.py:680
  22.9 5.1 %collective-permute-start.4 = (f32[288,128]{1,0:T(8,128)S(1)}, f32[288,128]{1,0:T(8,128)S(1)}, u32[]{:S(2)}, u32[]{:S(2)}) collective-permute-start(f32[288,128]{1,0:T(8,128)S(1)} %get-tuple-element.55), channel_id=1, source_target_pairs={{0,16},{8,24},{16,0},{24,8},{1,17},{9,25},{17,1},{25,9},{2,18},{10... | collective-permute-start | bytes 442376 | tf_op jit(solution)/shard_map/ppermute | solution.py:680
  37.1 8.0 %collective-permute-start.5 = (f32[192,128]{1,0:T(8,128)S(1)}, f32[192,128]{1,0:T(8,128)S(1)}, u32[]{:S(2)}, u32[]{:S(2)}) collective-permute-start(f32[192,128]{1,0:T(8,128)S(1)} %get-tuple-element.68), channel_id=1, source_target_pairs={{0,24},{8,16},{16,8},{24,0},{1,25},{9,17},{17,9},{25,1},{2,26},{10... | collective-permute-start | bytes 294920 | tf_op jit(solution)/shard_map/ppermute | solution.py:680
  39.4 5.7 %collective-permute-start.6 = (f32[192,128]{1,0:T(8,128)S(1)}, f32[192,128]{1,0:T(8,128)S(1)}, u32[]{:S(2)}, u32[]{:S(2)}) collective-permute-start(f32[192,128]{1,0:T(8,128)S(1)} %get-tuple-element.69), channel_id=1, source_target_pairs={{0,8},{8,0},{16,24},{24,16},{1,9},{9,1},{17,25},{25,17},{2,10},{10... | collective-permute-start | bytes 294920 | tf_op jit(solution)/shard_map/ppermute | solution.py:680
  45.1 4.7 %collective-permute-start.7 = (f32[192,128]{1,0:T(8,128)S(1)}, f32[192,128]{1,0:T(8,128)S(1)}, u32[]{:S(2)}, u32[]{:S(2)}) collective-permute-start(f32[192,128]{1,0:T(8,128)S(1)} %get-tuple-element.73), channel_id=1, source_target_pairs={{0,16},{8,24},{16,0},{24,8},{1,17},{9,25},{17,1},{25,9},{2,18},{10... | collective-permute-start | bytes 294920 | tf_op jit(solution)/shard_map/ppermute | solution.py:680

commit v4 on v1

--- a/solution.py
+++ b/solution.py
@@ -24,10 +24,6 @@
 outer_step = 0.02
 inner_step = 0.01
 oxygen_mass = 16.0
-
-REACH = 1
-X_HALO = 2 * REACH
-P_HALO = REACH
 
 F32 = jnp.float32
 BF16 = jnp.bfloat16
@@ -176,15 +172,14 @@
         moved = permuted(jnp.concatenate(atoms, axis=0), perm)
         xo[cell] = moved[:n]
         po[cell] = moved[n:]
-    for out, xs, ps in (
-        (to_right, (cells - 2, cells - 1), cells - 1),
-        (to_left, (0, 1), 0),
-    ):
-        out[9 * lb :, :] = jnp.zeros((8, slots), F32)
-        for e, cell in enumerate(xs):
-            out[pl.ds(e * n, n), :] = xo[cell]
-            out[pl.ds(9 * lb + e, 1), :] = charges[cell : cell + 1]
-        out[pl.ds(2 * n, n), :] = po[ps]
+    write_ends(to_right, to_left, xo, charges, lb, cells, slots)
+
+
+def write_ends(to_right, to_left, xs, charges, lb, cells, slots):
+    for out, cell in ((to_right, cells - 1), (to_left, 0)):
+        out[3 * lb :, :] = jnp.zeros((8, slots), F32)
+        out[pl.ds(0, 3 * lb), :] = xs[cell]
+        out[pl.ds(3 * lb, 1), :] = charges[cell : cell + 1, :]
 
 
 def put_tiles(scratch, first, count, rows):
@@ -428,83 +423,80 @@
     PairLoop(mols, slots, lb, keep).cells(store, Rows(q_ref, 0), 1, cells - 1, forces, 64)
 
 
-def edge_kernel(nb, group, lb, cells, mols, slots, b_ref, *refs):
+def edge_forces(cells, lb, mols, slots, x_ref, q_ref, left, right, inner, own, scratch):
+    forces, keep = scratch[:2]
+    halo = Store(scratch[2:], lb)
+    n = 3 * lb
+    charge = [left[pl.ds(n, 1), :], right[pl.ds(n, 1), :]]
+    for e, edge in enumerate((left, right)):
+        rows = edge[pl.ds(0, n), :]
+        build_tiles(halo.tiles, e * lb, lb, rows[:lb], rows[lb : 2 * lb], rows[2 * lb :])
+
+    class Edges:
+        def __getitem__(self, e):
+            return jnp.where(e == 0, charge[0], charge[1])
+
+    prepare(halo, Edges(), 2, slots)
+    loop = PairLoop(mols, slots, lb, keep)
+    last = cells - 1
+    near = (
+        (0, ((halo, 0), (own, 0), (own, 1))),
+        (last, ((own, last - 1), (own, last), (halo, 1))),
+    )
+    for e, (cell, stores) in enumerate(near):
+        for pair in range(loop.pairs):
+            peers = [(store, at * loop.pairs + pair) for store, at in stores]
+            out = loop.pair(peers, q_ref[cell : cell + 1, :])
+            for h in range(2):
+                forces[pl.ds((e * lb + 2 * pair + h) * 8, 8), :] = out[h]
+
+    def read(w):
+        source, at = (inner, w - 1) if 0 < w < last else (forces, 0 if w == 0 else 1)
+        return jnp.concatenate([read_force(source, at, lb, c) for c in range(3)], axis=0)
+
+    return read
+
+
+def kick_kernel(nb, group, lb, cells, mols, slots, b_ref, *refs):
     x_ref, p_ref, q_ref, left, right, inner = refs[:6]
     own = Store(refs[6 : 6 + STORE], lb)
-    refs = refs[6 + STORE :]
-    outs, q_out = refs[:nb], refs[nb]
-    kicked, halo_forces, keep = refs[nb + 1 : nb + 4]
-    halo = Store(refs[nb + 4 :], lb)
+    outs = refs[6 + STORE : 6 + STORE + nb]
+    kicked, *scratch = refs[6 + STORE + nb :]
+    read = edge_forces(cells, lb, mols, slots, x_ref, q_ref, left, right, inner, own, scratch)
     n = 3 * lb
-    count = cells + 2 * X_HALO
-    b = b_ref[0]
-
-    charge_rows = [left[pl.ds(9 * lb + e, 1), :] for e in range(2)]
-    charge_rows += [q_ref[c : c + 1, :] for c in range(cells)]
-    charge_rows += [right[pl.ds(9 * lb + e, 1), :] for e in range(2)]
-    q_out[...] = jnp.zeros(q_out.shape, F32)
-    for w in range(count):
-        q_out[w : w + 1, :] = charge_rows[w]
-    for e in range(4):
-        edge = (left, right)[e // 2]
-        rows = edge[pl.ds((e % 2) * n, n), :]
-        build_tiles(halo.tiles, e * lb, lb, rows[:lb], rows[lb : 2 * lb], rows[2 * lb :])
-
-    class Edges:
-        def __getitem__(self, e):
-            return q_out[pl.ds(jnp.where(e < 2, e, e + cells), 1), :]
-
-    prepare(halo, Edges(), 4, slots)
-    loop = PairLoop(mols, slots, lb, keep)
-
-    def place(w):
-        if w < X_HALO:
-            return halo, w
-        if w >= cells + X_HALO:
-            return halo, w - cells
-        return own, w - X_HALO
-
-    targets = (1, 2, cells + 1, cells + 2)
-
-    def edge_step(step, carry):
-        for e, w in enumerate(targets):
-            for u in range(loop.unroll):
-                index = step * loop.unroll + u
-                peers = [
-                    (store, cell * loop.pairs + index) for store, cell in map(place, (w - 1, w, w + 1))
-                ]
-                out = loop.pair(peers, charge_rows[w])
-                for h in range(2):
-                    at = (e * lb + 2 * index + h) * 8
-                    halo_forces[pl.ds(pl.multiple_of(at, 8), 8), :] = out[h]
-        return carry
-
-    lax.fori_loop(0, loop.per_cell, edge_step, 0)
-    half = 0.5 * outer_step
-    for w in range(1, count - 1):
-        if w < X_HALO:
-            old = left[pl.ds(2 * n, n), :]
-        elif w >= cells + X_HALO:
-            old = right[pl.ds(2 * n, n), :]
-        else:
-            old = p_ref[w - X_HALO]
-        source, cell = (
-            (halo_forces, targets.index(w)) if w in targets else (inner, w - X_HALO - 1)
-        )
-        force = jnp.concatenate([read_force(source, cell, lb, c) for c in range(3)], axis=0)
-        kicked[w - 1] = old + half * force
-    width = group + 2 * P_HALO
+    for w in range(cells):
+        kicked[w] = p_ref[w] + (0.5 * outer_step) * read(w)
     for i, k in enumerate(block_order(nb)):
-        first = jnp.bitwise_xor(b, k) * group
-        for w in range(width):
-            outs[i][pl.ds((width + w) * n, n), :] = kicked[first + w]
-            source = first + w - P_HALO
-            inside = x_ref[jnp.clip(source, 0, cells - 1)]
-            if w < P_HALO:
-                inside = jnp.where(source < 0, left[pl.ds(n, n), :], inside)
-            elif w >= group + P_HALO:
-                inside = jnp.where(source >= cells, right[pl.ds(0, n), :], inside)
-            outs[i][pl.ds(w * n, n), :] = inside
+        first = jnp.bitwise_xor(b_ref[0], k) * group
+        for w in range(group):
+            outs[i][pl.ds(w * n, n), :] = x_ref[first + w]
+            outs[i][pl.ds((group + w) * n, n), :] = kicked[first + w]
+
+
+def gather_kernel(nb, group, lb, cells, slots, b_ref, *refs):
+    blocks, q_ref = refs[:nb], refs[nb]
+    xs, ps, to_right, to_left = refs[nb + 1 :]
+    n = 3 * lb
+    for i, k in enumerate(block_order(nb)):
+        first = jnp.bitwise_xor(b_ref[0], k) * group
+        for w in range(group):
+            xs[first + w] = blocks[i][pl.ds(w * n, n), :]
+            ps[first + w] = blocks[i][pl.ds((group + w) * n, n), :]
+    write_ends(to_right, to_left, xs, q_ref, lb, cells, slots)
+
+
+def final_kernel(cells, lb, mols, slots, *refs):
+    x_ref, p_ref, q_ref, left, right, inner, perm_ref = refs[:7]
+    own = Store(refs[7 : 7 + STORE], lb)
+    outs, scratch = refs[7 + STORE : 9 + STORE], refs[9 + STORE :]
+    read = edge_forces(cells, lb, mols, slots, x_ref, q_ref, left, right, inner, own, scratch)
+    for w in range(cells):
+        state = jnp.concatenate([x_ref[w], p_ref[w] + (0.5 * outer_step) * read(w)], axis=0)
+        state = unpermuted(state, perm_ref[w])
+        for a in range(2):
+            for c in range(3):
+                row = (a * 3 + c) * lb
+                outs[a][pl.ds(c * cells + w, lb, stride=3 * cells), :] = state[row : row + lb]
 
 
 class Rows:
@@ -543,14 +535,13 @@
 
 def steps_kernel(nb, group, lb, mols, slots, b_ref, *refs):
     blocks = refs[:nb]
-    step_ref, q_ref, xv = refs[nb : nb + 3]
+    step_ref, q_ref = refs[nb : nb + 2]
+    outs = refs[nb + 2 :]
     beads = nb * lb
-    store = Store(refs[nb + 3 :], beads)
-    width = group + 2 * P_HALO
     n = 3 * lb
     b = b_ref[0]
     step = step_ref[b]
-    charges = Rows(q_ref, b * group + P_HALO)
+    charges = Rows(q_ref, b * group)
 
     def advance(states):
         flat = [
@@ -569,7 +560,7 @@
 
     def gather(w, a, comp):
         return jnp.concatenate(
-            [block[pl.ds((a * width + w) * n + comp * lb, lb), :] for block in blocks], axis=0
+            [block[pl.ds((a * group + w) * n + comp * lb, lb), :] for block in blocks], axis=0
         )
 
     def kick(state, oxygen, scale):
@@ -577,8 +568,8 @@
         force = bond_forces(*pos, oxygen, mols, slots)
         return pos, [v + scale * f for v, f in zip(vel, force)]
 
-    for first in range(0, width, 2):
-        members = range(first, min(first + 2, width))
+    for first in range(0, group, 2):
+        members = range(first, min(first + 2, group))
         charge = [charges[w] for w in members]
         oxygen = [(q < -1.5).astype(F32) for q in charge]
         inverse = [jnp.where(q < -1.5, 1.0 / oxygen_mass, 1.0) for q in charge]
@@ -596,51 +587,13 @@
             ]
             states = advance(states)
         for w, state, q, o, scale in zip(members, states, charge, oxygen, inverse):
-            if 1 <= w <= width - 2:
-                pos, vel = kick(state, o, (0.5 * inner_step) * scale)
-                mass = jnp.where(q < -1.5, oxygen_mass, 1.0)
+            pos, vel = kick(state, o, (0.5 * inner_step) * scale)
+            mass = jnp.where(q < -1.5, oxygen_mass, 1.0)
+            for a, values in enumerate((pos, [v * mass for v in vel])):
                 for c in range(3):
-                    xv[w - 1, pl.ds(c * beads, beads), :] = pos[c]
-                    xv[w - 1, pl.ds((3 + c) * beads, beads), :] = vel[c] * mass
-            build_tiles(store.tiles, w * beads, beads, *state[0])
-    prepare(store, charges, width, slots)
-
-
-def final_kernel(nb, group, lb, mols, slots, b_ref, *refs):
-    perm_ref, q_ref, xv = refs[:3]
-    beads = nb * lb
-    store = Store(refs[3 : 3 + STORE], beads)
-    ys = refs[3 + STORE : 3 + STORE + nb]
-    forces, keep = refs[3 + STORE + nb :]
-    b = b_ref[0]
-    charges = Rows(q_ref, b * group + P_HALO)
-    loop = PairLoop(mols, slots, beads, keep)
-    loop.cells(store, charges, P_HALO, P_HALO + group, forces, 32)
-    for w in range(group):
-        old = xv[w]
-        m = 3 * beads
-        force = jnp.concatenate([read_force(forces, w, beads, c) for c in range(3)], axis=0)
-        state = jnp.concatenate([old[:m], old[m:] + (0.5 * outer_step) * force], axis=0)
-        state = unpermuted(state, perm_ref[b * group + w])
-        for a in range(2):
-            for c in range(3):
-                for k in range(nb):
-                    row = (a * 3 + c) * beads + k * lb
-                    ys[k][pl.ds(((a * group + w) * 3 + c) * lb, lb), :] = state[row : row + lb]
-
-
-def unpack_kernel(nb, group, lb, cells, b_ref, *refs):
-    ys = refs[:nb]
-    outs = refs[nb:]
-    b = b_ref[0]
-    for i, k in enumerate(block_order(nb)):
-        source = jnp.bitwise_xor(b, k)
-        for a in range(2):
-            for w in range(group):
-                for c in range(3):
-                    outs[a][pl.ds(c * cells + source * group + w, lb, stride=3 * cells), :] = ys[
-                        i
-                    ][pl.ds(((a * group + w) * 3 + c) * lb, lb), :]
+                    for i in range(nb):
+                        rows = values[c][i * lb : (i + 1) * lb]
+                        outs[i][pl.ds((a * group + w) * n + c * lb, lb), :] = rows
 
 
 def call(kernel, outs, scratch, scalar, *operands, space=pltpu.VMEM):
@@ -668,18 +621,45 @@
     mols = molecules.shape[1]
     group = cells // nb
     beads = lb * nb
-    width = group + 2 * P_HALO
     b = lax.axis_index("bead").astype(jnp.int32).reshape(1)
 
     def shape(*dims):
         return jax.ShapeDtypeStruct(dims, F32)
 
-    edge = shape(9 * lb + 8, slots)
     rows = lb * 3 * cells
+    state = [shape(cells, 3 * lb, slots)] * 2
+    ends = [shape(3 * lb + 8, slots)] * 2
+    blocks = [shape(2 * group * 3 * lb, slots)] * nb
+    store = [jax.ShapeDtypeStruct(*entry) for entry in store_shapes(cells, lb, slots)]
+    keep = pltpu.VMEM((slots, slots), F32)
+    edge_scratch = [pltpu.VMEM((2 * lb * 8, slots), F32), keep] + [
+        pltpu.VMEM(*entry) for entry in store_shapes(2, lb, slots)
+    ]
+
+    def halos(to_right, to_left):
+        left = lax.ppermute(to_right, "space", [(s, (s + 1) % ns) for s in range(ns)])
+        right = lax.ppermute(to_left, "space", [(s, (s - 1) % ns) for s in range(ns)])
+        return left, right
+
+    def inside(xs, charges):
+        own = call(
+            functools.partial(own_kernel, cells, lb, slots), store, [], None, xs, charges
+        )
+        (inner,) = call(
+            functools.partial(interior_kernel, cells, lb, mols, slots),
+            [shape((cells - 2) * lb * 8, slots)],
+            [keep],
+            None,
+            charges,
+            *own,
+        )
+        return own, inner
+
     xs, ps, perm, charges, to_right, to_left = call(
         functools.partial(order_kernel, lb, cells, mols, slots),
-        [shape(cells, 3 * lb, slots)] * 2
-        + [jax.ShapeDtypeStruct((cells, slots, slots), BF16), shape(cells, slots), edge, edge],
+        state
+        + [jax.ShapeDtypeStruct((cells, slots, slots), BF16), shape(cells, slots)]
+        + ends,
         [
             pltpu.VMEM((3, cells, mols), jnp.int32),
             pltpu.VMEM((rows, slots), F32),
@@ -698,36 +678,12 @@
         ),
         space=pltpu.HBM,
     )
-    left = lax.ppermute(to_right, "space", [(s, (s + 1) % ns) for s in range(ns)])
-    right = lax.ppermute(to_left, "space", [(s, (s - 1) % ns) for s in range(ns)])
-    q_rows = -(-(cells + 2 * X_HALO) // 8) * 8
-
-    def store(count, store_beads):
-        return [
-            jax.ShapeDtypeStruct(*entry) for entry in store_shapes(count, store_beads, slots)
-        ]
-
-    keep = pltpu.VMEM((slots, slots), F32)
-    own = call(
-        functools.partial(own_kernel, cells, lb, slots), store(cells, lb), [], None, xs, charges
-    )
-    (inner,) = call(
-        functools.partial(interior_kernel, cells, lb, mols, slots),
-        [shape((cells - 2) * lb * 8, slots)],
-        [keep],
-        None,
-        charges,
-        *own,
-    )
-    *blocks, q_wide = call(
-        functools.partial(edge_kernel, nb, group, lb, cells, mols, slots),
-        [shape(2 * width * 3 * lb, slots)] * nb + [shape(q_rows, slots)],
-        [
-            pltpu.VMEM((cells + 2 * P_HALO, 3 * lb, slots), F32),
-            pltpu.VMEM((4 * lb * 8, slots), F32),
-            keep,
-        ]
-        + [pltpu.VMEM(*entry) for entry in store_shapes(4, lb, slots)],
+    left, right = halos(to_right, to_left)
+    own, inner = inside(xs, charges)
+    sent = call(
+        functools.partial(kick_kernel, nb, group, lb, cells, mols, slots),
+        blocks,
+        [pltpu.VMEM((cells, 3 * lb, slots), F32)] + edge_scratch,
         b,
         xs,
         ps,
@@ -737,34 +693,38 @@
         inner,
         *own,
     )
-    blocks = exchange(blocks, nb)
-    step = jnp.asarray(propagator(beads, lb))
-    xv, *stepped = call(
+    stepped = call(
         functools.partial(steps_kernel, nb, group, lb, mols, slots),
-        [shape(group, 6 * beads, slots)] + store(width, beads),
+        blocks,
         [],
         b,
-        *blocks,
-        step,
-        q_wide,
-    )
-    ys = call(
-        functools.partial(final_kernel, nb, group, lb, mols, slots),
-        [shape(2 * group * 3 * lb, slots)] * nb,
-        [pltpu.VMEM((group * beads * 8, slots), F32), keep],
-        b,
-        perm,
-        q_wide,
-        xv,
-        *stepped,
-    )
-    ys = exchange(ys, nb)
-    new_x, new_p = call(
-        functools.partial(unpack_kernel, nb, group, lb, cells),
-        [shape(lb * 3 * cells, slots)] * 2,
+        *exchange(sent, nb),
+        jnp.asarray(propagator(beads, lb)),
+        charges,
+    )
+    xs, ps, to_right, to_left = call(
+        functools.partial(gather_kernel, nb, group, lb, cells, slots),
+        state + ends,
         [],
         b,
-        *ys,
+        *exchange(stepped, nb),
+        charges,
+    )
+    left, right = halos(to_right, to_left)
+    own, inner = inside(xs, charges)
+    new_x, new_p = call(
+        functools.partial(final_kernel, cells, lb, mols, slots),
+        [shape(rows, slots)] * 2,
+        edge_scratch,
+        None,
+        xs,
+        ps,
+        charges,
+        left,
+        right,
+        inner,
+        perm,
+        *own,
     )
     return new_x.reshape(positions.shape), new_p.reshape(positions.shape)
 

time: 49.6 us -> 50.2 us (1.012)
  starting transfers between devices: 11.8 us -> 15.3 us
  Pallas kernels: 28.1 us -> 26.4 us
  waiting for transfers between devices: 8.98 us -> 7.59 us
    ppermute x2 -> x4, starting transfers between devices: 4.61 us -> 8.2 us  [the longest x2 7.63 us: halos(): lax.ppermute(to_left, 'space', [(s, (s - 1) % ns) for s in range(ns)])]
    pallas_call x7 -> x9, Pallas kernels: 28.1 us -> 26.4 us  [call(): pl.pallas_call(kernel, out_shape=outs, in_specs=([] if scalar is None els...]
    ppermute x6, waiting for transfers between devices: 8.97 us -> 7.58 us  [exchange(): lax.ppermute(block, 'bead', [(i, i ^ k) for i in range(nb)])]
  transfers between devices with their start and end apart: 8 -> 10, of which waited for: 6 -> 6; matrix products, arithmetic and copies ran while one was open for 0% -> 0% of each run, Pallas kernels for 18% -> 35%
where the time goes in v4:
time: 50.2 us; the launch traced here: 50.1 us
  Pallas kernels  26.4 us (53%)
  starting transfers between devices  15.3 us (30%)
  waiting for transfers between devices  7.59 us (15%)
  between operations  0.74 us (1%)
    pallas_call x9, Pallas kernels, call(): pl.pallas_call(kernel, out_shape=outs, in_specs=([] if scalar is None els...  26.4 us
    ppermute x2, starting transfers between devices, halos(): lax.ppermute(to_left, 'space', [(s, (s - 1) % ns) for s in range(ns)])  7.63 us
    ppermute x6, waiting for transfers between devices, exchange(): lax.ppermute(block, 'bead', [(i, i ^ k) for i in range(nb)])  7.58 us
    ppermute x6, starting transfers between devices, exchange(): lax.ppermute(block, 'bead', [(i, i ^ k) for i in range(nb)])  7.15 us
  transfers between devices with their start and end apart: 10, of which 6 were waited for; matrix products, arithmetic and copies ran while one was open for 0% of the time, Pallas kernels for 35%

profile of v4, /device:TPU:0, one launch (start us, length us, event | category | flops | bytes accessed | tf_op | source)
XLA Modules:
  0.0 50.1 jit_solution(12593784567215998346)
XLA Ops:
  0.6 2.0 %shard_map.59 = (f32[16,24,128]{2,1,0:T(8,128)S(1)}, f32[16,24,128]{2,1,0:T(8,128)S(1)}, bf16[16,128,128]{2,1,0:T(8,128)(2,1)S(1)}, f32[16,128]{1,0:T(8,128)S(1)...) custom-call(s32[3,16,42]{2,1,0:T(8,128)} %bitcast.8, f32[384,128]{1,0:T(8,128)} %bitcast.6, f32[384,128]{1,0:T(8,128)} %bitcast.7), custom_call_target="tpu_custom_call" | custom-call | tf_op jit(solution)/shard_map/pallas_call | solution.py:602
  2.7 0.5 %collective-permute-start = (f32[32,128]{1,0:T(8,128)S(1)}, f32[32,128]{1,0:T(8,128)S(1)}, u32[]{:S(2)}, u32[]{:S(2)}) collective-permute-start(f32[32,128]{1,0:T(8,128)S(1)} %get-tuple-element.37), channel_id=1, source_target_pairs={{0,1},{1,2},{2,3},{3,4},{4,5},{5,6},{6,7},{7,0},{8,9},{9,10},{10,1... | collective-permute-start | bytes 49160 | tf_op jit(solution)/shard_map/ppermute | solution.py:640
  3.2 4.1 %collective-permute-start.1 = (f32[32,128]{1,0:T(8,128)S(1)}, f32[32,128]{1,0:T(8,128)S(1)}, u32[]{:S(2)}, u32[]{:S(2)}) collective-permute-start(f32[32,128]{1,0:T(8,128)S(1)} %get-tuple-element.38), channel_id=1, source_target_pairs={{0,7},{1,0},{2,1},{3,2},{4,3},{5,4},{6,5},{7,6},{8,15},{9,8},{10,9... | collective-permute-start | bytes 49160 | tf_op jit(solution)/shard_map/ppermute | solution.py:641
  7.3 1.2 %shard_map.60 = (f32[1024,128]{1,0:T(8,128)S(1)}, bf16[64,128,64]{2,1,0:T(8,128)(2,1)S(1)}, bf16[64,32,128]{2,1,0:T(8,128)(2,1)S(1)}, bf16[64,32,128]{2,1,0:T(8,...) custom-call(f32[16,24,128]{2,1,0:T(8,128)S(1)} %get-tuple-element.34.x_ref.refs_0_, ...), custom_call_target="tpu_custom_call" | custom-call | tf_op jit(solution)/shard_map/pallas_call | solution.py:602
  8.5 7.7 %shard_map.61.refs_5_ = f32[896,128]{1,0:T(8,128)S(1)} custom-call(f32[16,128]{1,0:T(8,128)S(1)} %get-tuple-element.36.q_ref.refs_2_.refs_5_.refs_4_, f32[1024,128]{1,0:T(8,128)S(1)} %get-tuple-element.39.refs_0_.refs_6_, bf16[64,128,64]{2,1,0:T(8,128)(2,1)S(1)} %get-tuple-element.40.refs_1_.refs_7_, ...), custom_call_target="tpu_custom_call" | custom-call | tf_op jit(solution)/shard_map/pallas_call | solution.py:602
  16.1 0.0 collective-permute-done.refs_3_
  16.1 0.0 collective-permute-done.1.refs_4_
  16.1 0.0 copy-start
  16.2 1.9 %shard_map.62 = (f32[192,128]{1,0:T(8,128)S(1)}, f32[192,128]{1,0:T(8,128)S(1)}, f32[192,128]{1,0:T(8,128)S(1)}, f32[192,128]{1,0:T(8,128)S(1)}) custom-call(s32[1]{0:T(128)} %bitcast.b_ref, f32[16,24,128]{2,1,0:T(8,128)S(1)} %get-tuple-element.34.x_ref.refs_0_, f32[16,24,128]{2,1,0:T(8,128)S(1)} %get-tuple-element.35.refs_1_, ...), custom_call_target="tpu_custom_call" | custom-call | tf_op jit(solution)/shard_map/pallas_call | solution.py:602
  18.0 3.0 %collective-permute-start.2 = (f32[192,128]{1,0:T(8,128)S(1)}, f32[192,128]{1,0:T(8,128)S(1)}, u32[]{:S(2)}, u32[]{:S(2)}) collective-permute-start(f32[192,128]{1,0:T(8,128)S(1)} %get-tuple-element.46), channel_id=1, source_target_pairs={{0,24},{8,16},{16,8},{24,0},{1,25},{9,17},{17,9},{25,1},{2,26},{10... | collective-permute-start | bytes 294920 | tf_op jit(solution)/shard_map/ppermute | solution.py:614
  21.0 0.5 %collective-permute-start.3 = (f32[192,128]{1,0:T(8,128)S(1)}, f32[192,128]{1,0:T(8,128)S(1)}, u32[]{:S(2)}, u32[]{:S(2)}) collective-permute-start(f32[192,128]{1,0:T(8,128)S(1)} %get-tuple-element.47), channel_id=1, source_target_pairs={{0,8},{8,0},{16,24},{24,16},{1,9},{9,1},{17,25},{25,17},{2,10},{10... | collective-permute-start | bytes 294920 | tf_op jit(solution)/shard_map/ppermute | solution.py:614
  21.5 0.1 collective-permute-start.4
  21.6 2.1 %collective-permute-done.2.refs_1_ = f32[192,128]{1,0:T(8,128)S(1)} collective-permute-done((f32[192,128]{1,0:T(8,128)S(1)}, f32[192,128]{1,0:T(8,128)S(1)}, u32[]{:S(2)}, u32[]{:S(2)}) %collective-permute-start.2) | collective-permute-done | bytes 98336 | tf_op jit(solution)/shard_map/ppermute | solution.py:614
  23.7 1.9 %collective-permute-done.3.refs_2_ = f32[192,128]{1,0:T(8,128)S(1)} collective-permute-done((f32[192,128]{1,0:T(8,128)S(1)}, f32[192,128]{1,0:T(8,128)S(1)}, u32[]{:S(2)}, u32[]{:S(2)}) %collective-permute-start.3) | collective-permute-done | bytes 98336 | tf_op jit(solution)/shard_map/ppermute | solution.py:614
  25.6 0.5 %collective-permute-done.4.refs_3_ = f32[192,128]{1,0:T(8,128)S(1)} collective-permute-done((f32[192,128]{1,0:T(8,128)S(1)}, f32[192,128]{1,0:T(8,128)S(1)}, u32[]{:S(2)}, u32[]{:S(2)}) %collective-permute-start.4) | collective-permute-done | bytes 98336 | tf_op jit(solution)/shard_map/ppermute | solution.py:614
  26.1 0.0 copy-done
  26.1 1.6 %shard_map.63 = (f32[192,128]{1,0:T(8,128)S(1)}, f32[192,128]{1,0:T(8,128)S(1)}, f32[192,128]{1,0:T(8,128)S(1)}, f32[192,128]{1,0:T(8,128)S(1)}) custom-call(s32[1]{0:T(128)} %bitcast.b_ref, f32[192,128]{1,0:T(8,128)S(1)} %get-tuple-element.45.refs_0_, f32[192,128]{1,0:T(8,128)S(1)} %collective-permute-done.2.refs_1_, ...), custom_call_target="tpu_custom_call" | custom-call | tf_op jit(solution)/shard_map/pallas_call | solution.py:602
  27.7 1.5 %collective-permute-start.5 = (f32[192,128]{1,0:T(8,128)S(1)}, f32[192,128]{1,0:T(8,128)S(1)}, u32[]{:S(2)}, u32[]{:S(2)}) collective-permute-start(f32[192,128]{1,0:T(8,128)S(1)} %get-tuple-element.50), channel_id=1, source_target_pairs={{0,24},{8,16},{16,8},{24,0},{1,25},{9,17},{17,9},{25,1},{2,26},{10... | collective-permute-start | bytes 294920 | tf_op jit(solution)/shard_map/ppermute | solution.py:614
  29.2 0.5 %collective-permute-start.6 = (f32[192,128]{1,0:T(8,128)S(1)}, f32[192,128]{1,0:T(8,128)S(1)}, u32[]{:S(2)}, u32[]{:S(2)}) collective-permute-start(f32[192,128]{1,0:T(8,128)S(1)} %get-tuple-element.51), channel_id=1, source_target_pairs={{0,8},{8,0},{16,24},{24,16},{1,9},{9,1},{17,25},{25,17},{2,10},{10... | collective-permute-start | bytes 294920 | tf_op jit(solution)/shard_map/ppermute | solution.py:614
  29.7 1.5 %collective-permute-start.7 = (f32[192,128]{1,0:T(8,128)S(1)}, f32[192,128]{1,0:T(8,128)S(1)}, u32[]{:S(2)}, u32[]{:S(2)}) collective-permute-start(f32[192,128]{1,0:T(8,128)S(1)} %get-tuple-element.52), channel_id=1, source_target_pairs={{0,16},{8,24},{16,0},{24,8},{1,17},{9,25},{17,1},{25,9},{2,18},{10... | collective-permute-start | bytes 294920 | tf_op jit(solution)/shard_map/ppermute | solution.py:614
  31.3 2.0 %collective-permute-done.5.refs_1_ = f32[192,128]{1,0:T(8,128)S(1)} collective-permute-done((f32[192,128]{1,0:T(8,128)S(1)}, f32[192,128]{1,0:T(8,128)S(1)}, u32[]{:S(2)}, u32[]{:S(2)}) %collective-permute-start.5) | collective-permute-done | bytes 98336 | tf_op jit(solution)/shard_map/ppermute | solution.py:614
  33.3 0.5 %collective-permute-done.6.refs_2_ = f32[192,128]{1,0:T(8,128)S(1)} collective-permute-done((f32[192,128]{1,0:T(8,128)S(1)}, f32[192,128]{1,0:T(8,128)S(1)}, u32[]{:S(2)}, u32[]{:S(2)}) %collective-permute-start.6) | collective-permute-done | bytes 98336 | tf_op jit(solution)/shard_map/ppermute | solution.py:614
  33.8 0.5 %collective-permute-done.7.refs_3_ = f32[192,128]{1,0:T(8,128)S(1)} collective-permute-done((f32[192,128]{1,0:T(8,128)S(1)}, f32[192,128]{1,0:T(8,128)S(1)}, u32[]{:S(2)}, u32[]{:S(2)}) %collective-permute-start.7) | collective-permute-done | bytes 98336 | tf_op jit(solution)/shard_map/ppermute | solution.py:614
  34.4 0.1 collective-permute-start.8
  34.4 3.5 %collective-permute-start.9 = (f32[32,128]{1,0:T(8,128)S(1)}, f32[32,128]{1,0:T(8,128)S(1)}, u32[]{:S(2)}, u32[]{:S(2)}) collective-permute-start(f32[32,128]{1,0:T(8,128)S(1)} %get-tuple-element.56), channel_id=1, source_target_pairs={{0,7},{1,0},{2,1},{3,2},{4,3},{5,4},{6,5},{7,6},{8,15},{9,8},{10,9... | collective-permute-start | bytes 49160 | tf_op jit(solution)/shard_map/ppermute | solution.py:641
  38.0 1.2 %shard_map.65 = (f32[1024,128]{1,0:T(8,128)S(1)}, bf16[64,128,64]{2,1,0:T(8,128)(2,1)S(1)}, bf16[64,32,128]{2,1,0:T(8,128)(2,1)S(1)}, bf16[64,32,128]{2,1,0:T(8,...) custom-call(f32[16,24,128]{2,1,0:T(8,128)S(1)} %get-tuple-element.53.x_ref.refs_0_, ...), custom_call_target="tpu_custom_call" | custom-call | tf_op jit(solution)/shard_map/pallas_call | solution.py:602
  39.2 7.6 %shard_map.66.refs_5_ = f32[896,128]{1,0:T(8,128)S(1)} custom-call(f32[16,128]{1,0:T(8,128)S(1)} %get-tuple-element.36.q_ref.refs_2_.refs_5_.refs_4_, f32[1024,128]{1,0:T(8,128)S(1)} %get-tuple-element.57.refs_0_.refs_7_, bf16[64,128,64]{2,1,0:T(8,128)(2,1)S(1)} %get-tuple-element.58.refs_1_.refs_8_, ...), custom_call_target="tpu_custom_call" | custom-call | tf_op jit(solution)/shard_map/pallas_call | solution.py:602
  46.8 0.0 collective-permute-done.8.refs_3_
  46.8 0.0 collective-permute-done.9.refs_4_
  46.8 3.2 %shard_map.67 = (f32[384,128]{1,0:T(8,128)}, f32[384,128]{1,0:T(8,128)}) custom-call(f32[16,24,128]{2,1,0:T(8,128)S(1)} %get-tuple-element.53.x_ref.refs_0_, f32[16,24,128]{2,1,0:T(8,128)S(1)} %get-tuple-element.54.refs_1_, f32[16,128]{1,0:T(8,128)S(1)} %get-tuple-element.36.q_ref.refs_2_.refs_5_.refs_4_, f32[32,128]{1,0:T(8,128)S(1)} %collective-permute-done.8.refs_3_, ...), custom_call_target="tpu_custom_call" | custom-call | tf_op jit(solution)/shard_map/pallas_call | solution.py:602
  (1 shorter events, 0.0 us)
Async XLA Ops:
  2.7 13.5 %collective-permute-start = (f32[32,128]{1,0:T(8,128)S(1)}, f32[32,128]{1,0:T(8,128)S(1)}, u32[]{:S(2)}, u32[]{:S(2)}) collective-permute-start(f32[32,128]{1,0:T(8,128)S(1)} %get-tuple-element.37), channel_id=1, source_target_pairs={{0,1},{1,2},{2,3},{3,4},{4,5},{5,6},{6,7},{7,0},{8,9},{9,10},{10,1... | collective-permute-start | bytes 49160 | tf_op jit(solution)/shard_map/ppermute | solution.py:640
  3.2 13.0 %collective-permute-start.1 = (f32[32,128]{1,0:T(8,128)S(1)}, f32[32,128]{1,0:T(8,128)S(1)}, u32[]{:S(2)}, u32[]{:S(2)}) collective-permute-start(f32[32,128]{1,0:T(8,128)S(1)} %get-tuple-element.38), channel_id=1, source_target_pairs={{0,7},{1,0},{2,1},{3,2},{4,3},{5,4},{6,5},{7,6},{8,15},{9,8},{10,9... | collective-permute-start | bytes 49160 | tf_op jit(solution)/shard_map/ppermute | solution.py:641
  16.1 10.0 %copy-start = (bf16[4,64,384]{2,1,0:T(8,128)(2,1)S(1)}, bf16[4,64,384]{2,1,0:T(8,128)(2,1)}, u32[]{:S(2)}) copy-start(bf16[4,64,384]{2,1,0:T(8,128)(2,1)} %constant.7.clone.refs_4_) | copy-start | bytes 589828
  18.0 5.7 %collective-permute-start.2 = (f32[192,128]{1,0:T(8,128)S(1)}, f32[192,128]{1,0:T(8,128)S(1)}, u32[]{:S(2)}, u32[]{:S(2)}) collective-permute-start(f32[192,128]{1,0:T(8,128)S(1)} %get-tuple-element.46), channel_id=1, source_target_pairs={{0,24},{8,16},{16,8},{24,0},{1,25},{9,17},{17,9},{25,1},{2,26},{10... | collective-permute-start | bytes 294920 | tf_op jit(solution)/shard_map/ppermute | solution.py:614
  21.0 4.6 %collective-permute-start.3 = (f32[192,128]{1,0:T(8,128)S(1)}, f32[192,128]{1,0:T(8,128)S(1)}, u32[]{:S(2)}, u32[]{:S(2)}) collective-permute-start(f32[192,128]{1,0:T(8,128)S(1)} %get-tuple-element.47), channel_id=1, source_target_pairs={{0,8},{8,0},{16,24},{24,16},{1,9},{9,1},{17,25},{25,17},{2,10},{10... | collective-permute-start | bytes 294920 | tf_op jit(solution)/shard_map/ppermute | solution.py:614
  21.5 4.6 %collective-permute-start.4 = (f32[192,128]{1,0:T(8,128)S(1)}, f32[192,128]{1,0:T(8,128)S(1)}, u32[]{:S(2)}, u32[]{:S(2)}) collective-permute-start(f32[192,128]{1,0:T(8,128)S(1)} %get-tuple-element.48), channel_id=1, source_target_pairs={{0,16},{8,24},{16,0},{24,8},{1,17},{9,25},{17,1},{25,9},{2,18},{10... | collective-permute-start | bytes 294920 | tf_op jit(solution)/shard_map/ppermute | solution.py:614
  27.7 5.6 %collective-permute-start.5 = (f32[192,128]{1,0:T(8,128)S(1)}, f32[192,128]{1,0:T(8,128)S(1)}, u32[]{:S(2)}, u32[]{:S(2)}) collective-permute-start(f32[192,128]{1,0:T(8,128)S(1)} %get-tuple-element.50), channel_id=1, source_target_pairs={{0,24},{8,16},{16,8},{24,0},{1,25},{9,17},{17,9},{25,1},{2,26},{10... | collective-permute-start | bytes 294920 | tf_op jit(solution)/shard_map/ppermute | solution.py:614
  29.2 4.6 %collective-permute-start.6 = (f32[192,128]{1,0:T(8,128)S(1)}, f32[192,128]{1,0:T(8,128)S(1)}, u32[]{:S(2)}, u32[]{:S(2)}) collective-permute-start(f32[192,128]{1,0:T(8,128)S(1)} %get-tuple-element.51), channel_id=1, source_target_pairs={{0,8},{8,0},{16,24},{24,16},{1,9},{9,1},{17,25},{25,17},{2,10},{10... | collective-permute-start | bytes 294920 | tf_op jit(solution)/shard_map/ppermute | solution.py:614
  29.7 4.6 %collective-permute-start.7 = (f32[192,128]{1,0:T(8,128)S(1)}, f32[192,128]{1,0:T(8,128)S(1)}, u32[]{:S(2)}, u32[]{:S(2)}) collective-permute-start(f32[192,128]{1,0:T(8,128)S(1)} %get-tuple-element.52), channel_id=1, source_target_pairs={{0,16},{8,24},{16,0},{24,8},{1,17},{9,25},{17,1},{25,9},{2,18},{10... | collective-permute-start | bytes 294920 | tf_op jit(solution)/shard_map/ppermute | solution.py:614
  34.4 12.4 %collective-permute-start.8 = (f32[32,128]{1,0:T(8,128)S(1)}, f32[32,128]{1,0:T(8,128)S(1)}, u32[]{:S(2)}, u32[]{:S(2)}) collective-permute-start(f32[32,128]{1,0:T(8,128)S(1)} %get-tuple-element.55), channel_id=1, source_target_pairs={{0,1},{1,2},{2,3},{3,4},{4,5},{5,6},{6,7},{7,0},{8,9},{9,10},{10,1... | collective-permute-start | bytes 49160 | tf_op jit(solution)/shard_map/ppermute | solution.py:640
  34.4 12.4 %collective-permute-start.9 = (f32[32,128]{1,0:T(8,128)S(1)}, f32[32,128]{1,0:T(8,128)S(1)}, u32[]{:S(2)}, u32[]{:S(2)}) collective-permute-start(f32[32,128]{1,0:T(8,128)S(1)} %get-tuple-element.56), channel_id=1, source_target_pairs={{0,7},{1,0},{2,1},{3,2},{4,3},{5,4},{6,5},{7,6},{8,15},{9,8},{10,9... | collective-permute-start | bytes 49160 | tf_op jit(solution)/shard_map/ppermute | solution.py:641

commit v5 on v4

--- a/solution.py
+++ b/solution.py
@@ -54,7 +54,7 @@
 
 
 def block_order(nb):
-    return sorted(range(nb), key=lambda k: (k > 0, -bin(k).count("1"), k))
+    return list(range(nb))
 
 
 def propagator(beads, beads_dev):
@@ -233,7 +233,7 @@
     ones_last = jnp.where(row8 == 7, 1.0, 0.0)
     pairs = beads // 2
     total = count * pairs
-    unroll = max(n for n in range(1, max(2, min(17, total // 4 + 1))) if total % n == 0)
+    unroll = max(n for n in range(1, min(16, max(total // 4, 4)) + 1) if total % n == 0)
 
     def stack(values):
         return jnp.concatenate(values, axis=0).astype(BF16)

time: 50.2 us -> 50.5 us (level)
  waiting for transfers between devices: 7.59 us -> 8.2 us
    ppermute x6, waiting for transfers between devices: 7.58 us -> 8.19 us  [exchange(): lax.ppermute(block, 'bead', [(i, i ^ k) for i in range(nb)])]
where the time goes in v5:
time: 50.5 us; the launch traced here: 50.4 us
  Pallas kernels  26.1 us (52%)
  starting transfers between devices  15.3 us (30%)
  waiting for transfers between devices  8.2 us (16%)
  between operations  0.74 us (1%)
    pallas_call x9, Pallas kernels, call(): pl.pallas_call(kernel, out_shape=outs, in_specs=([] if scalar is None els...  26.1 us
    ppermute x6, waiting for transfers between devices, exchange(): lax.ppermute(block, 'bead', [(i, i ^ k) for i in range(nb)])  8.19 us
    ppermute x2, starting transfers between devices, halos(): lax.ppermute(to_left, 'space', [(s, (s - 1) % ns) for s in range(ns)])  7.63 us
    ppermute x6, starting transfers between devices, exchange(): lax.ppermute(block, 'bead', [(i, i ^ k) for i in range(nb)])  7.11 us
  transfers between devices with their start and end apart: 10, of which 6 were waited for; matrix products, arithmetic and copies ran while one was open for 0% of the time, Pallas kernels for 35%

profile of v5, /device:TPU:0, one launch (start us, length us, event | category | flops | bytes accessed | tf_op | source)
XLA Modules:
  0.0 50.4 jit_solution(9579233630438851772)
XLA Ops:
  0.6 2.0 %shard_map.59 = (f32[16,24,128]{2,1,0:T(8,128)S(1)}, f32[16,24,128]{2,1,0:T(8,128)S(1)}, bf16[16,128,128]{2,1,0:T(8,128)(2,1)S(1)}, f32[16,128]{1,0:T(8,128)S(1)...) custom-call(s32[3,16,42]{2,1,0:T(8,128)} %bitcast.8, f32[384,128]{1,0:T(8,128)} %bitcast.6, f32[384,128]{1,0:T(8,128)} %bitcast.7), custom_call_target="tpu_custom_call" | custom-call | tf_op jit(solution)/shard_map/pallas_call | solution.py:602
  2.7 0.5 %collective-permute-start = (f32[32,128]{1,0:T(8,128)S(1)}, f32[32,128]{1,0:T(8,128)S(1)}, u32[]{:S(2)}, u32[]{:S(2)}) collective-permute-start(f32[32,128]{1,0:T(8,128)S(1)} %get-tuple-element.37), channel_id=1, source_target_pairs={{0,1},{1,2},{2,3},{3,4},{4,5},{5,6},{6,7},{7,0},{8,9},{9,10},{10,1... | collective-permute-start | bytes 49160 | tf_op jit(solution)/shard_map/ppermute | solution.py:640
  3.2 4.1 %collective-permute-start.1 = (f32[32,128]{1,0:T(8,128)S(1)}, f32[32,128]{1,0:T(8,128)S(1)}, u32[]{:S(2)}, u32[]{:S(2)}) collective-permute-start(f32[32,128]{1,0:T(8,128)S(1)} %get-tuple-element.38), channel_id=1, source_target_pairs={{0,7},{1,0},{2,1},{3,2},{4,3},{5,4},{6,5},{7,6},{8,15},{9,8},{10,9... | collective-permute-start | bytes 49160 | tf_op jit(solution)/shard_map/ppermute | solution.py:641
  7.3 1.2 %shard_map.60 = (f32[1024,128]{1,0:T(8,128)S(1)}, bf16[64,128,64]{2,1,0:T(8,128)(2,1)S(1)}, bf16[64,32,128]{2,1,0:T(8,128)(2,1)S(1)}, bf16[64,32,128]{2,1,0:T(8,...) custom-call(f32[16,24,128]{2,1,0:T(8,128)S(1)} %get-tuple-element.34.x_ref.refs_0_, ...), custom_call_target="tpu_custom_call" | custom-call | tf_op jit(solution)/shard_map/pallas_call | solution.py:602
  8.5 7.7 %shard_map.61.refs_5_ = f32[896,128]{1,0:T(8,128)S(1)} custom-call(f32[16,128]{1,0:T(8,128)S(1)} %get-tuple-element.36.q_ref.refs_2_.refs_5_.refs_4_, f32[1024,128]{1,0:T(8,128)S(1)} %get-tuple-element.39.refs_0_.refs_6_, bf16[64,128,64]{2,1,0:T(8,128)(2,1)S(1)} %get-tuple-element.40.refs_1_.refs_7_, ...), custom_call_target="tpu_custom_call" | custom-call | tf_op jit(solution)/shard_map/pallas_call | solution.py:602
  16.1 0.0 collective-permute-done.refs_3_
  16.1 0.0 collective-permute-done.1.refs_4_
  16.1 0.0 copy-start
  16.2 1.7 %shard_map.62 = (f32[192,128]{1,0:T(8,128)S(1)}, f32[192,128]{1,0:T(8,128)S(1)}, f32[192,128]{1,0:T(8,128)S(1)}, f32[192,128]{1,0:T(8,128)S(1)}) custom-call(s32[1]{0:T(128)} %bitcast.b_ref, f32[16,24,128]{2,1,0:T(8,128)S(1)} %get-tuple-element.34.x_ref.refs_0_, f32[16,24,128]{2,1,0:T(8,128)S(1)} %get-tuple-element.35.refs_1_, ...), custom_call_target="tpu_custom_call" | custom-call | tf_op jit(solution)/shard_map/pallas_call | solution.py:602
  17.9 2.0 %collective-permute-start.2 = (f32[192,128]{1,0:T(8,128)S(1)}, f32[192,128]{1,0:T(8,128)S(1)}, u32[]{:S(2)}, u32[]{:S(2)}) collective-permute-start(f32[192,128]{1,0:T(8,128)S(1)} %get-tuple-element.46), channel_id=1, source_target_pairs={{0,8},{8,0},{16,24},{24,16},{1,9},{9,1},{17,25},{25,17},{2,10},{10... | collective-permute-start | bytes 294920 | tf_op jit(solution)/shard_map/ppermute | solution.py:614
  19.9 1.5 %collective-permute-start.3 = (f32[192,128]{1,0:T(8,128)S(1)}, f32[192,128]{1,0:T(8,128)S(1)}, u32[]{:S(2)}, u32[]{:S(2)}) collective-permute-start(f32[192,128]{1,0:T(8,128)S(1)} %get-tuple-element.47), channel_id=1, source_target_pairs={{0,16},{8,24},{16,0},{24,8},{1,17},{9,25},{17,1},{25,9},{2,18},{10... | collective-permute-start | bytes 294920 | tf_op jit(solution)/shard_map/ppermute | solution.py:614
  21.4 0.0 collective-permute-start.4
  21.5 2.2 %collective-permute-done.2.refs_1_ = f32[192,128]{1,0:T(8,128)S(1)} collective-permute-done((f32[192,128]{1,0:T(8,128)S(1)}, f32[192,128]{1,0:T(8,128)S(1)}, u32[]{:S(2)}, u32[]{:S(2)}) %collective-permute-start.2) | collective-permute-done | bytes 98336 | tf_op jit(solution)/shard_map/ppermute | solution.py:614
  23.6 1.3 %collective-permute-done.3.refs_2_ = f32[192,128]{1,0:T(8,128)S(1)} collective-permute-done((f32[192,128]{1,0:T(8,128)S(1)}, f32[192,128]{1,0:T(8,128)S(1)}, u32[]{:S(2)}, u32[]{:S(2)}) %collective-permute-start.3) | collective-permute-done | bytes 98336 | tf_op jit(solution)/shard_map/ppermute | solution.py:614
  24.9 2.0 %collective-permute-done.4.refs_3_ = f32[192,128]{1,0:T(8,128)S(1)} collective-permute-done((f32[192,128]{1,0:T(8,128)S(1)}, f32[192,128]{1,0:T(8,128)S(1)}, u32[]{:S(2)}, u32[]{:S(2)}) %collective-permute-start.4) | collective-permute-done | bytes 98336 | tf_op jit(solution)/shard_map/ppermute | solution.py:614
  26.9 0.0 copy-done
  26.9 1.6 %shard_map.63 = (f32[192,128]{1,0:T(8,128)S(1)}, f32[192,128]{1,0:T(8,128)S(1)}, f32[192,128]{1,0:T(8,128)S(1)}, f32[192,128]{1,0:T(8,128)S(1)}) custom-call(s32[1]{0:T(128)} %bitcast.b_ref, f32[192,128]{1,0:T(8,128)S(1)} %get-tuple-element.45.refs_0_, f32[192,128]{1,0:T(8,128)S(1)} %collective-permute-done.2.refs_1_, ...), custom_call_target="tpu_custom_call" | custom-call | tf_op jit(solution)/shard_map/pallas_call | solution.py:602
  28.5 0.6 %collective-permute-start.5 = (f32[192,128]{1,0:T(8,128)S(1)}, f32[192,128]{1,0:T(8,128)S(1)}, u32[]{:S(2)}, u32[]{:S(2)}) collective-permute-start(f32[192,128]{1,0:T(8,128)S(1)} %get-tuple-element.50), channel_id=1, source_target_pairs={{0,8},{8,0},{16,24},{24,16},{1,9},{9,1},{17,25},{25,17},{2,10},{10... | collective-permute-start | bytes 294920 | tf_op jit(solution)/shard_map/ppermute | solution.py:614
  29.1 0.2 collective-permute-start.6
  29.3 2.8 %collective-permute-start.7 = (f32[192,128]{1,0:T(8,128)S(1)}, f32[192,128]{1,0:T(8,128)S(1)}, u32[]{:S(2)}, u32[]{:S(2)}) collective-permute-start(f32[192,128]{1,0:T(8,128)S(1)} %get-tuple-element.52), channel_id=1, source_target_pairs={{0,24},{8,16},{16,8},{24,0},{1,25},{9,17},{17,9},{25,1},{2,26},{10... | collective-permute-start | bytes 294920 | tf_op jit(solution)/shard_map/ppermute | solution.py:614
  32.1 1.1 %collective-permute-done.5.refs_1_ = f32[192,128]{1,0:T(8,128)S(1)} collective-permute-done((f32[192,128]{1,0:T(8,128)S(1)}, f32[192,128]{1,0:T(8,128)S(1)}, u32[]{:S(2)}, u32[]{:S(2)}) %collective-permute-start.5) | collective-permute-done | bytes 98336 | tf_op jit(solution)/shard_map/ppermute | solution.py:614
  33.2 0.5 %collective-permute-done.6.refs_2_ = f32[192,128]{1,0:T(8,128)S(1)} collective-permute-done((f32[192,128]{1,0:T(8,128)S(1)}, f32[192,128]{1,0:T(8,128)S(1)}, u32[]{:S(2)}, u32[]{:S(2)}) %collective-permute-start.6) | collective-permute-done | bytes 98336 | tf_op jit(solution)/shard_map/ppermute | solution.py:614
  33.7 1.1 %collective-permute-done.7.refs_3_ = f32[192,128]{1,0:T(8,128)S(1)} collective-permute-done((f32[192,128]{1,0:T(8,128)S(1)}, f32[192,128]{1,0:T(8,128)S(1)}, u32[]{:S(2)}, u32[]{:S(2)}) %collective-permute-start.7) | collective-permute-done | bytes 98336 | tf_op jit(solution)/shard_map/ppermute | solution.py:614
  34.8 0.1 collective-permute-start.8
  34.9 3.5 %collective-permute-start.9 = (f32[32,128]{1,0:T(8,128)S(1)}, f32[32,128]{1,0:T(8,128)S(1)}, u32[]{:S(2)}, u32[]{:S(2)}) collective-permute-start(f32[32,128]{1,0:T(8,128)S(1)} %get-tuple-element.56), channel_id=1, source_target_pairs={{0,7},{1,0},{2,1},{3,2},{4,3},{5,4},{6,5},{7,6},{8,15},{9,8},{10,9... | collective-permute-start | bytes 49160 | tf_op jit(solution)/shard_map/ppermute | solution.py:641
  38.4 1.2 %shard_map.65 = (f32[1024,128]{1,0:T(8,128)S(1)}, bf16[64,128,64]{2,1,0:T(8,128)(2,1)S(1)}, bf16[64,32,128]{2,1,0:T(8,128)(2,1)S(1)}, bf16[64,32,128]{2,1,0:T(8,...) custom-call(f32[16,24,128]{2,1,0:T(8,128)S(1)} %get-tuple-element.53.x_ref.refs_0_, ...), custom_call_target="tpu_custom_call" | custom-call | tf_op jit(solution)/shard_map/pallas_call | solution.py:602
  39.6 7.6 %shard_map.66.refs_5_ = f32[896,128]{1,0:T(8,128)S(1)} custom-call(f32[16,128]{1,0:T(8,128)S(1)} %get-tuple-element.36.q_ref.refs_2_.refs_5_.refs_4_, f32[1024,128]{1,0:T(8,128)S(1)} %get-tuple-element.57.refs_0_.refs_7_, bf16[64,128,64]{2,1,0:T(8,128)(2,1)S(1)} %get-tuple-element.58.refs_1_.refs_8_, ...), custom_call_target="tpu_custom_call" | custom-call | tf_op jit(solution)/shard_map/pallas_call | solution.py:602
  47.2 0.0 collective-permute-done.8.refs_3_
  47.3 0.0 collective-permute-done.9.refs_4_
  47.3 3.1 %shard_map.67 = (f32[384,128]{1,0:T(8,128)}, f32[384,128]{1,0:T(8,128)}) custom-call(f32[16,24,128]{2,1,0:T(8,128)S(1)} %get-tuple-element.53.x_ref.refs_0_, f32[16,24,128]{2,1,0:T(8,128)S(1)} %get-tuple-element.54.refs_1_, f32[16,128]{1,0:T(8,128)S(1)} %get-tuple-element.36.q_ref.refs_2_.refs_5_.refs_4_, f32[32,128]{1,0:T(8,128)S(1)} %collective-permute-done.8.refs_3_, ...), custom_call_target="tpu_custom_call" | custom-call | tf_op jit(solution)/shard_map/pallas_call | solution.py:602
  (1 shorter events, 0.0 us)
Async XLA Ops:
  2.7 13.5 %collective-permute-start = (f32[32,128]{1,0:T(8,128)S(1)}, f32[32,128]{1,0:T(8,128)S(1)}, u32[]{:S(2)}, u32[]{:S(2)}) collective-permute-start(f32[32,128]{1,0:T(8,128)S(1)} %get-tuple-element.37), channel_id=1, source_target_pairs={{0,1},{1,2},{2,3},{3,4},{4,5},{5,6},{6,7},{7,0},{8,9},{9,10},{10,1... | collective-permute-start | bytes 49160 | tf_op jit(solution)/shard_map/ppermute | solution.py:640
  3.2 13.0 %collective-permute-start.1 = (f32[32,128]{1,0:T(8,128)S(1)}, f32[32,128]{1,0:T(8,128)S(1)}, u32[]{:S(2)}, u32[]{:S(2)}) collective-permute-start(f32[32,128]{1,0:T(8,128)S(1)} %get-tuple-element.38), channel_id=1, source_target_pairs={{0,7},{1,0},{2,1},{3,2},{4,3},{5,4},{6,5},{7,6},{8,15},{9,8},{10,9... | collective-permute-start | bytes 49160 | tf_op jit(solution)/shard_map/ppermute | solution.py:641
  16.1 10.8 %copy-start = (bf16[4,64,384]{2,1,0:T(8,128)(2,1)S(1)}, bf16[4,64,384]{2,1,0:T(8,128)(2,1)}, u32[]{:S(2)}) copy-start(bf16[4,64,384]{2,1,0:T(8,128)(2,1)} %constant.7.clone.refs_4_) | copy-start | bytes 589828
  17.9 5.7 %collective-permute-start.2 = (f32[192,128]{1,0:T(8,128)S(1)}, f32[192,128]{1,0:T(8,128)S(1)}, u32[]{:S(2)}, u32[]{:S(2)}) collective-permute-start(f32[192,128]{1,0:T(8,128)S(1)} %get-tuple-element.46), channel_id=1, source_target_pairs={{0,8},{8,0},{16,24},{24,16},{1,9},{9,1},{17,25},{25,17},{2,10},{10... | collective-permute-start | bytes 294920 | tf_op jit(solution)/shard_map/ppermute | solution.py:614
  19.9 5.0 %collective-permute-start.3 = (f32[192,128]{1,0:T(8,128)S(1)}, f32[192,128]{1,0:T(8,128)S(1)}, u32[]{:S(2)}, u32[]{:S(2)}) collective-permute-start(f32[192,128]{1,0:T(8,128)S(1)} %get-tuple-element.47), channel_id=1, source_target_pairs={{0,16},{8,24},{16,0},{24,8},{1,17},{9,25},{17,1},{25,9},{2,18},{10... | collective-permute-start | bytes 294920 | tf_op jit(solution)/shard_map/ppermute | solution.py:614
  21.4 5.5 %collective-permute-start.4 = (f32[192,128]{1,0:T(8,128)S(1)}, f32[192,128]{1,0:T(8,128)S(1)}, u32[]{:S(2)}, u32[]{:S(2)}) collective-permute-start(f32[192,128]{1,0:T(8,128)S(1)} %get-tuple-element.48), channel_id=1, source_target_pairs={{0,24},{8,16},{16,8},{24,0},{1,25},{9,17},{17,9},{25,1},{2,26},{10... | collective-permute-start | bytes 294920 | tf_op jit(solution)/shard_map/ppermute | solution.py:614
  28.5 4.7 %collective-permute-start.5 = (f32[192,128]{1,0:T(8,128)S(1)}, f32[192,128]{1,0:T(8,128)S(1)}, u32[]{:S(2)}, u32[]{:S(2)}) collective-permute-start(f32[192,128]{1,0:T(8,128)S(1)} %get-tuple-element.50), channel_id=1, source_target_pairs={{0,8},{8,0},{16,24},{24,16},{1,9},{9,1},{17,25},{25,17},{2,10},{10... | collective-permute-start | bytes 294920 | tf_op jit(solution)/shard_map/ppermute | solution.py:614
  29.1 4.6 %collective-permute-start.6 = (f32[192,128]{1,0:T(8,128)S(1)}, f32[192,128]{1,0:T(8,128)S(1)}, u32[]{:S(2)}, u32[]{:S(2)}) collective-permute-start(f32[192,128]{1,0:T(8,128)S(1)} %get-tuple-element.51), channel_id=1, source_target_pairs={{0,16},{8,24},{16,0},{24,8},{1,17},{9,25},{17,1},{25,9},{2,18},{10... | collective-permute-start | bytes 294920 | tf_op jit(solution)/shard_map/ppermute | solution.py:614
  29.3 5.5 %collective-permute-start.7 = (f32[192,128]{1,0:T(8,128)S(1)}, f32[192,128]{1,0:T(8,128)S(1)}, u32[]{:S(2)}, u32[]{:S(2)}) collective-permute-start(f32[192,128]{1,0:T(8,128)S(1)} %get-tuple-element.52), channel_id=1, source_target_pairs={{0,24},{8,16},{16,8},{24,0},{1,25},{9,17},{17,9},{25,1},{2,26},{10... | collective-permute-start | bytes 294920 | tf_op jit(solution)/shard_map/ppermute | solution.py:614
  34.8 12.4 %collective-permute-start.8 = (f32[32,128]{1,0:T(8,128)S(1)}, f32[32,128]{1,0:T(8,128)S(1)}, u32[]{:S(2)}, u32[]{:S(2)}) collective-permute-start(f32[32,128]{1,0:T(8,128)S(1)} %get-tuple-element.55), channel_id=1, source_target_pairs={{0,1},{1,2},{2,3},{3,4},{4,5},{5,6},{6,7},{7,0},{8,9},{9,10},{10,1... | collective-permute-start | bytes 49160 | tf_op jit(solution)/shard_map/ppermute | solution.py:640
  34.9 12.4 %collective-permute-start.9 = (f32[32,128]{1,0:T(8,128)S(1)}, f32[32,128]{1,0:T(8,128)S(1)}, u32[]{:S(2)}, u32[]{:S(2)}) collective-permute-start(f32[32,128]{1,0:T(8,128)S(1)} %get-tuple-element.56), channel_id=1, source_target_pairs={{0,7},{1,0},{2,1},{3,2},{4,3},{5,4},{6,5},{7,6},{8,15},{9,8},{10,9... | collective-permute-start | bytes 49160 | tf_op jit(solution)/shard_map/ppermute | solution.py:641

commit v6 on v5

--- a/solution.py
+++ b/solution.py
@@ -54,7 +54,7 @@
 
 
 def block_order(nb):
-    return list(range(nb))
+    return sorted(range(nb), key=lambda k: (k > 0, -bin(k).count("1"), k))
 
 
 def propagator(beads, beads_dev):
@@ -477,11 +477,11 @@
     blocks, q_ref = refs[:nb], refs[nb]
     xs, ps, to_right, to_left = refs[nb + 1 :]
     n = 3 * lb
-    for i, k in enumerate(block_order(nb)):
+    for k in range(nb):
         first = jnp.bitwise_xor(b_ref[0], k) * group
         for w in range(group):
-            xs[first + w] = blocks[i][pl.ds(w * n, n), :]
-            ps[first + w] = blocks[i][pl.ds((group + w) * n, n), :]
+            xs[first + w] = blocks[k][pl.ds(w * n, n), :]
+            ps[first + w] = blocks[k][pl.ds((group + w) * n, n), :]
     write_ends(to_right, to_left, xs, q_ref, lb, cells, slots)
 
 
@@ -591,9 +591,9 @@
             mass = jnp.where(q < -1.5, oxygen_mass, 1.0)
             for a, values in enumerate((pos, [v * mass for v in vel])):
                 for c in range(3):
-                    for i in range(nb):
+                    for i, k in enumerate(block_order(nb)):
                         rows = values[c][i * lb : (i + 1) * lb]
-                        outs[i][pl.ds((a * group + w) * n + c * lb, lb), :] = rows
+                        outs[k][pl.ds((a * group + w) * n + c * lb, lb), :] = rows
 
 
 def call(kernel, outs, scratch, scalar, *operands, space=pltpu.VMEM):
@@ -609,10 +609,10 @@
     )(*(() if scalar is None else (scalar,)), *operands)
 
 
-def exchange(blocks, nb):
+def exchange(blocks, order):
     return [
-        lax.ppermute(block, "bead", [(i, i ^ k) for i in range(nb)]) if k else block
-        for block, k in zip(blocks, block_order(nb))
+        lax.ppermute(block, "bead", [(i, i ^ k) for i in range(len(order))]) if k else block
+        for block, k in zip(blocks, order)
     ]
 
 
@@ -698,7 +698,7 @@
         blocks,
         [],
         b,
-        *exchange(sent, nb),
+        *exchange(sent, block_order(nb)),
         jnp.asarray(propagator(beads, lb)),
         charges,
     )
@@ -707,7 +707,7 @@
         state + ends,
         [],
         b,
-        *exchange(stepped, nb),
+        *exchange(stepped, range(nb)),
         charges,
     )
     left, right = halos(to_right, to_left)

time: 50.5 us -> 50.9 us (level)
  no operation moved by 1% of the time
where the time goes in v6:
time: 50.9 us; the launch traced here: 50.7 us
  Pallas kernels  26.1 us (51%)
  starting transfers between devices  15.3 us (30%)
  waiting for transfers between devices  8.55 us (17%)
  between operations  0.74 us (1%)
    pallas_call x9, Pallas kernels, call(): pl.pallas_call(kernel, out_shape=outs, in_specs=([] if scalar is None els...  26.1 us
    ppermute x6, waiting for transfers between devices, exchange(): lax.ppermute(block, 'bead', [(i, i ^ k) for i in range(len(order))])  8.54 us
    ppermute x2, starting transfers between devices, halos(): lax.ppermute(to_left, 'space', [(s, (s - 1) % ns) for s in range(ns)])  7.63 us
    ppermute x6, starting transfers between devices, exchange(): lax.ppermute(block, 'bead', [(i, i ^ k) for i in range(len(order))])  7.15 us
  transfers between devices with their start and end apart: 10, of which 6 were waited for; matrix products, arithmetic and copies ran while one was open for 0% of the time, Pallas kernels for 35%

profile of v6, /device:TPU:0, one launch (start us, length us, event | category | flops | bytes accessed | tf_op | source)
XLA Modules:
  0.0 50.7 jit_solution(9758220878297556405)
XLA Ops:
  0.6 2.0 %shard_map.59 = (f32[16,24,128]{2,1,0:T(8,128)S(1)}, f32[16,24,128]{2,1,0:T(8,128)S(1)}, bf16[16,128,128]{2,1,0:T(8,128)(2,1)S(1)}, f32[16,128]{1,0:T(8,128)S(1)...) custom-call(s32[3,16,42]{2,1,0:T(8,128)} %bitcast.8, f32[384,128]{1,0:T(8,128)} %bitcast.6, f32[384,128]{1,0:T(8,128)} %bitcast.7), custom_call_target="tpu_custom_call" | custom-call | tf_op jit(solution)/shard_map/pallas_call | solution.py:602
  2.7 0.5 %collective-permute-start = (f32[32,128]{1,0:T(8,128)S(1)}, f32[32,128]{1,0:T(8,128)S(1)}, u32[]{:S(2)}, u32[]{:S(2)}) collective-permute-start(f32[32,128]{1,0:T(8,128)S(1)} %get-tuple-element.37), channel_id=1, source_target_pairs={{0,1},{1,2},{2,3},{3,4},{4,5},{5,6},{6,7},{7,0},{8,9},{9,10},{10,1... | collective-permute-start | bytes 49160 | tf_op jit(solution)/shard_map/ppermute | solution.py:640
  3.2 4.1 %collective-permute-start.1 = (f32[32,128]{1,0:T(8,128)S(1)}, f32[32,128]{1,0:T(8,128)S(1)}, u32[]{:S(2)}, u32[]{:S(2)}) collective-permute-start(f32[32,128]{1,0:T(8,128)S(1)} %get-tuple-element.38), channel_id=1, source_target_pairs={{0,7},{1,0},{2,1},{3,2},{4,3},{5,4},{6,5},{7,6},{8,15},{9,8},{10,9... | collective-permute-start | bytes 49160 | tf_op jit(solution)/shard_map/ppermute | solution.py:641
  7.3 1.2 %shard_map.60 = (f32[1024,128]{1,0:T(8,128)S(1)}, bf16[64,128,64]{2,1,0:T(8,128)(2,1)S(1)}, bf16[64,32,128]{2,1,0:T(8,128)(2,1)S(1)}, bf16[64,32,128]{2,1,0:T(8,...) custom-call(f32[16,24,128]{2,1,0:T(8,128)S(1)} %get-tuple-element.34.x_ref.refs_0_, ...), custom_call_target="tpu_custom_call" | custom-call | tf_op jit(solution)/shard_map/pallas_call | solution.py:602
  8.5 7.7 %shard_map.61.refs_5_ = f32[896,128]{1,0:T(8,128)S(1)} custom-call(f32[16,128]{1,0:T(8,128)S(1)} %get-tuple-element.36.q_ref.refs_2_.refs_5_.refs_4_, f32[1024,128]{1,0:T(8,128)S(1)} %get-tuple-element.39.refs_0_.refs_6_, bf16[64,128,64]{2,1,0:T(8,128)(2,1)S(1)} %get-tuple-element.40.refs_1_.refs_7_, ...), custom_call_target="tpu_custom_call" | custom-call | tf_op jit(solution)/shard_map/pallas_call | solution.py:602
  16.1 0.0 collective-permute-done.refs_3_
  16.1 0.0 collective-permute-done.1.refs_4_
  16.1 0.0 copy-start
  16.2 1.7 %shard_map.62 = (f32[192,128]{1,0:T(8,128)S(1)}, f32[192,128]{1,0:T(8,128)S(1)}, f32[192,128]{1,0:T(8,128)S(1)}, f32[192,128]{1,0:T(8,128)S(1)}) custom-call(s32[1]{0:T(128)} %bitcast.b_ref, f32[16,24,128]{2,1,0:T(8,128)S(1)} %get-tuple-element.34.x_ref.refs_0_, f32[16,24,128]{2,1,0:T(8,128)S(1)} %get-tuple-element.35.refs_1_, ...), custom_call_target="tpu_custom_call" | custom-call | tf_op jit(solution)/shard_map/pallas_call | solution.py:602
  17.9 3.0 %collective-permute-start.2 = (f32[192,128]{1,0:T(8,128)S(1)}, f32[192,128]{1,0:T(8,128)S(1)}, u32[]{:S(2)}, u32[]{:S(2)}) collective-permute-start(f32[192,128]{1,0:T(8,128)S(1)} %get-tuple-element.46), channel_id=1, source_target_pairs={{0,24},{8,16},{16,8},{24,0},{1,25},{9,17},{17,9},{25,1},{2,26},{10... | collective-permute-start | bytes 294920 | tf_op jit(solution)/shard_map/ppermute | solution.py:614
  20.9 0.5 %collective-permute-start.3 = (f32[192,128]{1,0:T(8,128)S(1)}, f32[192,128]{1,0:T(8,128)S(1)}, u32[]{:S(2)}, u32[]{:S(2)}) collective-permute-start(f32[192,128]{1,0:T(8,128)S(1)} %get-tuple-element.47), channel_id=1, source_target_pairs={{0,8},{8,0},{16,24},{24,16},{1,9},{9,1},{17,25},{25,17},{2,10},{10... | collective-permute-start | bytes 294920 | tf_op jit(solution)/shard_map/ppermute | solution.py:614
  21.4 0.1 collective-permute-start.4
  21.5 2.1 %collective-permute-done.2.refs_1_ = f32[192,128]{1,0:T(8,128)S(1)} collective-permute-done((f32[192,128]{1,0:T(8,128)S(1)}, f32[192,128]{1,0:T(8,128)S(1)}, u32[]{:S(2)}, u32[]{:S(2)}) %collective-permute-start.2) | collective-permute-done | bytes 98336 | tf_op jit(solution)/shard_map/ppermute | solution.py:614
  23.6 1.9 %collective-permute-done.3.refs_2_ = f32[192,128]{1,0:T(8,128)S(1)} collective-permute-done((f32[192,128]{1,0:T(8,128)S(1)}, f32[192,128]{1,0:T(8,128)S(1)}, u32[]{:S(2)}, u32[]{:S(2)}) %collective-permute-start.3) | collective-permute-done | bytes 98336 | tf_op jit(solution)/shard_map/ppermute | solution.py:614
  25.5 0.5 %collective-permute-done.4.refs_3_ = f32[192,128]{1,0:T(8,128)S(1)} collective-permute-done((f32[192,128]{1,0:T(8,128)S(1)}, f32[192,128]{1,0:T(8,128)S(1)}, u32[]{:S(2)}, u32[]{:S(2)}) %collective-permute-start.4) | collective-permute-done | bytes 98336 | tf_op jit(solution)/shard_map/ppermute | solution.py:614
  26.0 0.0 copy-done
  26.0 1.6 %shard_map.63 = (f32[192,128]{1,0:T(8,128)S(1)}, f32[192,128]{1,0:T(8,128)S(1)}, f32[192,128]{1,0:T(8,128)S(1)}, f32[192,128]{1,0:T(8,128)S(1)}) custom-call(s32[1]{0:T(128)} %bitcast.b_ref, f32[192,128]{1,0:T(8,128)S(1)} %get-tuple-element.45.refs_0_, f32[192,128]{1,0:T(8,128)S(1)} %collective-permute-done.2.refs_1_, ...), custom_call_target="tpu_custom_call" | custom-call | tf_op jit(solution)/shard_map/pallas_call | solution.py:602
  27.6 1.6 %collective-permute-start.5 = (f32[192,128]{1,0:T(8,128)S(1)}, f32[192,128]{1,0:T(8,128)S(1)}, u32[]{:S(2)}, u32[]{:S(2)}) collective-permute-start(f32[192,128]{1,0:T(8,128)S(1)} %get-tuple-element.50), channel_id=1, source_target_pairs={{0,8},{8,0},{16,24},{24,16},{1,9},{9,1},{17,25},{25,17},{2,10},{10... | collective-permute-start | bytes 294920 | tf_op jit(solution)/shard_map/ppermute | solution.py:614
  29.1 0.5 %collective-permute-start.6 = (f32[192,128]{1,0:T(8,128)S(1)}, f32[192,128]{1,0:T(8,128)S(1)}, u32[]{:S(2)}, u32[]{:S(2)}) collective-permute-start(f32[192,128]{1,0:T(8,128)S(1)} %get-tuple-element.51), channel_id=1, source_target_pairs={{0,16},{8,24},{16,0},{24,8},{1,17},{9,25},{17,1},{25,9},{2,18},{10... | collective-permute-start | bytes 294920 | tf_op jit(solution)/shard_map/ppermute | solution.py:614
  29.6 1.5 %collective-permute-start.7 = (f32[192,128]{1,0:T(8,128)S(1)}, f32[192,128]{1,0:T(8,128)S(1)}, u32[]{:S(2)}, u32[]{:S(2)}) collective-permute-start(f32[192,128]{1,0:T(8,128)S(1)} %get-tuple-element.52), channel_id=1, source_target_pairs={{0,24},{8,16},{16,8},{24,0},{1,25},{9,17},{17,9},{25,1},{2,26},{10... | collective-permute-start | bytes 294920 | tf_op jit(solution)/shard_map/ppermute | solution.py:614
  31.1 1.1 %collective-permute-done.5.refs_1_ = f32[192,128]{1,0:T(8,128)S(1)} collective-permute-done((f32[192,128]{1,0:T(8,128)S(1)}, f32[192,128]{1,0:T(8,128)S(1)}, u32[]{:S(2)}, u32[]{:S(2)}) %collective-permute-start.5) | collective-permute-done | bytes 98336 | tf_op jit(solution)/shard_map/ppermute | solution.py:614
  32.2 1.5 %collective-permute-done.6.refs_2_ = f32[192,128]{1,0:T(8,128)S(1)} collective-permute-done((f32[192,128]{1,0:T(8,128)S(1)}, f32[192,128]{1,0:T(8,128)S(1)}, u32[]{:S(2)}, u32[]{:S(2)}) %collective-permute-start.6) | collective-permute-done | bytes 98336 | tf_op jit(solution)/shard_map/ppermute | solution.py:614
  33.8 1.4 %collective-permute-done.7.refs_3_ = f32[192,128]{1,0:T(8,128)S(1)} collective-permute-done((f32[192,128]{1,0:T(8,128)S(1)}, f32[192,128]{1,0:T(8,128)S(1)}, u32[]{:S(2)}, u32[]{:S(2)}) %collective-permute-start.7) | collective-permute-done | bytes 98336 | tf_op jit(solution)/shard_map/ppermute | solution.py:614
  35.2 0.1 collective-permute-start.8
  35.3 3.5 %collective-permute-start.9 = (f32[32,128]{1,0:T(8,128)S(1)}, f32[32,128]{1,0:T(8,128)S(1)}, u32[]{:S(2)}, u32[]{:S(2)}) collective-permute-start(f32[32,128]{1,0:T(8,128)S(1)} %get-tuple-element.56), channel_id=1, source_target_pairs={{0,7},{1,0},{2,1},{3,2},{4,3},{5,4},{6,5},{7,6},{8,15},{9,8},{10,9... | collective-permute-start | bytes 49160 | tf_op jit(solution)/shard_map/ppermute | solution.py:641
  38.8 1.2 %shard_map.65 = (f32[1024,128]{1,0:T(8,128)S(1)}, bf16[64,128,64]{2,1,0:T(8,128)(2,1)S(1)}, bf16[64,32,128]{2,1,0:T(8,128)(2,1)S(1)}, bf16[64,32,128]{2,1,0:T(8,...) custom-call(f32[16,24,128]{2,1,0:T(8,128)S(1)} %get-tuple-element.53.x_ref.refs_0_, ...), custom_call_target="tpu_custom_call" | custom-call | tf_op jit(solution)/shard_map/pallas_call | solution.py:602
  40.0 7.6 %shard_map.66.refs_5_ = f32[896,128]{1,0:T(8,128)S(1)} custom-call(f32[16,128]{1,0:T(8,128)S(1)} %get-tuple-element.36.q_ref.refs_2_.refs_5_.refs_4_, f32[1024,128]{1,0:T(8,128)S(1)} %get-tuple-element.57.refs_0_.refs_7_, bf16[64,128,64]{2,1,0:T(8,128)(2,1)S(1)} %get-tuple-element.58.refs_1_.refs_8_, ...), custom_call_target="tpu_custom_call" | custom-call | tf_op jit(solution)/shard_map/pallas_call | solution.py:602
  47.6 0.0 collective-permute-done.8.refs_3_
  47.6 0.0 collective-permute-done.9.refs_4_
  47.7 3.1 %shard_map.67 = (f32[384,128]{1,0:T(8,128)}, f32[384,128]{1,0:T(8,128)}) custom-call(f32[16,24,128]{2,1,0:T(8,128)S(1)} %get-tuple-element.53.x_ref.refs_0_, f32[16,24,128]{2,1,0:T(8,128)S(1)} %get-tuple-element.54.refs_1_, f32[16,128]{1,0:T(8,128)S(1)} %get-tuple-element.36.q_ref.refs_2_.refs_5_.refs_4_, f32[32,128]{1,0:T(8,128)S(1)} %collective-permute-done.8.refs_3_, ...), custom_call_target="tpu_custom_call" | custom-call | tf_op jit(solution)/shard_map/pallas_call | solution.py:602
  (1 shorter events, 0.0 us)
Async XLA Ops:
  2.7 13.5 %collective-permute-start = (f32[32,128]{1,0:T(8,128)S(1)}, f32[32,128]{1,0:T(8,128)S(1)}, u32[]{:S(2)}, u32[]{:S(2)}) collective-permute-start(f32[32,128]{1,0:T(8,128)S(1)} %get-tuple-element.37), channel_id=1, source_target_pairs={{0,1},{1,2},{2,3},{3,4},{4,5},{5,6},{6,7},{7,0},{8,9},{9,10},{10,1... | collective-permute-start | bytes 49160 | tf_op jit(solution)/shard_map/ppermute | solution.py:640
  3.2 13.0 %collective-permute-start.1 = (f32[32,128]{1,0:T(8,128)S(1)}, f32[32,128]{1,0:T(8,128)S(1)}, u32[]{:S(2)}, u32[]{:S(2)}) collective-permute-start(f32[32,128]{1,0:T(8,128)S(1)} %get-tuple-element.38), channel_id=1, source_target_pairs={{0,7},{1,0},{2,1},{3,2},{4,3},{5,4},{6,5},{7,6},{8,15},{9,8},{10,9... | collective-permute-start | bytes 49160 | tf_op jit(solution)/shard_map/ppermute | solution.py:641
  16.1 9.9 %copy-start = (bf16[4,64,384]{2,1,0:T(8,128)(2,1)S(1)}, bf16[4,64,384]{2,1,0:T(8,128)(2,1)}, u32[]{:S(2)}) copy-start(bf16[4,64,384]{2,1,0:T(8,128)(2,1)} %constant.7.clone.refs_4_) | copy-start | bytes 589828
  17.9 5.7 %collective-permute-start.2 = (f32[192,128]{1,0:T(8,128)S(1)}, f32[192,128]{1,0:T(8,128)S(1)}, u32[]{:S(2)}, u32[]{:S(2)}) collective-permute-start(f32[192,128]{1,0:T(8,128)S(1)} %get-tuple-element.46), channel_id=1, source_target_pairs={{0,24},{8,16},{16,8},{24,0},{1,25},{9,17},{17,9},{25,1},{2,26},{10... | collective-permute-start | bytes 294920 | tf_op jit(solution)/shard_map/ppermute | solution.py:614
  20.9 4.6 %collective-permute-start.3 = (f32[192,128]{1,0:T(8,128)S(1)}, f32[192,128]{1,0:T(8,128)S(1)}, u32[]{:S(2)}, u32[]{:S(2)}) collective-permute-start(f32[192,128]{1,0:T(8,128)S(1)} %get-tuple-element.47), channel_id=1, source_target_pairs={{0,8},{8,0},{16,24},{24,16},{1,9},{9,1},{17,25},{25,17},{2,10},{10... | collective-permute-start | bytes 294920 | tf_op jit(solution)/shard_map/ppermute | solution.py:614
  21.4 4.6 %collective-permute-start.4 = (f32[192,128]{1,0:T(8,128)S(1)}, f32[192,128]{1,0:T(8,128)S(1)}, u32[]{:S(2)}, u32[]{:S(2)}) collective-permute-start(f32[192,128]{1,0:T(8,128)S(1)} %get-tuple-element.48), channel_id=1, source_target_pairs={{0,16},{8,24},{16,0},{24,8},{1,17},{9,25},{17,1},{25,9},{2,18},{10... | collective-permute-start | bytes 294920 | tf_op jit(solution)/shard_map/ppermute | solution.py:614
  27.6 4.7 %collective-permute-start.5 = (f32[192,128]{1,0:T(8,128)S(1)}, f32[192,128]{1,0:T(8,128)S(1)}, u32[]{:S(2)}, u32[]{:S(2)}) collective-permute-start(f32[192,128]{1,0:T(8,128)S(1)} %get-tuple-element.50), channel_id=1, source_target_pairs={{0,8},{8,0},{16,24},{24,16},{1,9},{9,1},{17,25},{25,17},{2,10},{10... | collective-permute-start | bytes 294920 | tf_op jit(solution)/shard_map/ppermute | solution.py:614
  29.1 4.6 %collective-permute-start.6 = (f32[192,128]{1,0:T(8,128)S(1)}, f32[192,128]{1,0:T(8,128)S(1)}, u32[]{:S(2)}, u32[]{:S(2)}) collective-permute-start(f32[192,128]{1,0:T(8,128)S(1)} %get-tuple-element.51), channel_id=1, source_target_pairs={{0,16},{8,24},{16,0},{24,8},{1,17},{9,25},{17,1},{25,9},{2,18},{10... | collective-permute-start | bytes 294920 | tf_op jit(solution)/shard_map/ppermute | solution.py:614
  29.6 5.5 %collective-permute-start.7 = (f32[192,128]{1,0:T(8,128)S(1)}, f32[192,128]{1,0:T(8,128)S(1)}, u32[]{:S(2)}, u32[]{:S(2)}) collective-permute-start(f32[192,128]{1,0:T(8,128)S(1)} %get-tuple-element.52), channel_id=1, source_target_pairs={{0,24},{8,16},{16,8},{24,0},{1,25},{9,17},{17,9},{25,1},{2,26},{10... | collective-permute-start | bytes 294920 | tf_op jit(solution)/shard_map/ppermute | solution.py:614
  35.2 12.4 %collective-permute-start.8 = (f32[32,128]{1,0:T(8,128)S(1)}, f32[32,128]{1,0:T(8,128)S(1)}, u32[]{:S(2)}, u32[]{:S(2)}) collective-permute-start(f32[32,128]{1,0:T(8,128)S(1)} %get-tuple-element.55), channel_id=1, source_target_pairs={{0,1},{1,2},{2,3},{3,4},{4,5},{5,6},{6,7},{7,0},{8,9},{9,10},{10,1... | collective-permute-start | bytes 49160 | tf_op jit(solution)/shard_map/ppermute | solution.py:640
  35.3 12.4 %collective-permute-start.9 = (f32[32,128]{1,0:T(8,128)S(1)}, f32[32,128]{1,0:T(8,128)S(1)}, u32[]{:S(2)}, u32[]{:S(2)}) collective-permute-start(f32[32,128]{1,0:T(8,128)S(1)} %get-tuple-element.56), channel_id=1, source_target_pairs={{0,7},{1,0},{2,1},{3,2},{4,3},{5,4},{6,5},{7,6},{8,15},{9,8},{10,9... | collective-permute-start | bytes 49160 | tf_op jit(solution)/shard_map/ppermute | solution.py:641
